TPU v7x, 256 devices: a whole 4x4x8 slice. The times are simulated.
256 devices in a mesh: inst: 32 (over y, x, z_lo), tp: 8 (over z_hi, core).
Axes of the slice: x: 4, y: 4, z: 8 (z_hi: 4, z_lo: 2; z = z_hi * 2 + z_lo), core: 2. Of those that a mesh axis runs over, the one named last changes fastest.
Arguments:
- queries: bfloat16 [256, 4, 8192], P('inst', None, 'tp'), may hold values from -12 to 12
- new_kv: bfloat16 [256, 4, 2048], P('inst', None, 'tp'), may hold values from -7.5 to 7.5
- pool: bfloat16 [2560, 128, 2048], P('inst', None, 'tp'), may hold values from -5 to 5
- page: int32 [256, 32], P('inst'), may hold values from 0 to 143, as said below
- lengths: int32 [256], P('inst'), may hold values from 1 to 4096, as said below
- outbox: int32 [32, 32, 2], P('inst'), may hold values from 0 to 79, as said below
- prefix_store: bfloat16 [131072, 2048], P(('inst', 'tp')), may hold values from -5 to 5
- owner: int32 [1], replicated, may hold values from 0 to 31
- flags: int32 [256], P('inst'), may hold values 0 or 1
Outputs:
- attention: bfloat16 [256, 4, 8192], P('inst', None, 'tp')
Inputs may be any that keep to these rules, and one draw needn't show every extreme that they name: `page`: for request r, entries j < ceil(lengths[r] / 128) name distinct blocks of its instance's store: a value under 80 is a block of the instance's own pool that it sends to no one, and 80 + s * 2 + c is the c-th block that instance s sends it; each of the 64 received blocks is named exactly once. Later entries are arbitrary. On every instance the named blocks number at most 80, and exactly 80 on some instance. `lengths`: one request of every instance has exactly 4096 tokens. `outbox`: for each source instance the 64 entries are distinct blocks of its pool.
All inputs are finite; a program needn't handle non-finite values. No bound on the sum of `flags` on one device may be relied on, other than what follows from the above.
Results may differ from a plain program's by a relative error of at most 0.0028.
Values may be sent and summed in bfloat16 or wider, within the bound.
No kernel may reach another device: no remote copies, remote signals or barrier semaphores. Data moves between devices by JAX's collectives and lax.ppermute only.
A program may use at most 128 MiB of HBM per device.

v0:
```python
import jax
import jax.numpy as jnp
from jax import lax
from jax.sharding import PartitionSpec as P

HD = 128


NEG = -1e30


def spread(array, axis, root):
    mine = lax.axis_index(axis) == root
    return lax.psum(jnp.where(mine, array, jnp.zeros_like(array)), axis)


def part_stats(scores, valid):
    masked = jnp.where(valid, scores, -jnp.inf)
    top = jnp.max(masked, axis=-1)
    top = jnp.where(jnp.any(valid, axis=-1), top, NEG)
    weights = jnp.where(valid, jnp.exp(scores - top[..., None]), 0.0).astype(jnp.bfloat16)
    total = jnp.sum(weights.astype(jnp.float32), axis=-1)
    return (top, weights, total)


def combine_parts(parts):
    peak = parts[0][0].max(axis=1)
    for entry in parts[1:]:
        peak = jnp.maximum(peak, entry[0].max(axis=1))
    numer = jnp.zeros(parts[0][2].shape[:1] + parts[0][2].shape[2:], jnp.float32)
    denom = jnp.zeros(peak.shape, jnp.float32)
    for top, total, out in parts:
        factor = jnp.exp(top - peak[:, None])
        numer = numer + jnp.sum(factor[..., None] * out, axis=1)
        denom = denom + jnp.sum(factor * total, axis=1)
    return numer / denom[..., None]


def request_partials(q_rows, blocks, counts, scale):
    scores = (
        jnp.einsum(
            "rsngd,rjtnd->rjsngt", q_rows, blocks[:, :, :, :, 0], preferred_element_type=jnp.float32
        )
        * scale
    )
    place = jnp.arange(blocks.shape[2], dtype=jnp.int32)
    valid = place[None, None, :] < counts[:, :, None]
    valid = jnp.broadcast_to(valid[:, :, None, None, None, :], scores.shape)
    top, weights, total = part_stats(scores, valid)
    out = jnp.einsum(
        "rjsngt,rjtnd->rjsngd", weights, blocks[:, :, :, :, 1], preferred_element_type=jnp.float32
    )
    positions = blocks.shape[0] * blocks.shape[1]
    return (
        top.reshape((positions,) + top.shape[2:]),
        total.reshape((positions,) + total.shape[2:]),
        out.reshape((positions,) + out.shape[2:]),
    )


def per_device(queries, new_kv, pool, page, lengths, outbox, prefix_store, owner, flags):
    scale = HD ** (-0.5)
    req = queries.shape[0]
    steps = queries.shape[1]
    block = pool.shape[1]
    pool_size = pool.shape[0]
    width = pool.shape[2]
    heads_kv = width // (2 * HD)
    group = queries.shape[2] // (HD * heads_kv)
    inst = lax.axis_size("inst")
    slots_each = outbox.shape[2]
    maxb = page.shape[1]
    incoming = inst * slots_each
    q_rows = queries.reshape(req, steps, heads_kv, group, HD)
    fresh = new_kv.reshape(req, steps, heads_kv, 2, HD)
    blocks_here = pool.reshape(pool_size, block, heads_kv, 2, HD)
    shard = spread(prefix_store, "inst", owner[0])
    prefix = lax.all_to_all(shard, "tp", split_axis=1, concat_axis=0, tiled=True)
    prefix = prefix.reshape(prefix.shape[0] // block, block, heads_kv, 2, HD)
    counts = jnp.clip(
        lengths[:, None] - jnp.arange(maxb, dtype=jnp.int32)[None, :] * block, 0, block
    )
    flat_ids = page.reshape(-1)
    outgoing = pool[outbox[0].reshape(-1)].reshape(inst, slots_each, block, width)
    arrived = lax.all_to_all(outgoing, "inst", split_axis=0, concat_axis=0, tiled=True)
    store = jnp.concatenate(
        [blocks_here, arrived.reshape(incoming, block, heads_kv, 2, HD)], axis=0
    )
    gathered = store[flat_ids].reshape(req, maxb, block, heads_kv, 2, HD)
    ctx_top, ctx_total, ctx_out = request_partials(q_rows, gathered, counts, scale)
    ctx_top = ctx_top.reshape((req, maxb) + ctx_top.shape[1:])
    ctx_total = ctx_total.reshape((req, maxb) + ctx_total.shape[1:])
    ctx_out = ctx_out.reshape((req, maxb) + ctx_out.shape[1:])
    pre_scores = (
        jnp.einsum(
            "rsngd,ptnd->rpsngt", q_rows, prefix[:, :, :, 0], preferred_element_type=jnp.float32
        )
        * scale
    )
    pre_valid = jnp.broadcast_to((flags == 1)[:, None, None, None, None, None], pre_scores.shape)
    pre_top, pre_weights, pre_total = part_stats(pre_scores, pre_valid)
    pre_out = jnp.einsum(
        "rpsngt,ptnd->rpsngd", pre_weights, prefix[:, :, :, 1], preferred_element_type=jnp.float32
    )
    new_scores = (
        jnp.einsum(
            "rsngd,rund->rsngu", q_rows, fresh[:, :, :, 0], preferred_element_type=jnp.float32
        )
        * scale
    )
    order = jnp.arange(steps, dtype=jnp.int32)
    new_valid = jnp.broadcast_to(
        (order[None, :] <= order[:, None])[None, :, None, None, :], new_scores.shape
    )
    new_top, new_weights, new_total = part_stats(new_scores, new_valid)
    new_out = jnp.einsum(
        "rsngu,rund->rsngd", new_weights, fresh[:, :, :, 1], preferred_element_type=jnp.float32
    )
    result = combine_parts(
        [
            (pre_top, pre_total, pre_out),
            (ctx_top, ctx_total, ctx_out),
            (new_top[:, None], new_total[:, None], new_out[:, None]),
        ]
    )
    return result.astype(jnp.bfloat16).reshape(req, steps, heads_kv * group * HD)


def solution(mesh):
    placed = (
        P("inst", None, "tp"),
        P("inst", None, "tp"),
        P("inst", None, "tp"),
        P("inst", None),
        P("inst"),
        P("inst", None, None),
        P(("inst", "tp"), None),
        P(),
        P("inst"),
    )
    return jax.shard_map(
        per_device, mesh=mesh, in_specs=placed, out_specs=P("inst", None, "tp"), check_vma=False
    )
```

profile of v0, /device:TPU:1, one launch (start us, length us, event | category | flops | bytes accessed | tf_op | source)
XLA Modules:
  0.0 526.2 jit_solution(5960552342041739917)
XLA Ops:
  7.3 2.5 copy.87
  9.9 306.2 %all-reduce.2.cloned.1.call-done = bf16[512,8,256]{0,2,1:T(8,128)(2,1)} async-done(((bf16[512,8,256]{0,2,1:T(8,128)(2,1)}), bf16[512,8,256]{0,2,1:T(8,128)(2,1)}) %all-reduce.2.cloned.1.call-update) | async-done | bytes 2097168 | tf_op jit(solution)/shard_map/psum | solution.py:14
  316.1 28.0 %all-to-all-start = ((bf16[512,8,256]{0,2,1:T(8,128)(2,1)}), bf16[512,8,256]{0,2,1:T(8,128)(2,1)S(1)}, u32[]{:S(2)}, u32[]{:S(2)}) async-start(bf16[512,8,256]{0,2,1:T(8,128)(2,1)} %all-reduce.2.cloned.1.call-done), calls=%async_computation | async-start | bytes 4194304 | tf_op jit(solution)/shard_map/all_to_all | solution.py:78
  344.3 5.2 gather_fusion
  349.5 6.4 %copy.94 = bf16[64,128,256]{1,2,0:T(8,128)(2,1)} copy(bf16[64,128,256]{2,1,0:T(8,128)(2,1)} %gather_fusion) | data formatting | bytes 8388608 | tf_op jit(solution)/shard_map/gather | solution.py:84
  355.9 35.9 %all-to-all-done = bf16[512,8,256]{0,2,1:T(8,128)(2,1)S(1)} async-done(((bf16[512,8,256]{0,2,1:T(8,128)(2,1)}), bf16[512,8,256]{0,2,1:T(8,128)(2,1)S(1)}, u32[]{:S(2)}, u32[]{:S(2)}) %all-to-all-start) | async-done | bytes 2097184 | tf_op jit(solution)/shard_map/all_to_all | solution.py:78
  391.8 4.9 all-to-all-start.1
  396.7 8.0 %copy.92 = bf16[80,128,256]{1,2,0:T(8,128)(2,1)} copy(bf16[80,128,256]{2,1,0:T(8,128)(2,1)} %param.11) | data formatting | bytes 10485760 | tf_op args[2]
  404.9 8.0 %copy.95 = bf16[80,128,1,2,128]{4,1,3,0,2:T(8,128)(2,1)} copy(bf16[80,128,1,2,128]{1,4,3,0,2:T(8,128)(2,1)} %bitcast.171) | data formatting | bytes 10485760 | tf_op jit(solution)/shard_map/reshape | solution.py:76
  412.9 17.8 %broadcast_reduce_fusion = pred[8,32,4,8]{3,2,0,1:T(4,128)(4,1)S(1)} fusion(pred[8]{0:T(512)(128)(4,1)S(1)} %broadcast_compare_fusion), kind=kLoop, calls=%fused_computation.28 | loop fusion | flops 1040384 | bytes 8200 | tf_op jit(solution)/shard_map/reduce_or | solution.py:20
  432.1 2.7 copy.88
  434.9 3.1 reshape.405
  439.4 1.9 copy.119
  441.3 2.9 fusion.4
  444.6 1.7 copy.121
  446.5 6.4 %copy.96 = bf16[64,128,1,2,128]{4,1,3,0,2:T(8,128)(2,1)} copy(bf16[64,128,1,2,128]{1,4,3,0,2:T(8,128)(2,1)} %bitcast.11) | data formatting | bytes 8388608 | tf_op jit(solution)/shard_map/reshape | solution.py:87
  453.0 7.7 %maximum_bitcast_fusion = bf16[144,128,2,128]{3,1,2,0:T(8,128)(2,1)} fusion(bf16[64,128,1,2,128]{4,1,3,0,2:T(8,128)(2,1)} %copy.96, bf16[80,128,1,2,128]{4,1,3,0,2:T(8,128)(2,1)} %copy.95), kind=kLoop, calls=%fused_computation.2 | loop fusion | flops 4718592 | bytes 18874368 | tf_op jit(solution)/shard_map/concatenate | solution.py:86
  460.7 13.4 %gather_fusion.1 = bf16[256,128,2,128]{3,1,2,0:T(8,128)(2,1)} fusion(bf16[144,128,2,128]{3,1,2,0:T(8,128)(2,1)} %maximum_bitcast_fusion, s32[1024]{0:T(1024)S(1)} %pad_clamp_fusion), kind=kCustom, calls=%fused_computation.1 | custom fusion | bytes 33555456 | tf_op jit(solution)/shard_map/gather | solution.py:89
  474.1 14.1 %copy.97 = bf16[256,128,2,128]{3,1,0,2:T(8,128)(2,1)} copy(bf16[256,128,2,128]{3,1,2,0:T(8,128)(2,1)} %gather_fusion.1) | data formatting | bytes 33554432 | tf_op jit(solution)/shard_map/gather | solution.py:89
  488.3 8.3 %fusion.8 = (f32[8,32,4,8]{3,2,1,0:T(4,128)S(1)}, f32[8,32,128,4,8]{2,4,3,1,0:T(8,128)}) fusion(pred[8,32,128]{2,1,0:T(8,128)(4,1)S(1)} %iota_compare_fusion, bf16[8,4,8,128,1]{3,2,1,0,4:T(8,128)(2,1)S(1)} %reshape.443, bf16[8,32,128,1,2,128]{5,2,1,0,4,3:T(8,128)(2,1)} %bitcast.172), kind=kOutput, calls=%fused_computation.19 | convolution fusion | flops 271572992 | bytes 12713984 | tf_op jit(solution)/shard_map/rsngd,rjtnd->rjsngt/dot_general | solution.py:41
  497.5 4.1 convert_reduce_fusion.1
  502.3 4.4 convert_reduce_fusion
  507.5 6.1 %fusion.3 = f32[8,128,4,8]{1,3,2,0:T(8,128)S(1)} fusion(bf16[8,32,128,1,2,128]{5,2,1,0,4,3:T(8,128)(2,1)} %bitcast.173, f32[8,32,4,8]{3,2,1,0:T(4,128)S(1)} %copy.104, f32[8,32,128,4,8]{2,4,3,1,0:T(8,128)} %get-tuple-element.24, f32[8,32,4,8]{3,2,1,0:T(4,128)S(1)} %copy.105, pred[8,32,128]{2,1,0:T(8,128)(4,1)S(1)} %iota_compare_fusion), kind=kOutput, calls=%fused_computation.10 | convolution fusion | flops 274694144 | bytes 12812288 | tf_op jit(solution)/shard_map/rjsngt,rjtnd->rjsngd/dot_general | solution.py:50
  514.3 4.1 fusion.2
  (54 shorter events, 8.0 us)
Async XLA Ops:
  6.5 309.5 %all-reduce.2.cloned.1.call-start = ((), (), s32[]{:S(2)}) async-start(), calls=%async_computation.2 | async-start | bytes 4194304 | tf_op jit(solution)/shard_map/psum | solution.py:14
  9.9 334.2 %copy-start.4 = (s32[1,32,2]{1,2,0:T(2,128)S(1)}, s32[1,32,2]{1,2,0:T(2,128)}, u32[]{:S(2)}) copy-start(s32[1,32,2]{1,2,0:T(2,128)} %param.14) | copy-start | bytes 772
  316.1 75.7 %all-to-all-start = ((bf16[512,8,256]{0,2,1:T(8,128)(2,1)}), bf16[512,8,256]{0,2,1:T(8,128)(2,1)S(1)}, u32[]{:S(2)}, u32[]{:S(2)}) async-start(bf16[512,8,256]{0,2,1:T(8,128)(2,1)} %all-reduce.2.cloned.1.call-done), calls=%async_computation | async-start | bytes 4194304 | tf_op jit(solution)/shard_map/all_to_all | solution.py:78
  391.8 54.7 %all-to-all-start.1 = ((bf16[32,2,128,256]{2,3,1,0:T(8,128)(2,1)}), bf16[32,2,128,256]{2,3,1,0:T(8,128)(2,1)}, u32[]{:S(2)}, u32[]{:S(2)}) async-start(bf16[32,2,128,256]{2,3,1,0:T(8,128)(2,1)} %bitcast.174), calls=%async_computation.1 | async-start | bytes 8388608 | tf_op jit(solution)/shard_map/all_to_all | solution.py:85
  396.7 8.0 %copy-start.1 = (bf16[8,4,1024]{2,1,0:T(4,128)(2,1)S(1)}, bf16[8,4,1024]{2,1,0:T(4,128)(2,1)}, u32[]{:S(2)}) copy-start(bf16[8,4,1024]{2,1,0:T(4,128)(2,1)} %param.9) | copy-start | bytes 196612
  404.8 8.0 %copy-start.3 = (s32[8,32]{1,0:T(8,128)S(1)}, s32[8,32]{1,0:T(8,128)}, u32[]{:S(2)}) copy-start(s32[8,32]{1,0:T(8,128)} %param.12) | copy-start | bytes 3076
  404.9 8.1 %copy-start.6 = (s32[8]{0:T(128)S(1)}, s32[8]{0:T(128)}, u32[]{:S(2)}) copy-start(s32[8]{0:T(128)} %param.17) | copy-start | bytes 100
  404.9 26.2 %copy-start.2 = (bf16[8,4,256]{2,1,0:T(4,128)(2,1)S(1)}, bf16[8,4,256]{2,1,0:T(4,128)(2,1)}, u32[]{:S(2)}) copy-start(bf16[8,4,256]{2,1,0:T(4,128)(2,1)} %param.10) | copy-start | bytes 49156
  404.9 26.3 %copy-start.5 = (s32[8]{0:T(128)S(1)}, s32[8]{0:T(128)}, u32[]{:S(2)}) copy-start(s32[8]{0:T(128)} %param.13) | copy-start | bytes 100
  507.5 6.8 %copy-start = (bf16[32,128,1,1,128]{4,1,0,3,2:T(8,128)(2,1)S(1)}, bf16[32,128,1,1,128]{4,1,0,3,2:T(8,128)(2,1)}, u32[]{:S(2)}) copy-start(bf16[32,128,1,1,128]{4,1,0,3,2:T(8,128)(2,1)} %copy.121) | copy-start | bytes 3145732
Sparse Core Ops, SparseCore 0:
  10.0 306.0 all-reduce.1
where the time goes:
time: 537 us; the launch traced here: 526 us
  waiting for transfers between devices  342 us (64%)
  local copies, waits for them, and re-layouts  79.2 us (15%)
  other arithmetic  35.5 us (7%)
  starting transfers between devices  32.9 us (6%)
  matrix products  22 us (4%)
  between operations  14.3 us (3%)
    psum x1, waiting for transfers between devices, spread(): return lax.psum(jnp.where(mine, array, jnp.zeros_like(array)), axis)  306 us
    all_to_all x1, waiting for transfers between devices, per_device(): lax.all_to_all(shard, 'tp', split_axis=1, concat_axis=0, tiled=True)  35.9 us
    all_to_all x1, starting transfers between devices, per_device(): lax.all_to_all(shard, 'tp', split_axis=1, concat_axis=0, tiled=True)  28 us
    gather x2, local copies, waits for them, and re-layouts, per_device(): gathered = store[flat_ids].reshape(req, maxb, block, heads_kv, 2, HD)  27.6 us
    reduce_or x3, other arithmetic, part_stats(): top = jnp.where(jnp.any(valid, axis=-1), top, NEG)  18.2 us
    unnamed x18, local copies, waits for them, and re-layouts  11.7 us
    gather x2, local copies, waits for them, and re-layouts, per_device(): pool[outbox[0].reshape(-1)].reshape(inst, slots_each, block, width)  11.6 us
  transfers between devices with their start and end apart: 3, of which 3 were waited for; matrix products, arithmetic and copies ran while one was open for 12% of the time, Pallas kernels for 0%

commit v1 on v0

v1 whole, which is shorter than its diff:
```python
import functools

import jax
import jax.numpy as jnp
from jax import lax
from jax.experimental import pallas as pl
from jax.experimental.pallas import tpu as pltpu
from jax.sharding import PartitionSpec as P

HD = 128
BLK = 128
CAP = 2
KEPT = 16
NEG = -1e30
F32 = jnp.float32
BF16 = jnp.bfloat16

VMEM = pl.BlockSpec(memory_space=pltpu.VMEM)
SMEM = pl.BlockSpec(memory_space=pltpu.SMEM)


def params():
    return pltpu.CompilerParams(vmem_limit_bytes=40 * 1024 * 1024)


def cost(us):
    return pl.CostEstimate(flops=0, bytes_accessed=int(us * 3.0e6), transcendentals=0)


def dot_nt(a, b):
    return lax.dot_general(a, b, (((1,), (1,)), ((), ())), preferred_element_type=F32)


def dot_nn(a, b):
    return lax.dot_general(a, b, (((1,), (0,)), ((), ())), preferred_element_type=F32)


def with_ones(values):
    return jnp.concatenate([values, jnp.ones_like(values)], axis=1)


def block_partial(q, keys, values, valid):
    scores = dot_nt(q, keys) * (HD ** -0.5)
    if valid is not None:
        scores = jnp.where(valid, scores, NEG)
    top = jnp.max(scores, axis=-1, keepdims=True)
    weights = jnp.exp(scores - top)
    if valid is not None:
        weights = jnp.where(valid, weights, 0.0)
    both = dot_nn(weights.astype(BF16), with_ones(values))
    return top, both[:, HD:], both[:, :HD]


def prep_kernel(pool_size, page, lens, q, pay, local, slot_req, counts):
    n = pay.shape[0]
    rows = q.shape[1]
    for k in range(KEPT):
        for field in range(3):
            local[field, k] = 0

    def request(r, kept):
        length = lens[r]

        def block(j, kept):
            b = page[r, j]
            valid = jnp.minimum(length - j * BLK, BLK)
            away = b >= pool_size

            @pl.when(away)
            def _():
                slot = b - pool_size
                slot_req[slot] = r
                counts[slot] = valid
                at = pl.multiple_of(lax.bitwise_and(slot, 1) * rows, rows)
                pay[lax.shift_right_logical(slot, 1), pl.ds(at, rows), :] = q[r]

            @pl.when(jnp.logical_not(away))
            def _():
                local[0, kept] = b
                local[1, kept] = r
                local[2, kept] = valid

            return kept + jnp.where(away, 0, 1)

        return lax.fori_loop(0, lax.shift_right_logical(length + BLK - 1, 7), block, kept)

    lax.fori_loop(0, q.shape[0], request, 0)
    upper = lax.broadcasted_iota(jnp.int32, (16, HD), 0) < 8

    def mark(d, carry):
        tile = jnp.where(upper, counts[2 * d], counts[2 * d + 1])
        pay[d, CAP * rows : CAP * rows + 16, :] = tile.astype(F32).astype(BF16)
        return carry

    lax.fori_loop(0, n, mark, 0)


def prep(page, lengths, q, pool_size, n):
    req, rows, _ = q.shape
    return pl.pallas_call(
        functools.partial(prep_kernel, pool_size),
        out_shape=(
            jax.ShapeDtypeStruct((n, CAP * rows + 16, HD), BF16),
            jax.ShapeDtypeStruct((3, KEPT), jnp.int32),
            jax.ShapeDtypeStruct((n * CAP,), jnp.int32),
        ),
        in_specs=[SMEM, SMEM, VMEM],
        out_specs=(VMEM, SMEM, SMEM),
        scratch_shapes=[pltpu.SMEM((n * CAP,), jnp.int32)],
        compiler_params=params(),
        cost_estimate=cost(4),
        name="prep",
    )(page, lengths, q)


def remote_kernel(outbox, pool, pay, ret):
    n = pay.shape[0]
    rows = (pay.shape[1] - 16) // CAP
    each = BLK // rows
    lane = lax.broadcasted_iota(jnp.int32, (rows, BLK), 1)

    def group(g, carry):
        stats = []
        for i in range(each):
            d = g * each + i
            marks = pay[d, CAP * rows : CAP * rows + 16, :].astype(F32)
            stat = jnp.zeros((rows, BLK), F32)
            for c in range(CAP):
                kv = pool[outbox[d * CAP + c]]
                valid = lane < marks[8 * c : 8 * c + 1, :].astype(jnp.int32)
                top, total, out = block_partial(
                    pay[d, c * rows : (c + 1) * rows, :], kv[:, :HD], kv[:, HD:], valid
                )
                ret[d, c * rows : (c + 1) * rows, :] = out
                stat = jnp.where(lane == 2 * c, top, stat)
                stat = jnp.where(lane == 2 * c + 1, total, stat)
            stats.append(stat)
        turned = jnp.concatenate(stats, axis=0).T[:8]
        for i in range(each):
            ret[g * each + i, CAP * rows : CAP * rows + 8, :] = turned
        return carry

    lax.fori_loop(0, n // each, group, 0)


def remote_partials(outbox, pool, pay):
    n, height, _ = pay.shape
    return pl.pallas_call(
        remote_kernel,
        out_shape=jax.ShapeDtypeStruct((n, height - 8, HD), F32),
        in_specs=[SMEM, VMEM, VMEM],
        out_specs=VMEM,
        compiler_params=params(),
        cost_estimate=cost(8),
        name="remote_partials",
    )(outbox, pool, pay)


def local_kernel(local, pool, q, fresh, out_o, out_m, out_l):
    req, rows, _ = q.shape
    steps = rows // 8
    keys = fresh.shape[1]
    step = lax.broadcasted_iota(jnp.int32, (rows, keys), 0) // 8
    place = lax.broadcasted_iota(jnp.int32, (rows, keys), 1)
    causal = (place <= step) & (place < steps)
    for r in range(req):
        top, total, out = block_partial(q[r], fresh[r, :, :HD], fresh[r, :, HD:], causal)
        out_o[r] = out
        out_l[r] = total
        out_m[r] = jnp.broadcast_to(top, (rows, HD))
    lane = lax.broadcasted_iota(jnp.int32, (rows, BLK), 1)

    def batch(g, carry):
        found = []
        for i in range(8):
            k = g * 8 + i
            kv = pool[local[0, k]]
            found.append(
                block_partial(q[local[1, k]], kv[:, :HD], kv[:, HD:], lane < local[2, k])
            )
        for i in range(8):
            r = local[1, g * 8 + i]
            top, total, out = found[i]
            old = out_m[r]
            new = jnp.maximum(old, top)
            keep, add = jnp.exp(old - new), jnp.exp(top - new)
            out_m[r] = new
            out_l[r] = out_l[r] * keep + total * add
            out_o[r] = out_o[r] * keep + out * add
        return carry

    lax.fori_loop(0, KEPT // 8, batch, 0)


def local_partials(local, pool, q, fresh):
    one = jax.ShapeDtypeStruct(q.shape, F32)
    return pl.pallas_call(
        local_kernel,
        out_shape=(one, one, one),
        in_specs=[SMEM, VMEM, VMEM, VMEM],
        out_specs=(VMEM, VMEM, VMEM),
        compiler_params=params(),
        cost_estimate=cost(6),
        name="local_partials",
    )(local, pool, q, fresh)


def prefix_kernel(q, kv, out_o, out_m, out_l):
    pieces, shares, tokens, _ = kv.shape
    each = BLK // tokens
    out_o[...] = jnp.zeros_like(out_o)
    out_l[...] = jnp.zeros_like(out_l)
    out_m[...] = jnp.full_like(out_m, NEG)

    def share(t, carry):
        found = []
        for b in range(pieces // each):
            block = kv[b * each : (b + 1) * each, t].reshape(BLK, 2 * HD)
            found.append(block_partial(q[...], block[:, :HD], block[:, HD:], None))
        old = out_m[...]
        new = old
        for top, _, _ in found:
            new = jnp.maximum(new, top)
        keep = jnp.exp(old - new)
        acc_l, acc_o = out_l[...] * keep, out_o[...] * keep
        for top, total, out in found:
            add = jnp.exp(top - new)
            acc_l = acc_l + total * add
            acc_o = acc_o + out * add
        out_m[...] = new
        out_l[...] = acc_l
        out_o[...] = acc_o
        return carry

    lax.fori_loop(0, shares, share, 0)


def prefix_partials(q, kv):
    one = jax.ShapeDtypeStruct(q.shape, F32)
    return pl.pallas_call(
        prefix_kernel,
        out_shape=(one, one, one),
        in_specs=[VMEM, VMEM],
        out_specs=(VMEM, VMEM, VMEM),
        compiler_params=params(),
        cost_estimate=cost(8),
        name="prefix_partials",
    )(q, kv)


def final_kernel(me, slot_req, flags, ret, lo, lm, ll, po, pm, plen, out, top, total, acc, turned):
    req, rows, _ = lo.shape
    n = ret.shape[0]
    batch = min(16, n)
    body = CAP * rows
    for r in range(req):
        use = flags[r] == 1
        past = jnp.where(use, pm[r], NEG)
        top[r] = jnp.maximum(lm[r], past)
    for g in range(n // batch):
        tiles = ret[g * batch : (g + 1) * batch, body : body + 8, :]
        turned[g] = tiles.reshape(batch * 8, BLK).T
    mine = pl.multiple_of(lax.rem(me[0], BLK // rows) * rows, rows)
    for g in range(n // batch):
        stats = turned[g, pl.ds(mine, rows), :]
        for i in range(batch):
            for c in range(CAP):
                r = slot_req[(g * batch + i) * CAP + c]
                col = 8 * i + 2 * c
                top[r] = jnp.maximum(top[r], stats[:, col : col + 1])
    for r in range(req):
        use = flags[r] == 1
        peak = top[r]
        past = jnp.exp(jnp.where(use, pm[r], NEG) - peak)
        here = jnp.exp(lm[r] - peak)
        total[r] = ll[r] * here + plen[r] * past
        acc[r] = lo[r] * here + po[r] * past
    for g in range(n // batch):
        stats = turned[g, pl.ds(mine, rows), :]
        for i in range(batch):
            for c in range(CAP):
                s = g * batch + i
                r = slot_req[s * CAP + c]
                col = 8 * i + 2 * c
                factor = jnp.exp(stats[:, col : col + 1] - top[r])
                total[r] += stats[:, col + 1 : col + 2] * factor
                acc[r] += ret[s, c * rows : (c + 1) * rows, :] * factor
    for r in range(req):
        out[r] = (acc[r] / total[r]).astype(BF16)


def final(me, slot_req, flags, ret, here, past):
    req, rows, _ = here[0].shape
    n = ret.shape[0]
    batch = min(16, n)
    whole = pltpu.VMEM((req, rows, HD), F32)
    return pl.pallas_call(
        final_kernel,
        out_shape=jax.ShapeDtypeStruct((req, rows, HD), BF16),
        in_specs=[SMEM, SMEM, SMEM] + [VMEM] * 7,
        out_specs=VMEM,
        scratch_shapes=[whole, whole, whole, pltpu.VMEM((n // batch, BLK, batch * 8), F32)],
        compiler_params=params(),
        cost_estimate=cost(4),
        name="final",
    )(me, slot_req, flags, ret, *here, *past)


def after(value, other):
    return lax.optimization_barrier((value, other))[0]


def per_device(queries, new_kv, pool, page, lengths, outbox, prefix_store, owner, flags):
    req, steps, width = queries.shape
    pool_size = pool.shape[0]
    group = width // HD
    rows = steps * group
    n = lax.axis_size("inst")
    shares = lax.axis_size("tp")
    me = lax.axis_index("inst").astype(jnp.int32).reshape(1)
    held, wide = prefix_store.shape
    tokens = held // n

    scattered = lax.all_to_all(
        prefix_store.reshape(n, tokens, wide), "inst", split_axis=0, concat_axis=0, tiled=True
    )
    q = queries.reshape(req, rows, HD)
    pay, local, slot_req = prep(page, lengths, q, pool_size, n)
    asked = lax.all_to_all(pay, "inst", split_axis=0, concat_axis=0, tiled=True)
    piece = lax.dynamic_index_in_dim(scattered, owner[0], 0, keepdims=False)
    piece = piece.reshape(tokens, shares, wide // shares).transpose(1, 0, 2)
    piece = lax.all_to_all(
        after(piece, asked), "tp", split_axis=0, concat_axis=0, tiled=True
    )
    ret = remote_partials(outbox.reshape(-1), pool, asked)
    fresh = jnp.pad(new_kv, ((0, 0), (0, 16 - steps), (0, 0)))
    here = local_partials(local, pool, q, fresh)
    prefix = lax.all_to_all(
        jnp.broadcast_to(piece[None], (n,) + piece.shape),
        "inst",
        split_axis=0,
        concat_axis=0,
        tiled=True,
    )
    back = lax.all_to_all(after(ret, prefix), "inst", split_axis=0, concat_axis=0, tiled=True)
    past = prefix_partials(q.reshape(req * rows, HD), prefix)
    past = [x.reshape(req, rows, HD) for x in past]
    out = final(me, slot_req, flags, back, here, past)
    return out.reshape(req, steps, width)


def solution(mesh):
    placed = (
        P("inst", None, "tp"),
        P("inst", None, "tp"),
        P("inst", None, "tp"),
        P("inst", None),
        P("inst"),
        P("inst", None, None),
        P(("inst", "tp"), None),
        P(),
        P("inst"),
    )
    return jax.shard_map(
        per_device, mesh=mesh, in_specs=placed, out_specs=P("inst", None, "tp"), check_vma=False
    )
```

time: 537 us -> 137 us (0.26); the launches traced: 526 us -> 135 us
  waiting for transfers between devices: 342 us -> 43.1 us
  local copies, waits for them, and re-layouts: 79.2 us -> 15.3 us
  other arithmetic: 35.5 us -> 0 us
  Pallas kernels: 0 us -> 35.3 us
  matrix products: 22 us -> 0 us
  blocking collectives: 0 us -> 18.3 us
  between operations: 14.3 us -> 0.85 us
  starting transfers between devices: 32.9 us -> 21.9 us
    psum x1 -> x0, waiting for transfers between devices: 306 us -> none  [spread(): return lax.psum(jnp.where(mine, array, jnp.zeros_like(array)), axis)]
    gather x4 -> x0, local copies, waits for them, and re-layouts: 39.2 us -> none  [the longest x2 27.6 us: per_device(): gathered = store[flat_ids].reshape(req, maxb, block, heads_kv, 2, HD)]
    pallas_call x0 -> x5, Pallas kernels: none -> 35.3 us  [the longest x1 17.8 us: remote_partials(): pl.pallas_call(remote_kernel, out_shape=jax.ShapeDtypeStruct((n, height -...]
    dot_general x6 -> x0, matrix products: 22 us -> none  [the longest x1 8.27 us: request_partials(): jnp.einsum('rsngd,rjtnd->rjsngt', q_rows, blocks[:, :, :, :, 0], preferre...]
    all_to_all x0 -> x1, blocking collectives: none -> 18.3 us  [per_device(): lax.all_to_all(after(piece, asked), 'tp', split_axis=0, concat_axis=0, ti...]
    reduce_or x3 -> x0, other arithmetic: 18.2 us -> none  [part_stats(): top = jnp.where(jnp.any(valid, axis=-1), top, NEG)]
    reshape x6 -> x3, local copies, waits for them, and re-layouts: 18.2 us -> 0.79 us  [the longest x1 0.65 us: per_device(): return out.reshape(req, steps, width)]
    all_to_all x2 -> x4, starting transfers between devices: 32.9 us -> 21.9 us  [the longest x1 9.37 us: per_device(): lax.all_to_all(prefix_store.reshape(n, tokens, wide), 'inst', split_axis=...]
  transfers between devices with their start and end apart: 3 -> 4, of which waited for: 3 -> 3; matrix products, arithmetic and copies ran while one was open for 12% -> 0% of each run, Pallas kernels for 0% -> 25%
where the time goes in v1:
time: 137 us; the launch traced here: 135 us
  waiting for transfers between devices  43.1 us (31%)
  Pallas kernels  35.3 us (26%)
  starting transfers between devices  21.9 us (16%)
  blocking collectives  18.3 us (13%)
  local copies, waits for them, and re-layouts  15.3 us (11%)
    all_to_all x1, waiting for transfers between devices, per_device(): lax.all_to_all(prefix_store.reshape(n, tokens, wide), 'inst', split_axis=...  24.8 us
    all_to_all x1, blocking collectives, per_device(): lax.all_to_all(after(piece, asked), 'tp', split_axis=0, concat_axis=0, ti...  18.3 us
    pallas_call x1, Pallas kernels, remote_partials(): pl.pallas_call(remote_kernel, out_shape=jax.ShapeDtypeStruct((n, height -...  17.8 us
    unnamed x38, local copies, waits for them, and re-layouts  12.9 us
    all_to_all x1, waiting for transfers between devices, per_device(): asked = lax.all_to_all(pay, 'inst', split_axis=0, concat_axis=0, tiled=True)  10.4 us
    all_to_all x1, starting transfers between devices, per_device(): lax.all_to_all(prefix_store.reshape(n, tokens, wide), 'inst', split_axis=...  9.37 us
    all_to_all x1, waiting for transfers between devices, per_device(): lax.all_to_all(jnp.broadcast_to(piece[None], (n,) + piece.shape), 'inst',...  7.83 us
    pallas_call x1, Pallas kernels, prefix_partials(): pl.pallas_call(prefix_kernel, out_shape=(one, one, one), in_specs=[VMEM,...  6.43 us
  transfers between devices with their start and end apart: 4, of which 3 were waited for; matrix products, arithmetic and copies ran while one was open for 0% of the time, Pallas kernels for 25%

profile of v1, /device:TPU:1, one launch (start us, length us, event | category | flops | bytes accessed | tf_op | source)
XLA Modules:
  0.0 134.7 jit_solution(2519915920216820997)
XLA Ops:
  0.0 9.4 %all-to-all-start.1 = ((bf16[32,16,2048]{2,1,0:T(8,128)(2,1)}), bf16[32,16,2048]{2,1,0:T(8,128)(2,1)S(1)}, u32[]{:S(2)}, u32[]{:S(2)}) async-start(bf16[32,16,2048]{2,1,0:T(8,128)(2,1)} %bitcast.17), calls=%async_computation.1 | async-start | bytes 4194304 | tf_op jit(solution)/shard_map/all_to_all | solution.py:324
  9.5 3.4 %prep.1 = (bf16[32,80,128]{2,1,0:T(8,128)(2,1)}, s32[3,16]{1,0:T(4,128)S(1)}, s32[64]{0:T(128)S(1)}) custom-call(s32[8,32]{1,0:T(8,128)S(1)} %copy-done.12, s32[8]{0:T(128)S(1)} %copy-done.13, bf16[8,32,128]{2,1,0:T(8,128)(2,1)S(1)} %reshape.30.q), custom_call_target="tpu_custom_call" | custom-call | bytes 12000000 | tf_op jit(solution)/shard_map/prep/pallas_call | solution.py:100
  12.8 24.8 %all-to-all-done.1 = bf16[32,16,2048]{2,1,0:T(8,128)(2,1)S(1)} async-done(((bf16[32,16,2048]{2,1,0:T(8,128)(2,1)}), bf16[32,16,2048]{2,1,0:T(8,128)(2,1)S(1)}, u32[]{:S(2)}, u32[]{:S(2)}) %all-to-all-start.1) | async-done | bytes 2097184 | tf_op jit(solution)/shard_map/all_to_all | solution.py:324
  37.6 3.9 %all-to-all-start = ((bf16[32,80,128]{2,1,0:T(8,128)(2,1)}), bf16[32,80,128]{2,1,0:T(8,128)(2,1)S(1)}, u32[]{:S(2)}, u32[]{:S(2)}) async-start(bf16[32,80,128]{2,1,0:T(8,128)(2,1)} %get-tuple-element.17), calls=%async_computation | async-start | bytes 1310720 | tf_op jit(solution)/shard_map/all_to_all | solution.py:329
  42.2 10.4 %all-to-all-done.pay = bf16[32,80,128]{2,1,0:T(8,128)(2,1)S(1)} async-done(((bf16[32,80,128]{2,1,0:T(8,128)(2,1)}), bf16[32,80,128]{2,1,0:T(8,128)(2,1)S(1)}, u32[]{:S(2)}, u32[]{:S(2)}) %all-to-all-start) | async-done | bytes 655392 | tf_op jit(solution)/shard_map/all_to_all | solution.py:329
  52.7 18.3 %all_to_all.25 = bf16[8,16,256]{2,1,0:T(8,128)(2,1)S(1)} all-to-all(bf16[8,16,256]{2,1,0:T(8,128)(2,1)S(1)} %copy.14), channel_id=1, replica_groups=mesh['inst'=32,'tp'=8] {'tp'}, dimensions={0} | all-to-all | bytes 131072 | tf_op jit(solution)/shard_map/all_to_all | solution.py:332
  71.0 1.6 %broadcast_in_dim.2 = bf16[32,8,16,256]{3,2,1,0:T(8,128)(2,1)} broadcast(bf16[8,16,256]{2,1,0:T(8,128)(2,1)S(1)} %all_to_all.25), dimensions={1,2,3} | broadcast | bytes 2162688 | tf_op jit(solution)/shard_map/broadcast_in_dim | solution.py:339
  72.6 4.1 %all-to-all-start.3 = ((bf16[32,8,16,256]{3,2,1,0:T(8,128)(2,1)}), bf16[32,8,16,256]{3,2,1,0:T(8,128)(2,1)S(1)}, u32[]{:S(2)}, u32[]{:S(2)}) async-start(bf16[32,8,16,256]{3,2,1,0:T(8,128)(2,1)} %broadcast_in_dim.2), calls=%async_computation.3 | async-start | bytes 4194304 | tf_op jit(solution)/shard_map/all_to_all | solution.py:338
  77.0 2.5 %copy-done = bf16[80,128,256]{2,1,0:T(8,128)(2,1)S(1)} copy-done((bf16[80,128,256]{2,1,0:T(8,128)(2,1)S(1)}, bf16[80,128,256]{2,1,0:T(8,128)(2,1)}, u32[]{:S(2)}) %copy-start) | copy-done | bytes 5242904
  79.4 17.8 %remote_partials.1 = f32[32,72,128]{2,1,0:T(8,128)} custom-call(s32[64]{0:T(128)S(1)} %reshape.31.outbox, bf16[80,128,256]{2,1,0:T(8,128)(2,1)S(1)} %copy-done, bf16[32,80,128]{2,1,0:T(8,128)(2,1)S(1)} %all-to-all-done.pay), custom_call_target="tpu_custom_call" | custom-call | bytes 24000000 | tf_op jit(solution)/shard_map/remote_partials/pallas_call | solution.py:148
  97.3 7.8 %all-to-all-done.3.kv = bf16[32,8,16,256]{3,2,1,0:T(8,128)(2,1)S(1)} async-done(((bf16[32,8,16,256]{3,2,1,0:T(8,128)(2,1)}), bf16[32,8,16,256]{3,2,1,0:T(8,128)(2,1)S(1)}, u32[]{:S(2)}, u32[]{:S(2)}) %all-to-all-start.3) | async-done | bytes 2097184 | tf_op jit(solution)/shard_map/all_to_all | solution.py:338
  105.1 4.4 %all-to-all-start.4 = ((f32[32,72,128]{2,1,0:T(8,128)}), f32[32,72,128]{2,1,0:T(8,128)S(1)}, u32[]{:S(2)}, u32[]{:S(2)}) async-start(f32[32,72,128]{2,1,0:T(8,128)} %remote_partials.1), calls=%async_computation.4 | async-start | bytes 2359296 | tf_op jit(solution)/shard_map/all_to_all | solution.py:345
  109.6 2.5 %copy-done.1 = bf16[80,128,256]{2,1,0:T(8,128)(2,1)S(1)} copy-done((bf16[80,128,256]{2,1,0:T(8,128)(2,1)S(1)}, bf16[80,128,256]{2,1,0:T(8,128)(2,1)}, u32[]{:S(2)}) %copy-start.1) | copy-done | bytes 5242904
  112.1 5.7 %local_partials.1 = (f32[8,32,128]{2,1,0:T(8,128)S(1)}, f32[8,32,128]{2,1,0:T(8,128)S(1)}, f32[8,32,128]{2,1,0:T(8,128)S(1)}) custom-call(s32[3,16]{1,0:T(4,128)S(1)} %get-tuple-element.20.local, bf16[80,128,256]{2,1,0:T(8,128)(2,1)S(1)} %copy-done.1, bf16[8,32,128]{2,1,0:T(8,128)(2,1)S(1)} %reshape.30.q, bf16[8,16,256]{2,1,0:T(8,128)(2,1)S(1)} %pad.4.fresh), custom_call_target="tpu_custom_call" | custom-call | bytes 18000000 | tf_op jit(solution)/shard_map/local_partials/pallas_call | solution.py:197
  117.9 0.7 copy-done.2
  119.2 6.4 %prefix_partials.1 = (f32[256,128]{1,0:T(8,128)S(1)}, f32[256,128]{1,0:T(8,128)S(1)}, f32[256,128]{1,0:T(8,128)S(1)}) custom-call(bf16[256,128]{1,0:T(8,128)(2,1)S(1)} %reshape_reshape.3.q, bf16[32,8,16,256]{3,2,1,0:T(8,128)(2,1)S(1)} %all-to-all-done.3.kv), custom_call_target="tpu_custom_call" | custom-call | bytes 24000000 | tf_op jit(solution)/shard_map/prefix_partials/pallas_call | solution.py:240
  126.9 0.7 copy-done.10
  127.6 0.9 copy-done.3
  128.5 0.9 copy-done.5
  129.4 0.9 copy-done.7
  130.3 0.9 copy-done.9
  131.2 0.9 copy-done.11
  132.1 2.0 %final.1 = bf16[8,32,128]{2,1,0:T(8,128)(2,1)S(1)} custom-call(s32[1]{0:T(128)} %bitcast.me, s32[64]{0:T(128)S(1)} %get-tuple-element.16.slot_req, s32[8]{0:T(128)S(1)} %copy-done.14, f32[32,72,128]{2,1,0:T(8,128)S(1)} %all-to-all-done.4.ret, f32[8,32,128]{2,1,0:T(8,128)S(1)} %get-tuple-element.21.lo, f32[8,32,128]{2,1,0:T(8,128)S(1)} %copy-done.3, ...), custom_call_target="tpu_custom_call" | custom-call | bytes 12000000 | tf_op jit(solution)/shard_map/final/pallas_call | solution.py:297
  134.1 0.6 reshape.37
  (36 shorter events, 2.3 us)
Async XLA Ops:
  0.0 9.4 %copy-start.15 = (bf16[8,4,1024]{2,1,0:T(4,128)(2,1)S(1)}, bf16[8,4,1024]{2,1,0:T(4,128)(2,1)}, u32[]{:S(2)}) copy-start(bf16[8,4,1024]{2,1,0:T(4,128)(2,1)} %param.9) | copy-start | bytes 196612
  0.0 9.4 %copy-start.12 = (s32[8,32]{1,0:T(8,128)S(1)}, s32[8,32]{1,0:T(8,128)}, u32[]{:S(2)}) copy-start(s32[8,32]{1,0:T(8,128)} %page.1) | copy-start | bytes 3076
  0.0 9.4 %copy-start.13 = (s32[8]{0:T(128)S(1)}, s32[8]{0:T(128)}, u32[]{:S(2)}) copy-start(s32[8]{0:T(128)} %lens.1) | copy-start | bytes 100
  0.0 37.6 %all-to-all-start.1 = ((bf16[32,16,2048]{2,1,0:T(8,128)(2,1)}), bf16[32,16,2048]{2,1,0:T(8,128)(2,1)S(1)}, u32[]{:S(2)}, u32[]{:S(2)}) async-start(bf16[32,16,2048]{2,1,0:T(8,128)(2,1)} %bitcast.17), calls=%async_computation.1 | async-start | bytes 4194304 | tf_op jit(solution)/shard_map/all_to_all | solution.py:324
  37.6 15.0 %all-to-all-start = ((bf16[32,80,128]{2,1,0:T(8,128)(2,1)}), bf16[32,80,128]{2,1,0:T(8,128)(2,1)S(1)}, u32[]{:S(2)}, u32[]{:S(2)}) async-start(bf16[32,80,128]{2,1,0:T(8,128)(2,1)} %get-tuple-element.17), calls=%async_computation | async-start | bytes 1310720 | tf_op jit(solution)/shard_map/all_to_all | solution.py:329
  72.6 4.2 %copy-start.17 = (s32[1,32,2]{1,2,0:T(2,128)S(1)}, s32[1,32,2]{1,2,0:T(2,128)}, u32[]{:S(2)}) copy-start(s32[1,32,2]{1,2,0:T(2,128)} %param.14) | copy-start | bytes 772
  72.6 32.5 %all-to-all-start.3 = ((bf16[32,8,16,256]{3,2,1,0:T(8,128)(2,1)}), bf16[32,8,16,256]{3,2,1,0:T(8,128)(2,1)S(1)}, u32[]{:S(2)}, u32[]{:S(2)}) async-start(bf16[32,8,16,256]{3,2,1,0:T(8,128)(2,1)} %broadcast_in_dim.2), calls=%async_computation.3 | async-start | bytes 4194304 | tf_op jit(solution)/shard_map/all_to_all | solution.py:338
  77.0 2.5 %copy-start = (bf16[80,128,256]{2,1,0:T(8,128)(2,1)S(1)}, bf16[80,128,256]{2,1,0:T(8,128)(2,1)}, u32[]{:S(2)}) copy-start(bf16[80,128,256]{2,1,0:T(8,128)(2,1)} %pool.3) | copy-start | bytes 15728644
  97.3 12.3 %copy-start.16 = (bf16[8,4,256]{2,1,0:T(4,128)(2,1)S(1)}, bf16[8,4,256]{2,1,0:T(4,128)(2,1)}, u32[]{:S(2)}) copy-start(bf16[8,4,256]{2,1,0:T(4,128)(2,1)} %param.10) | copy-start | bytes 49156
  105.1 22.5 %all-to-all-start.4 = ((f32[32,72,128]{2,1,0:T(8,128)}), f32[32,72,128]{2,1,0:T(8,128)S(1)}, u32[]{:S(2)}, u32[]{:S(2)}) async-start(f32[32,72,128]{2,1,0:T(8,128)} %remote_partials.1), calls=%async_computation.4 | async-start | bytes 2359296 | tf_op jit(solution)/shard_map/all_to_all | solution.py:345
  109.6 2.5 %copy-start.1 = (bf16[80,128,256]{2,1,0:T(8,128)(2,1)S(1)}, bf16[80,128,256]{2,1,0:T(8,128)(2,1)}, u32[]{:S(2)}) copy-start(bf16[80,128,256]{2,1,0:T(8,128)(2,1)} %pool.3) | copy-start | bytes 15728644
  117.8 0.7 copy-start.2
  118.5 0.6 copy-start.4
  119.2 8.4 %copy-start.14 = (s32[8]{0:T(128)S(1)}, s32[8]{0:T(128)}, u32[]{:S(2)}) copy-start(s32[8]{0:T(128)} %flags.1) | copy-start | bytes 100
  125.6 0.7 copy-start.6
  126.3 0.6 copy-start.8
  126.9 0.7 copy-start.10
  127.6 0.9 copy-start.3
  128.5 0.9 copy-start.5
  129.4 0.9 copy-start.7
  130.3 0.9 copy-start.9
  131.2 0.9 copy-start.11

commit v2 on v1

v2 whole, which is shorter than its diff:
```python
import functools

import jax
import jax.numpy as jnp
from jax import lax
from jax.experimental import pallas as pl
from jax.experimental.pallas import tpu as pltpu
from jax.sharding import PartitionSpec as P

HD = 128
BLK = 128
CAP = 2
KEPT = 16
NEG = -1e30
XS = 4
ZS = 2
F32 = jnp.float32
BF16 = jnp.bfloat16

VMEM = pl.BlockSpec(memory_space=pltpu.VMEM)
SMEM = pl.BlockSpec(memory_space=pltpu.SMEM)


def params():
    return pltpu.CompilerParams(vmem_limit_bytes=16 * 1024 * 1024)


def cost(us):
    return pl.CostEstimate(flops=0, bytes_accessed=int(us * 3.0e6), transcendentals=0)


def dot_nt(a, b):
    return lax.dot_general(a, b, (((1,), (1,)), ((), ())), preferred_element_type=F32)


def dot_nn(a, b):
    return lax.dot_general(a, b, (((1,), (0,)), ((), ())), preferred_element_type=F32)


def with_ones(values):
    return jnp.concatenate([values, jnp.ones_like(values)], axis=1)


def batch_partials(jobs):
    rows = jobs[0][0].shape[0]
    scores = jnp.concatenate([dot_nt(q, keys) for q, keys, _, _ in jobs], axis=0) * (HD ** -0.5)
    masked = jobs[0][3] is not None
    if masked:
        valid = jnp.concatenate([job[3] for job in jobs], axis=0)
        scores = jnp.where(valid, scores, NEG)
    top = jnp.max(scores, axis=-1, keepdims=True)
    weights = jnp.exp(scores - top)
    if masked:
        weights = jnp.where(valid, weights, 0.0)
    weights = weights.astype(BF16)
    found = []
    for i, (_, _, values, _) in enumerate(jobs):
        both = dot_nn(weights[i * rows : (i + 1) * rows], with_ones(values))
        found.append((top[i * rows : (i + 1) * rows], both[:, HD:], both[:, :HD]))
    return found


def prep_kernel(pool_size, page, lens, local, slot_req, counts):
    for k in range(KEPT):
        for field in range(3):
            local[field, k] = 0

    def request(r, kept):
        length = lens[r]

        def block(j, kept):
            b = page[r, j]
            valid = jnp.minimum(length - j * BLK, BLK)
            away = b >= pool_size

            @pl.when(away)
            def _():
                slot_req[b - pool_size] = r
                counts[b - pool_size] = valid

            @pl.when(jnp.logical_not(away))
            def _():
                local[0, kept] = b
                local[1, kept] = r
                local[2, kept] = valid

            return kept + jnp.where(away, 0, 1)

        return lax.fori_loop(0, lax.shift_right_logical(length + BLK - 1, 7), block, kept)

    lax.fori_loop(0, lens.shape[0], request, 0)


def prep(page, lengths, pool_size, slots):
    return pl.pallas_call(
        functools.partial(prep_kernel, pool_size),
        out_shape=(
            jax.ShapeDtypeStruct((3, KEPT), jnp.int32),
            jax.ShapeDtypeStruct((slots,), jnp.int32),
            jax.ShapeDtypeStruct((slots,), jnp.int32),
        ),
        in_specs=[SMEM, SMEM],
        out_specs=(SMEM, SMEM, SMEM),
        compiler_params=params(),
        cost_estimate=cost(3),
        name="prep",
    )(page, lengths)


def pack_kernel(spots, slot_req, counts, hold, q, c0, c1, c2, c3, pay):
    rows = q.shape[1]
    body = CAP * rows
    upper = lax.broadcasted_iota(jnp.int32, (16, HD), 0) < 8
    tokens = c0.shape[0] // len(spots)
    for d in range(len(spots)):
        for c in range(CAP):
            pay[d, c * rows : (c + 1) * rows, :] = q[slot_req[CAP * d + c]]
        tile = jnp.where(upper, counts[CAP * d], counts[CAP * d + 1])
        pay[d, body : body + 16, :] = tile.astype(F32).astype(BF16)
    for k, source in enumerate((c0, c1, c2, c3)):

        @pl.when(hold[0] == k)
        def _():
            for d, spot in enumerate(spots):
                for j in range(source.shape[1] // HD):
                    at = body + 16 + j * tokens
                    pay[d, at : at + tokens, :] = source[
                        spot * tokens : (spot + 1) * tokens, j * HD : (j + 1) * HD
                    ]


def pack(spots, slot_req, counts, hold, q, columns):
    n = len(spots)
    rows = q.shape[1]
    held, wide = columns[0].shape
    height = CAP * rows + 16 + (wide // HD) * (held // n)
    return pl.pallas_call(
        functools.partial(pack_kernel, spots),
        out_shape=jax.ShapeDtypeStruct((n, height, HD), BF16),
        in_specs=[SMEM, SMEM, SMEM] + [VMEM] * 5,
        out_specs=VMEM,
        compiler_params=params(),
        cost_estimate=cost(1.5),
        name="pack",
    )(slot_req, counts, hold, q, *columns)


def remote_kernel(outbox, pool, pay, ret):
    n = pay.shape[0]
    rows = (ret.shape[1] - 8) // CAP
    each = BLK // rows
    lane = lax.broadcasted_iota(jnp.int32, (rows, BLK), 1)

    def group(g, carry):
        jobs = []
        for i in range(each):
            d = g * each + i
            marks = pay[d, CAP * rows : CAP * rows + 16, :].astype(F32).astype(jnp.int32)
            for c in range(CAP):
                kv = pool[outbox[d * CAP + c]]
                valid = lane < marks[8 * c : 8 * c + 1, :]
                jobs.append((pay[d, c * rows : (c + 1) * rows, :], kv[:, :HD], kv[:, HD:], valid))
        found = batch_partials(jobs)
        stats = []
        for i in range(each):
            stat = jnp.zeros((rows, BLK), F32)
            for c in range(CAP):
                top, total, out = found[i * CAP + c]
                ret[g * each + i, c * rows : (c + 1) * rows, :] = out
                stat = jnp.where(lane == 2 * c, top, stat)
                stat = jnp.where(lane == 2 * c + 1, total, stat)
            stats.append(stat)
        turned = jnp.concatenate(stats, axis=0).T[:8]
        for i in range(each):
            ret[g * each + i, CAP * rows : CAP * rows + 8, :] = turned
        return carry

    lax.fori_loop(0, n // each, group, 0)


def remote_partials(outbox, pool, pay, rows):
    n = pay.shape[0]
    return pl.pallas_call(
        remote_kernel,
        out_shape=jax.ShapeDtypeStruct((n, CAP * rows + 8, HD), F32),
        in_specs=[SMEM, VMEM, VMEM],
        out_specs=VMEM,
        compiler_params=params(),
        cost_estimate=cost(8),
        name="remote_partials",
    )(outbox, pool, pay)


def local_kernel(local, pool, q, fresh, out_o, out_m, out_l):
    req, rows, _ = q.shape
    steps = rows // 8
    keys = fresh.shape[1]
    step = lax.broadcasted_iota(jnp.int32, (rows, keys), 0) // 8
    place = lax.broadcasted_iota(jnp.int32, (rows, keys), 1)
    causal = (place <= step) & (place < steps)
    found = batch_partials([(q[r], fresh[r, :, :HD], fresh[r, :, HD:], causal) for r in range(req)])
    for r, (top, total, out) in enumerate(found):
        out_o[r] = out
        out_l[r] = total
        out_m[r] = jnp.broadcast_to(top, (rows, HD))
    lane = lax.broadcasted_iota(jnp.int32, (rows, BLK), 1)

    def batch(g, carry):
        jobs = []
        for i in range(8):
            k = g * 8 + i
            kv = pool[local[0, k]]
            jobs.append((q[local[1, k]], kv[:, :HD], kv[:, HD:], lane < local[2, k]))
        found = batch_partials(jobs)
        for i in range(8):
            r = local[1, g * 8 + i]
            top, total, out = found[i]
            old = out_m[r]
            new = jnp.maximum(old, top)
            keep, add = jnp.exp(old - new), jnp.exp(top - new)
            out_m[r] = new
            out_l[r] = out_l[r] * keep + total * add
            out_o[r] = out_o[r] * keep + out * add
        return carry

    lax.fori_loop(0, KEPT // 8, batch, 0)


def local_partials(local, pool, q, fresh):
    one = jax.ShapeDtypeStruct(q.shape, F32)
    return pl.pallas_call(
        local_kernel,
        out_shape=(one, one, one),
        in_specs=[SMEM, VMEM, VMEM, VMEM],
        out_specs=(VMEM, VMEM, VMEM),
        compiler_params=params(),
        cost_estimate=cost(6),
        name="local_partials",
    )(local, pool, q, fresh)


def prefix_kernel(q0, q1, q2, q3, kv, p0, p1, p2, p3, q, out_o, out_m, out_l):
    pieces, shares, double, _ = kv.shape
    tokens = double // 2
    part = q0.shape[0]
    for s, source in enumerate((q0, q1, q2, q3)):
        q[s * part : (s + 1) * part, :] = source[...]
    out_o[...] = jnp.zeros_like(out_o)
    out_l[...] = jnp.zeros_like(out_l)
    out_m[...] = jnp.full_like(out_m, NEG)

    def pair(t, carry):
        jobs = []
        for b in range(2):
            keys = kv[:, 2 * t + b, :tokens].reshape(BLK, HD)
            values = kv[:, 2 * t + b, tokens:].reshape(BLK, HD)
            jobs.append((q[...], keys, values, None))
        found = batch_partials(jobs)
        old = out_m[...]
        new = jnp.maximum(jnp.maximum(old, found[0][0]), found[1][0])
        keep = jnp.exp(old - new)
        acc_l, acc_o = out_l[...] * keep, out_o[...] * keep
        for top, total, out in found:
            add = jnp.exp(top - new)
            acc_l = acc_l + total * add
            acc_o = acc_o + out * add
        out_m[...] = new
        out_l[...] = acc_l
        out_o[...] = acc_o
        return carry

    lax.fori_loop(0, shares // 2, pair, 0)
    lane = lax.broadcasted_iota(jnp.int32, (BLK, HD), 1)
    for s, target in enumerate((p0, p1, p2, p3)):
        target[:part, :] = out_o[s * part : (s + 1) * part, :]
        for k in range(part // BLK):
            at = s * part + k * BLK
            stat = jnp.where(lane == 0, out_m[at : at + BLK, :], out_l[at : at + BLK, :])
            target[part + 8 * k : part + 8 * k + 8, :] = stat.T[:8]


def prefix_partials(queries, kv):
    part = queries[0].shape[0]
    one = jax.ShapeDtypeStruct((part + 8 * (part // BLK), HD), F32)
    whole = pltpu.VMEM((XS * part, HD), F32)
    return pl.pallas_call(
        prefix_kernel,
        out_shape=(one,) * XS,
        in_specs=[VMEM] * (XS + 1),
        out_specs=(VMEM,) * XS,
        scratch_shapes=[pltpu.VMEM((XS * part, HD), BF16), whole, whole, whole],
        compiler_params=params(),
        cost_estimate=cost(6),
        name="prefix_partials",
    )(*queries, kv)


def final_kernel(me, slot_req, flags, ret, lo, lm, ll, p0, p1, p2, p3, out, top, total, acc, turned, past):
    req, rows, _ = lo.shape
    n = ret.shape[0]
    batch = min(16, n)
    body = CAP * rows
    part = req * rows
    tiles = part // BLK
    per = BLK // rows
    parts = (p0, p1, p2, p3)
    past[...] = jnp.concatenate([p[part:, :] for p in parts], axis=0).T
    for g in range(n // batch):
        turned[g] = ret[g * batch : (g + 1) * batch, body : body + 8, :].reshape(batch * 8, BLK).T
    mine = pl.multiple_of(lax.rem(me[0], per) * rows, rows)

    def past_stat(p, r, field):
        col = (p * tiles + r // per) * 8 + field
        return past[(r % per) * rows : (r % per + 1) * rows, col : col + 1]

    for r in range(req):
        use = flags[r] == 1
        peak = lm[r]
        for p in range(XS):
            peak = jnp.maximum(peak, jnp.where(use, past_stat(p, r, 0), NEG))
        top[r] = peak
    for g in range(n // batch):
        stats = turned[g, pl.ds(mine, rows), :]
        for i in range(batch):
            for c in range(CAP):
                r = slot_req[(g * batch + i) * CAP + c]
                col = 8 * i + 2 * c
                top[r] = jnp.maximum(top[r], stats[:, col : col + 1])
    for r in range(req):
        use = flags[r] == 1
        peak = top[r]
        factor = jnp.exp(lm[r] - peak)
        sum_l, sum_o = ll[r] * factor, lo[r] * factor
        for p in range(XS):
            factor = jnp.exp(jnp.where(use, past_stat(p, r, 0), NEG) - peak)
            sum_l = sum_l + past_stat(p, r, 1) * factor
            sum_o = sum_o + parts[p][r * rows : (r + 1) * rows, :] * factor
        total[r] = sum_l
        acc[r] = sum_o
    for g in range(n // batch):
        stats = turned[g, pl.ds(mine, rows), :]
        for i in range(batch):
            for c in range(CAP):
                s = g * batch + i
                r = slot_req[s * CAP + c]
                col = 8 * i + 2 * c
                factor = jnp.exp(stats[:, col : col + 1] - top[r])
                total[r] += stats[:, col + 1 : col + 2] * factor
                acc[r] += ret[s, c * rows : (c + 1) * rows, :] * factor
    for r in range(req):
        out[r] = (acc[r] / total[r]).astype(BF16)


def final(me, slot_req, flags, ret, here, past):
    req, rows, _ = here[0].shape
    n = ret.shape[0]
    batch = min(16, n)
    whole = pltpu.VMEM((req, rows, HD), F32)
    return pl.pallas_call(
        final_kernel,
        out_shape=jax.ShapeDtypeStruct((req, rows, HD), BF16),
        in_specs=[SMEM, SMEM, SMEM] + [VMEM] * (4 + XS),
        out_specs=VMEM,
        scratch_shapes=[
            whole,
            whole,
            whole,
            pltpu.VMEM((n // batch, BLK, batch * 8), F32),
            pltpu.VMEM((BLK, XS * (req * rows // BLK) * 8), F32),
        ],
        compiler_params=params(),
        cost_estimate=cost(3),
        name="final",
    )(me, slot_req, flags, ret, *here, *past)


def after(value, *others):
    return lax.optimization_barrier((value, others))[0]


def per_device(queries, new_kv, pool, page, lengths, outbox, prefix_store, owner, flags):
    req, steps, width = queries.shape
    pool_size = pool.shape[0]
    rows = steps * (width // HD)
    n = lax.axis_size("inst")
    shares = lax.axis_size("tp")
    ys = n // (XS * ZS)
    plane = ys * ZS
    me = lax.axis_index("inst").astype(jnp.int32)
    owned = owner[0]

    def index(y, x, z):
        return ((y % ys) * XS + x % XS) * ZS + z % ZS

    def move(value, dy, dx, dz):
        pairs = [
            (index(y, x, z), index(y + dy, x + dx, z + dz))
            for y in range(ys)
            for x in range(XS)
            for z in range(ZS)
        ]
        return lax.ppermute(value, "inst", pairs)

    steps_out = ((0, 0, 0), (0, 0, 1), (0, 1, 0), (1, 0, 0))
    wide = prefix_store.shape[1] // len(steps_out)
    columns = []
    holders = []
    for k, (dy, dx, dz) in enumerate(steps_out):
        part = prefix_store[:, k * wide : (k + 1) * wide]
        columns.append(move(part, dy, dx, dz) if k else part)
        holders.append(index(owned // (XS * ZS) + dy, owned // ZS + dx, owned + dz))
    hold = sum(jnp.where(me == holders[k], k, 0) for k in range(1, len(steps_out)))
    spots = [
        ((i // ZS) % XS) * plane + (i // (XS * ZS)) * ZS + i % ZS for i in range(n)
    ]

    q = queries.reshape(req, rows, HD)
    local, slot_req, counts = prep(page, lengths, pool_size, n * CAP)
    pay = pack(spots, slot_req, counts, hold.reshape(1), q, columns)
    asked = lax.all_to_all(pay, "inst", split_axis=0, concat_axis=0, tiled=True)
    flat = after(q.reshape(req * rows, HD), pay)
    guests = [flat] + [move(flat, 0, s, 0) for s in range(1, XS)]
    fresh = jnp.pad(new_kv, ((0, 0), (0, 16 - steps), (0, 0)))
    here = local_partials(local, pool, q, fresh)
    head = CAP * rows + 16
    piece = jnp.concatenate(
        [
            lax.dynamic_slice(asked, (h, head, 0), (1, asked.shape[1] - head, HD))
            for h in holders
        ],
        axis=0,
    ).reshape(shares, -1, HD)
    piece = lax.all_to_all(
        after(piece, *guests, *here), "tp", split_axis=0, concat_axis=0, tiled=True
    )
    ret = remote_partials(outbox.reshape(-1), pool, asked, rows)
    planes = [[index(y, x, z) for y in range(ys) for z in range(ZS)] for x in range(XS)]
    prefix = lax.all_to_all(
        jnp.broadcast_to(after(piece, ret)[None], (plane,) + piece.shape),
        "inst",
        split_axis=0,
        concat_axis=0,
        tiled=True,
        axis_index_groups=planes,
    )
    back = lax.all_to_all(after(ret, prefix), "inst", split_axis=0, concat_axis=0, tiled=True)
    past = prefix_partials(guests, prefix)
    past = [past[0]] + [move(past[s], 0, -s, 0) for s in range(1, XS)]
    out = final(me.reshape(1), slot_req, flags, back, here, past)
    return out.reshape(req, steps, width)


def solution(mesh):
    placed = (
        P("inst", None, "tp"),
        P("inst", None, "tp"),
        P("inst", None, "tp"),
        P("inst", None),
        P("inst"),
        P("inst", None, None),
        P(("inst", "tp"), None),
        P(),
        P("inst"),
    )
    return jax.shard_map(
        per_device, mesh=mesh, in_specs=placed, out_specs=P("inst", None, "tp"), check_vma=False
    )
```

time: 137 us -> 108 us (0.79); the launches traced: 135 us -> 107 us
  Pallas kernels: 35.3 us -> 17.9 us
  starting transfers between devices: 21.9 us -> 34.2 us
  waiting for transfers between devices: 43.1 us -> 31.5 us
  local copies, waits for them, and re-layouts: 15.3 us -> 8.52 us
  blocking collectives: 18.3 us -> 13.5 us
    all_to_all x2 -> x1, waiting for transfers between devices: 32.6 us -> 0.01 us  [per_device(): lax.all_to_all(after(piece, *guests, *here), 'tp', split_axis=0, concat_a...]
    ppermute x0 -> x9, waiting for transfers between devices: none -> 24 us  [move(): return lax.ppermute(value, 'inst', pairs)]
    ppermute x0 -> x9, starting transfers between devices: none -> 13.4 us  [move(): return lax.ppermute(value, 'inst', pairs)]
    pallas_call x2 -> x3, Pallas kernels: 24.3 us -> 11.3 us  [the longest x1 5.74 us: remote_partials(): pl.pallas_call(remote_kernel, out_shape=jax.ShapeDtypeStruct((n, CAP * ro...]
    unnamed x38 -> x17, local copies, waits for them, and re-layouts: 12.9 us -> 5.07 us
    all_to_all x1, blocking collectives: 18.3 us -> 13.5 us  [per_device(): lax.all_to_all(jnp.broadcast_to(after(piece, ret)[None], (plane,) + piece...]
    pallas_call x1, Pallas kernels: 5.72 us -> 1.91 us  [local_partials(): pl.pallas_call(local_kernel, out_shape=(one, one, one), in_specs=[SMEM, V...]
    all_to_all x1, waiting for transfers between devices: 10.4 us -> 7.49 us  [per_device(): asked = lax.all_to_all(pay, 'inst', split_axis=0, concat_axis=0, tiled=True)]
  transfers between devices with their start and end apart: 4 -> 12, of which waited for: 3 -> 8; matrix products, arithmetic and copies ran while one was open for 0% -> 1% of each run, Pallas kernels for 25% -> 13%
where the time goes in v2:
time: 108 us; the launch traced here: 107 us
  starting transfers between devices  34.2 us (32%)
  waiting for transfers between devices  31.5 us (29%)
  Pallas kernels  17.9 us (17%)
  blocking collectives  13.5 us (12%)
  local copies, waits for them, and re-layouts  8.52 us (8%)
    ppermute x9, waiting for transfers between devices, move(): return lax.ppermute(value, 'inst', pairs)  24 us
    all_to_all x1, blocking collectives, per_device(): lax.all_to_all(jnp.broadcast_to(after(piece, ret)[None], (plane,) + piece...  13.5 us
    ppermute x9, starting transfers between devices, move(): return lax.ppermute(value, 'inst', pairs)  13.4 us
    all_to_all x1, starting transfers between devices, per_device(): lax.all_to_all(after(piece, *guests, *here), 'tp', split_axis=0, concat_a...  11.2 us
    all_to_all x1, waiting for transfers between devices, per_device(): asked = lax.all_to_all(pay, 'inst', split_axis=0, concat_axis=0, tiled=True)  7.49 us
    pallas_call x1, Pallas kernels, remote_partials(): pl.pallas_call(remote_kernel, out_shape=jax.ShapeDtypeStruct((n, CAP * ro...  5.74 us
    all_to_all x1, starting transfers between devices, per_device(): asked = lax.all_to_all(pay, 'inst', split_axis=0, concat_axis=0, tiled=True)  5.54 us
    unnamed x17, local copies, waits for them, and re-layouts  5.07 us
  transfers between devices with their start and end apart: 12, of which 8 were waited for; matrix products, arithmetic and copies ran while one was open for 1% of the time, Pallas kernels for 13%

profile of v2, /device:TPU:1, one launch (start us, length us, event | category | flops | bytes accessed | tf_op | source)
XLA Modules:
  0.0 107.2 jit_solution(17459029286980053791)
XLA Ops:
  0.0 2.5 %fusion = (bf16[512,512]{1,0:T(8,128)(2,1)S(1)}, bf16[512,512]{1,0:T(8,128)(2,1)}, bf16[512,512]{1,0:T(8,128)(2,1)S(1)}, bf16[512,512]{1,0:T(8,128)(2,1)S(1)}) fusion(bf16[512,2048]{1,0:T(8,128)(2,1)} %param.15), kind=kLoop, calls=%fused_computation.5 | loop fusion | bytes 4194304 | tf_op jit(solution)/shard_map/slice | solution.py:409
  2.5 2.5 %collective-permute-start = (bf16[512,512]{1,0:T(8,128)(2,1)}, bf16[512,512]{1,0:T(8,128)(2,1)S(1)}, u32[]{:S(2)}, u32[]{:S(2)}) collective-permute-start(bf16[512,512]{1,0:T(8,128)(2,1)} %get-tuple-element.34), channel_id=1, source_target_pairs={{0,8},{8,0},{16,24},{24,16},{32,40},{40,32},{48,56},{56,48},{64,72... | collective-permute-start | bytes 1572872 | tf_op jit(solution)/shard_map/ppermute | solution.py:402
  6.2 1.3 %collective-permute-start.2 = (bf16[512,512]{1,0:T(8,128)(2,1)S(1)}, bf16[512,512]{1,0:T(8,128)(2,1)S(1)}, u32[]{:S(2)}, u32[]{:S(2)}) collective-permute-start(bf16[512,512]{1,0:T(8,128)(2,1)S(1)} %get-tuple-element.33), channel_id=1, source_target_pairs={{0,64},{8,72},{16,80},{24,88},{32,96},{40,104},{48,112},{56,120},{... | collective-permute-start | bytes 1572872 | tf_op jit(solution)/shard_map/ppermute | solution.py:402
  8.4 2.2 %prep.1 = (s32[3,16]{1,0:T(4,128)S(1)}, s32[64]{0:T(128)S(1)}, s32[64]{0:T(128)S(1)}) custom-call(s32[8,32]{1,0:T(8,128)S(1)} %copy-done.2, s32[8]{0:T(128)S(1)} %copy-done.4), custom_call_target="tpu_custom_call" | custom-call | bytes 9000000 | tf_op jit(solution)/shard_map/prep/pallas_call | solution.py:95
  10.6 5.3 %collective-permute-done.c1 = bf16[512,512]{1,0:T(8,128)(2,1)S(1)} collective-permute-done((bf16[512,512]{1,0:T(8,128)(2,1)}, bf16[512,512]{1,0:T(8,128)(2,1)S(1)}, u32[]{:S(2)}, u32[]{:S(2)}) %collective-permute-start) | collective-permute-done | bytes 524320 | tf_op jit(solution)/shard_map/ppermute | solution.py:402
  15.9 2.8 %collective-permute-done.1.c2 = bf16[512,512]{1,0:T(8,128)(2,1)S(1)} collective-permute-done((bf16[512,512]{1,0:T(8,128)(2,1)S(1)}, bf16[512,512]{1,0:T(8,128)(2,1)S(1)}, u32[]{:S(2)}, u32[]{:S(2)}) %collective-permute-start.1) | collective-permute-done | bytes 524320 | tf_op jit(solution)/shard_map/ppermute | solution.py:402
  19.7 1.8 %pack.1 = bf16[32,144,128]{2,1,0:T(8,128)(2,1)} custom-call(s32[64]{0:T(128)S(1)} %get-tuple-element.19.slot_req, s32[64]{0:T(128)S(1)} %get-tuple-element.20.counts, s32[1]{0:T(128)} %bitcast.2.hold, bf16[8,32,128]{2,1,0:T(8,128)(2,1)S(1)} %reshape.22.q, bf16[512,512]{1,0:T(8,128)(2,1)S(1)} %get-tuple-element.35.c0, ...), custom_call_target="tpu_custom_call" | custom-call | bytes 4500000 | tf_op jit(solution)/shard_map/pack/pallas_call | solution.py:137
  21.5 5.5 %all-to-all-start = ((bf16[32,144,128]{2,1,0:T(8,128)(2,1)}), bf16[32,144,128]{2,1,0:T(8,128)(2,1)S(1)}, u32[]{:S(2)}, u32[]{:S(2)}) async-start(bf16[32,144,128]{2,1,0:T(8,128)(2,1)} %pack.1), calls=%async_computation | async-start | bytes 2359296 | tf_op jit(solution)/shard_map/all_to_all | solution.py:420
  27.2 2.5 %copy-done = bf16[80,128,256]{2,1,0:T(8,128)(2,1)S(1)} copy-done((bf16[80,128,256]{2,1,0:T(8,128)(2,1)S(1)}, bf16[80,128,256]{2,1,0:T(8,128)(2,1)}, u32[]{:S(2)}) %copy-start) | copy-done | bytes 5242904
  29.7 1.9 %local_partials.1 = (f32[8,32,128]{2,1,0:T(8,128)S(1)}, f32[8,32,128]{2,1,0:T(8,128)S(1)}, f32[8,32,128]{2,1,0:T(8,128)S(1)}) custom-call(s32[3,16]{1,0:T(4,128)S(1)} %get-tuple-element.22.local, bf16[80,128,256]{2,1,0:T(8,128)(2,1)S(1)} %copy-done, bf16[8,32,128]{2,1,0:T(8,128)(2,1)S(1)} %reshape.22.q, bf16[8,16,256]{2,1,0:T(8,128)(2,1)S(1)} %pad.4.fresh), custom_call_target="tpu_custom_call" | custom-call | bytes 18000000 | tf_op jit(solution)/shard_map/local_partials/pallas_call | solution.py:231
  31.6 1.3 %collective-permute-start.3 = (bf16[256,128]{1,0:T(8,128)(2,1)S(1)}, bf16[256,128]{1,0:T(8,128)(2,1)S(1)}, u32[]{:S(2)}, u32[]{:S(2)}) collective-permute-start(bf16[256,128]{1,0:T(8,128)(2,1)S(1)} %reshape_reshape.3.q0), channel_id=1, source_target_pairs={{0,16},{8,24},{16,32},{24,40},{32,48},{40,56},{48,0},{56,8},{64,80... | collective-permute-start | bytes 196616 | tf_op jit(solution)/shard_map/ppermute | solution.py:402
  32.9 2.4 %collective-permute-start.4 = (bf16[256,128]{1,0:T(8,128)(2,1)S(1)}, bf16[256,128]{1,0:T(8,128)(2,1)S(1)}, u32[]{:S(2)}, u32[]{:S(2)}) collective-permute-start(bf16[256,128]{1,0:T(8,128)(2,1)S(1)} %reshape_reshape.3.q0), channel_id=1, source_target_pairs={{0,32},{8,40},{16,48},{24,56},{32,0},{40,8},{48,16},{56,24},{64,96... | collective-permute-start | bytes 196616 | tf_op jit(solution)/shard_map/ppermute | solution.py:402
  36.5 7.5 %all-to-all-done.pay = bf16[32,144,128]{2,1,0:T(8,128)(2,1)S(1)} async-done(((bf16[32,144,128]{2,1,0:T(8,128)(2,1)}), bf16[32,144,128]{2,1,0:T(8,128)(2,1)S(1)}, u32[]{:S(2)}, u32[]{:S(2)}) %all-to-all-start) | async-done | bytes 1179680 | tf_op jit(solution)/shard_map/all_to_all | solution.py:420
  44.9 11.2 %all-to-all-start.1 = ((bf16[8,32,128]{2,1,0:T(8,128)(2,1)}), bf16[8,32,128]{2,1,0:T(8,128)(2,1)S(1)}, u32[]{:S(2)}, u32[]{:S(2)}) async-start(bf16[8,32,128]{2,1,0:T(8,128)(2,1)} %bitcast.3), calls=%async_computation.1 | async-start | bytes 131072 | tf_op jit(solution)/shard_map/all_to_all | solution.py:433
  56.3 2.5 %copy-done.1 = bf16[80,128,256]{2,1,0:T(8,128)(2,1)S(1)} copy-done((bf16[80,128,256]{2,1,0:T(8,128)(2,1)S(1)}, bf16[80,128,256]{2,1,0:T(8,128)(2,1)}, u32[]{:S(2)}) %copy-start.1) | copy-done | bytes 5242904
  58.8 5.7 %remote_partials.1 = f32[32,72,128]{2,1,0:T(8,128)} custom-call(s32[64]{0:T(128)S(1)} %reshape.20.outbox, bf16[80,128,256]{2,1,0:T(8,128)(2,1)S(1)} %copy-done.1, bf16[32,144,128]{2,1,0:T(8,128)(2,1)S(1)} %all-to-all-done.pay), custom_call_target="tpu_custom_call" | custom-call | bytes 24000000 | tf_op jit(solution)/shard_map/remote_partials/pallas_call | solution.py:183
  64.6 13.5 %all_to_all.20.kv = bf16[8,8,32,128]{3,2,1,0:T(8,128)(2,1)S(1)} all-to-all(bf16[8,8,32,128]{3,2,1,0:T(8,128)(2,1)S(1)} %broadcast_in_dim.2), channel_id=1, replica_groups={{0,8,64,72,128,136,192,200},{16,24,80,88,144,152,208,216},{32,40,96,104..., dimensions={0} | all-to-all | bytes 1048576 | tf_op jit(solution)/shard_map/all_to_all | solution.py:438
  78.1 4.1 %all-to-all-start.3 = ((f32[32,72,128]{2,1,0:T(8,128)}), f32[32,72,128]{2,1,0:T(8,128)S(1)}, u32[]{:S(2)}, u32[]{:S(2)}) async-start(f32[32,72,128]{2,1,0:T(8,128)} %remote_partials.1), calls=%async_computation.3 | async-start | bytes 2359296 | tf_op jit(solution)/shard_map/all_to_all | solution.py:446
  82.2 3.8 %prefix_partials.1 = (f32[272,128]{1,0:T(8,128)S(1)}, f32[272,128]{1,0:T(8,128)S(1)}, f32[272,128]{1,0:T(8,128)S(1)}, f32[272,128]{1,0:T(8,128)S(1)}) custom-call(bf16[256,128]{1,0:T(8,128)(2,1)S(1)} %reshape_reshape.3.q0, bf16[256,128]{1,0:T(8,128)(2,1)S(1)} %collective-permute-done.3.q1, bf16[256,128]{1,0:T(8,128)(2,1)S(1)} %collective-permute-done.4.q2, ...), custom_call_target="tpu_custom_call" | custom-call | bytes 18000000 | tf_op jit(solution)/shard_map/prefix_partials/pallas_call | solution.py:286
  86.0 2.4 %collective-permute-start.6 = (f32[272,128]{1,0:T(8,128)S(1)}, f32[272,128]{1,0:T(8,128)S(1)}, u32[]{:S(2)}, u32[]{:S(2)}) collective-permute-start(f32[272,128]{1,0:T(8,128)S(1)} %get-tuple-element.30), channel_id=1, source_target_pairs={{0,48},{8,56},{16,0},{24,8},{32,16},{40,24},{48,32},{56,40},{64,11... | collective-permute-start | bytes 417800 | tf_op jit(solution)/shard_map/ppermute | solution.py:402
  89.5 9.7 %collective-permute-done.6.p1 = f32[272,128]{1,0:T(8,128)S(1)} collective-permute-done((f32[272,128]{1,0:T(8,128)S(1)}, f32[272,128]{1,0:T(8,128)S(1)}, u32[]{:S(2)}, u32[]{:S(2)}) %collective-permute-start.6) | collective-permute-done | bytes 139296 | tf_op jit(solution)/shard_map/ppermute | solution.py:402
  99.2 1.2 %collective-permute-done.7.p2 = f32[272,128]{1,0:T(8,128)S(1)} collective-permute-done((f32[272,128]{1,0:T(8,128)S(1)}, f32[272,128]{1,0:T(8,128)S(1)}, u32[]{:S(2)}, u32[]{:S(2)}) %collective-permute-start.7) | collective-permute-done | bytes 139296 | tf_op jit(solution)/shard_map/ppermute | solution.py:402
  100.4 3.6 %collective-permute-done.8.p3 = f32[272,128]{1,0:T(8,128)S(1)} collective-permute-done((f32[272,128]{1,0:T(8,128)S(1)}, f32[272,128]{1,0:T(8,128)S(1)}, u32[]{:S(2)}, u32[]{:S(2)}) %collective-permute-start.8) | collective-permute-done | bytes 139296 | tf_op jit(solution)/shard_map/ppermute | solution.py:402
  104.1 2.5 %final.1 = bf16[8,32,128]{2,1,0:T(8,128)(2,1)S(1)} custom-call(s32[1]{0:T(128)} %bitcast.me, s32[64]{0:T(128)S(1)} %get-tuple-element.19.slot_req, s32[8]{0:T(128)S(1)} %copy-done.3, f32[32,72,128]{2,1,0:T(8,128)S(1)} %all-to-all-done.3.ret, f32[8,32,128]{2,1,0:T(8,128)S(1)} %get-tuple-element.23.lo, f32[8,32,128]{2,1,0:T(8,128)S(1)} %get-tuple-element.24.lm, ...), custom_call_target="tpu_custom_call" | custom-call | bytes 9000000 | tf_op jit(solution)/shard_map/final/pallas_call | solution.py:359
  (33 shorter events, 6.6 us)
Async XLA Ops:
  0.0 8.3 %copy-start.5 = (bf16[8,4,1024]{2,1,0:T(4,128)(2,1)S(1)}, bf16[8,4,1024]{2,1,0:T(4,128)(2,1)}, u32[]{:S(2)}) copy-start(bf16[8,4,1024]{2,1,0:T(4,128)(2,1)} %param.9) | copy-start | bytes 196612
  0.0 8.4 %copy-start.2 = (s32[8,32]{1,0:T(8,128)S(1)}, s32[8,32]{1,0:T(8,128)}, u32[]{:S(2)}) copy-start(s32[8,32]{1,0:T(8,128)} %page.1) | copy-start | bytes 3076
  0.0 8.4 %copy-start.4 = (s32[8]{0:T(128)S(1)}, s32[8]{0:T(128)}, u32[]{:S(2)}) copy-start(s32[8]{0:T(128)} %lens.1) | copy-start | bytes 100
  2.5 13.4 %collective-permute-start = (bf16[512,512]{1,0:T(8,128)(2,1)}, bf16[512,512]{1,0:T(8,128)(2,1)S(1)}, u32[]{:S(2)}, u32[]{:S(2)}) collective-permute-start(bf16[512,512]{1,0:T(8,128)(2,1)} %get-tuple-element.34), channel_id=1, source_target_pairs={{0,8},{8,0},{16,24},{24,16},{32,40},{40,32},{48,56},{56,48},{64,72... | collective-permute-start | bytes 1572872 | tf_op jit(solution)/shard_map/ppermute | solution.py:402
  5.0 13.7 %collective-permute-start.1 = (bf16[512,512]{1,0:T(8,128)(2,1)S(1)}, bf16[512,512]{1,0:T(8,128)(2,1)S(1)}, u32[]{:S(2)}, u32[]{:S(2)}) collective-permute-start(bf16[512,512]{1,0:T(8,128)(2,1)S(1)} %get-tuple-element.36), channel_id=1, source_target_pairs={{0,16},{8,24},{16,32},{24,40},{32,48},{40,56},{48,0},{56,8},{64,80... | collective-permute-start | bytes 1572872 | tf_op jit(solution)/shard_map/ppermute | solution.py:402
  6.2 13.5 %collective-permute-start.2 = (bf16[512,512]{1,0:T(8,128)(2,1)S(1)}, bf16[512,512]{1,0:T(8,128)(2,1)S(1)}, u32[]{:S(2)}, u32[]{:S(2)}) collective-permute-start(bf16[512,512]{1,0:T(8,128)(2,1)S(1)} %get-tuple-element.33), channel_id=1, source_target_pairs={{0,64},{8,72},{16,80},{24,88},{32,96},{40,104},{48,112},{56,120},{... | collective-permute-start | bytes 1572872 | tf_op jit(solution)/shard_map/ppermute | solution.py:402
  21.5 5.6 %copy-start.6 = (bf16[8,4,256]{2,1,0:T(4,128)(2,1)S(1)}, bf16[8,4,256]{2,1,0:T(4,128)(2,1)}, u32[]{:S(2)}) copy-start(bf16[8,4,256]{2,1,0:T(4,128)(2,1)} %param.10) | copy-start | bytes 49156
  21.5 22.4 %all-to-all-start = ((bf16[32,144,128]{2,1,0:T(8,128)(2,1)}), bf16[32,144,128]{2,1,0:T(8,128)(2,1)S(1)}, u32[]{:S(2)}, u32[]{:S(2)}) async-start(bf16[32,144,128]{2,1,0:T(8,128)(2,1)} %pack.1), calls=%async_computation | async-start | bytes 2359296 | tf_op jit(solution)/shard_map/all_to_all | solution.py:420
  27.2 2.5 %copy-start = (bf16[80,128,256]{2,1,0:T(8,128)(2,1)S(1)}, bf16[80,128,256]{2,1,0:T(8,128)(2,1)}, u32[]{:S(2)}) copy-start(bf16[80,128,256]{2,1,0:T(8,128)(2,1)} %pool.3) | copy-start | bytes 15728644
  29.7 26.5 %copy-start.7 = (s32[1,32,2]{1,2,0:T(2,128)S(1)}, s32[1,32,2]{1,2,0:T(2,128)}, u32[]{:S(2)}) copy-start(s32[1,32,2]{1,2,0:T(2,128)} %param.14) | copy-start | bytes 772
  31.6 13.0 %collective-permute-start.3 = (bf16[256,128]{1,0:T(8,128)(2,1)S(1)}, bf16[256,128]{1,0:T(8,128)(2,1)S(1)}, u32[]{:S(2)}, u32[]{:S(2)}) collective-permute-start(bf16[256,128]{1,0:T(8,128)(2,1)S(1)} %reshape_reshape.3.q0), channel_id=1, source_target_pairs={{0,16},{8,24},{16,32},{24,40},{32,48},{40,56},{48,0},{56,8},{64,80... | collective-permute-start | bytes 196616 | tf_op jit(solution)/shard_map/ppermute | solution.py:402
  32.9 12.1 %collective-permute-start.4 = (bf16[256,128]{1,0:T(8,128)(2,1)S(1)}, bf16[256,128]{1,0:T(8,128)(2,1)S(1)}, u32[]{:S(2)}, u32[]{:S(2)}) collective-permute-start(bf16[256,128]{1,0:T(8,128)(2,1)S(1)} %reshape_reshape.3.q0), channel_id=1, source_target_pairs={{0,32},{8,40},{16,48},{24,56},{32,0},{40,8},{48,16},{56,24},{64,96... | collective-permute-start | bytes 196616 | tf_op jit(solution)/shard_map/ppermute | solution.py:402
  35.3 9.7 %collective-permute-start.5 = (bf16[256,128]{1,0:T(8,128)(2,1)S(1)}, bf16[256,128]{1,0:T(8,128)(2,1)S(1)}, u32[]{:S(2)}, u32[]{:S(2)}) collective-permute-start(bf16[256,128]{1,0:T(8,128)(2,1)S(1)} %reshape_reshape.3.q0), channel_id=1, source_target_pairs={{0,48},{8,56},{16,0},{24,8},{32,16},{40,24},{48,32},{56,40},{64,11... | collective-permute-start | bytes 196616 | tf_op jit(solution)/shard_map/ppermute | solution.py:402
  44.9 19.6 %all-to-all-start.1 = ((bf16[8,32,128]{2,1,0:T(8,128)(2,1)}), bf16[8,32,128]{2,1,0:T(8,128)(2,1)S(1)}, u32[]{:S(2)}, u32[]{:S(2)}) async-start(bf16[8,32,128]{2,1,0:T(8,128)(2,1)} %bitcast.3), calls=%async_computation.1 | async-start | bytes 131072 | tf_op jit(solution)/shard_map/all_to_all | solution.py:433
  56.3 2.5 %copy-start.1 = (bf16[80,128,256]{2,1,0:T(8,128)(2,1)S(1)}, bf16[80,128,256]{2,1,0:T(8,128)(2,1)}, u32[]{:S(2)}) copy-start(bf16[80,128,256]{2,1,0:T(8,128)(2,1)} %pool.3) | copy-start | bytes 15728644
  78.1 26.0 %copy-start.3 = (s32[8]{0:T(128)S(1)}, s32[8]{0:T(128)}, u32[]{:S(2)}) copy-start(s32[8]{0:T(128)} %flags.1) | copy-start | bytes 100
  78.1 26.0 %all-to-all-start.3 = ((f32[32,72,128]{2,1,0:T(8,128)}), f32[32,72,128]{2,1,0:T(8,128)S(1)}, u32[]{:S(2)}, u32[]{:S(2)}) async-start(f32[32,72,128]{2,1,0:T(8,128)} %remote_partials.1), calls=%async_computation.3 | async-start | bytes 2359296 | tf_op jit(solution)/shard_map/all_to_all | solution.py:446
  86.0 13.2 %collective-permute-start.6 = (f32[272,128]{1,0:T(8,128)S(1)}, f32[272,128]{1,0:T(8,128)S(1)}, u32[]{:S(2)}, u32[]{:S(2)}) collective-permute-start(f32[272,128]{1,0:T(8,128)S(1)} %get-tuple-element.30), channel_id=1, source_target_pairs={{0,48},{8,56},{16,0},{24,8},{32,16},{40,24},{48,32},{56,40},{64,11... | collective-permute-start | bytes 417800 | tf_op jit(solution)/shard_map/ppermute | solution.py:402
  88.4 12.1 %collective-permute-start.7 = (f32[272,128]{1,0:T(8,128)S(1)}, f32[272,128]{1,0:T(8,128)S(1)}, u32[]{:S(2)}, u32[]{:S(2)}) collective-permute-start(f32[272,128]{1,0:T(8,128)S(1)} %get-tuple-element.31), channel_id=1, source_target_pairs={{0,32},{8,40},{16,48},{24,56},{32,0},{40,8},{48,16},{56,24},{64,96... | collective-permute-start | bytes 417800 | tf_op jit(solution)/shard_map/ppermute | solution.py:402
  88.9 15.1 %collective-permute-start.8 = (f32[272,128]{1,0:T(8,128)S(1)}, f32[272,128]{1,0:T(8,128)S(1)}, u32[]{:S(2)}, u32[]{:S(2)}) collective-permute-start(f32[272,128]{1,0:T(8,128)S(1)} %get-tuple-element.32), channel_id=1, source_target_pairs={{0,16},{8,24},{16,32},{24,40},{32,48},{40,56},{48,0},{56,8},{64,80... | collective-permute-start | bytes 417800 | tf_op jit(solution)/shard_map/ppermute | solution.py:402

commit v3 on v2

--- a/solution.py
+++ b/solution.py
@@ -107,25 +107,28 @@
     )(page, lengths)
 
 
-def pack_kernel(spots, slot_req, counts, hold, q, c0, c1, c2, c3, pay):
+def pack_kernel(spots, slot_req, counts, hold, q, *refs):
+    sources, pay = refs[:-1], refs[-1]
     rows = q.shape[1]
     body = CAP * rows
     upper = lax.broadcasted_iota(jnp.int32, (16, HD), 0) < 8
-    tokens = c0.shape[0] // len(spots)
+    tokens = sources[0].shape[0] // len(spots)
+    most = sources[0].shape[1] // HD
     for d in range(len(spots)):
         for c in range(CAP):
             pay[d, c * rows : (c + 1) * rows, :] = q[slot_req[CAP * d + c]]
         tile = jnp.where(upper, counts[CAP * d], counts[CAP * d + 1])
         pay[d, body : body + 16, :] = tile.astype(F32).astype(BF16)
-    for k, source in enumerate((c0, c1, c2, c3)):
+    for k, source in enumerate(sources):
 
         @pl.when(hold[0] == k)
         def _():
             for d, spot in enumerate(spots):
-                for j in range(source.shape[1] // HD):
+                for j in range(most):
                     at = body + 16 + j * tokens
+                    col = (j % (source.shape[1] // HD)) * HD
                     pay[d, at : at + tokens, :] = source[
-                        spot * tokens : (spot + 1) * tokens, j * HD : (j + 1) * HD
+                        spot * tokens : (spot + 1) * tokens, col : col + HD
                     ]
 
 
@@ -137,12 +140,35 @@
     return pl.pallas_call(
         functools.partial(pack_kernel, spots),
         out_shape=jax.ShapeDtypeStruct((n, height, HD), BF16),
-        in_specs=[SMEM, SMEM, SMEM] + [VMEM] * 5,
+        in_specs=[SMEM, SMEM, SMEM, VMEM] + [VMEM] * len(columns),
         out_specs=VMEM,
         compiler_params=params(),
         cost_estimate=cost(1.5),
         name="pack",
     )(slot_req, counts, hold, q, *columns)
+
+
+def gather_kernel(spans, holders, asked, out):
+    first = 0
+    head = asked.shape[1] - spans[0]
+    flat = out.shape[1]
+    for k, span in enumerate(spans):
+        for h in range(span // flat):
+            at = head + h * flat
+            out[first] = asked[holders[k], at : at + flat, :]
+            first += 1
+
+
+def gather(spans, holders, asked, shares):
+    return pl.pallas_call(
+        functools.partial(gather_kernel, spans),
+        out_shape=jax.ShapeDtypeStruct((shares, sum(spans) // shares, HD), BF16),
+        in_specs=[SMEM, VMEM],
+        out_specs=VMEM,
+        compiler_params=params(),
+        cost_estimate=cost(0.5),
+        name="gather",
+    )(holders, asked)
 
 
 def remote_kernel(outbox, pool, pay, ret):
@@ -186,7 +212,7 @@
         in_specs=[SMEM, VMEM, VMEM],
         out_specs=VMEM,
         compiler_params=params(),
-        cost_estimate=cost(8),
+        cost_estimate=cost(6),
         name="remote_partials",
     )(outbox, pool, pay)
 
@@ -240,7 +266,7 @@
 
 
 def prefix_kernel(q0, q1, q2, q3, kv, p0, p1, p2, p3, q, out_o, out_m, out_l):
-    pieces, shares, double, _ = kv.shape
+    chips, cores, double = kv.shape[1], kv.shape[3], kv.shape[4]
     tokens = double // 2
     part = q0.shape[0]
     for s, source in enumerate((q0, q1, q2, q3)):
@@ -251,9 +277,9 @@
 
     def pair(t, carry):
         jobs = []
-        for b in range(2):
-            keys = kv[:, 2 * t + b, :tokens].reshape(BLK, HD)
-            values = kv[:, 2 * t + b, tokens:].reshape(BLK, HD)
+        for b in range(cores):
+            keys = kv[:, t, :, b, :tokens].reshape(BLK, HD)
+            values = kv[:, t, :, b, tokens:].reshape(BLK, HD)
             jobs.append((q[...], keys, values, None))
         found = batch_partials(jobs)
         old = out_m[...]
@@ -269,7 +295,7 @@
         out_o[...] = acc_o
         return carry
 
-    lax.fori_loop(0, shares // 2, pair, 0)
+    lax.fori_loop(0, chips, pair, 0)
     lane = lax.broadcasted_iota(jnp.int32, (BLK, HD), 1)
     for s, target in enumerate((p0, p1, p2, p3)):
         target[:part, :] = out_o[s * part : (s + 1) * part, :]
@@ -295,30 +321,16 @@
     )(*queries, kv)
 
 
-def final_kernel(me, slot_req, flags, ret, lo, lm, ll, p0, p1, p2, p3, out, top, total, acc, turned, past):
+def merge_kernel(me, slot_req, ret, lo, lm, ll, acc, top, total, turned):
     req, rows, _ = lo.shape
     n = ret.shape[0]
     batch = min(16, n)
     body = CAP * rows
-    part = req * rows
-    tiles = part // BLK
     per = BLK // rows
-    parts = (p0, p1, p2, p3)
-    past[...] = jnp.concatenate([p[part:, :] for p in parts], axis=0).T
     for g in range(n // batch):
         turned[g] = ret[g * batch : (g + 1) * batch, body : body + 8, :].reshape(batch * 8, BLK).T
     mine = pl.multiple_of(lax.rem(me[0], per) * rows, rows)
-
-    def past_stat(p, r, field):
-        col = (p * tiles + r // per) * 8 + field
-        return past[(r % per) * rows : (r % per + 1) * rows, col : col + 1]
-
-    for r in range(req):
-        use = flags[r] == 1
-        peak = lm[r]
-        for p in range(XS):
-            peak = jnp.maximum(peak, jnp.where(use, past_stat(p, r, 0), NEG))
-        top[r] = peak
+    top[...] = lm[...]
     for g in range(n // batch):
         stats = turned[g, pl.ds(mine, rows), :]
         for i in range(batch):
@@ -327,16 +339,9 @@
                 col = 8 * i + 2 * c
                 top[r] = jnp.maximum(top[r], stats[:, col : col + 1])
     for r in range(req):
-        use = flags[r] == 1
-        peak = top[r]
-        factor = jnp.exp(lm[r] - peak)
-        sum_l, sum_o = ll[r] * factor, lo[r] * factor
-        for p in range(XS):
-            factor = jnp.exp(jnp.where(use, past_stat(p, r, 0), NEG) - peak)
-            sum_l = sum_l + past_stat(p, r, 1) * factor
-            sum_o = sum_o + parts[p][r * rows : (r + 1) * rows, :] * factor
-        total[r] = sum_l
-        acc[r] = sum_o
+        factor = jnp.exp(lm[r] - top[r])
+        total[r] = ll[r] * factor
+        acc[r] = lo[r] * factor
     for g in range(n // batch):
         stats = turned[g, pl.ds(mine, rows), :]
         for i in range(batch):
@@ -347,31 +352,64 @@
                 factor = jnp.exp(stats[:, col : col + 1] - top[r])
                 total[r] += stats[:, col + 1 : col + 2] * factor
                 acc[r] += ret[s, c * rows : (c + 1) * rows, :] * factor
-    for r in range(req):
-        out[r] = (acc[r] / total[r]).astype(BF16)
-
-
-def final(me, slot_req, flags, ret, here, past):
-    req, rows, _ = here[0].shape
+
+
+def merge(me, slot_req, ret, here):
     n = ret.shape[0]
     batch = min(16, n)
-    whole = pltpu.VMEM((req, rows, HD), F32)
+    one = jax.ShapeDtypeStruct(here[0].shape, F32)
+    return pl.pallas_call(
+        merge_kernel,
+        out_shape=(one, one, one),
+        in_specs=[SMEM, SMEM] + [VMEM] * 4,
+        out_specs=(VMEM, VMEM, VMEM),
+        scratch_shapes=[pltpu.VMEM((n // batch, BLK, batch * 8), F32)],
+        compiler_params=params(),
+        cost_estimate=cost(2),
+        name="merge",
+    )(me, slot_req, ret, *here)
+
+
+def final_kernel(flags, acc, top, total, p0, p1, p2, p3, out, past):
+    req, rows, _ = acc.shape
+    part = req * rows
+    tiles = part // BLK
+    per = BLK // rows
+    parts = (p0, p1, p2, p3)
+    past[...] = jnp.concatenate([p[part:, :] for p in parts], axis=0).T
+    for r in range(req):
+        use = flags[r] == 1
+        at = (r % per) * rows
+        tops, sums = [], []
+        for p in range(XS):
+            col = (p * tiles + r // per) * 8
+            stat = past[at : at + rows, col : col + 2]
+            tops.append(jnp.where(use, stat[:, 0:1], NEG))
+            sums.append(stat[:, 1:2])
+        peak = top[r]
+        for found in tops:
+            peak = jnp.maximum(peak, found)
+        factor = jnp.exp(top[r] - peak)
+        sum_l, sum_o = total[r] * factor, acc[r] * factor
+        for p in range(XS):
+            factor = jnp.exp(tops[p] - peak)
+            sum_l = sum_l + sums[p] * factor
+            sum_o = sum_o + parts[p][r * rows : (r + 1) * rows, :] * factor
+        out[r] = (sum_o / sum_l).astype(BF16)
+
+
+def final(flags, merged, past):
+    req, rows, _ = merged[0].shape
     return pl.pallas_call(
         final_kernel,
         out_shape=jax.ShapeDtypeStruct((req, rows, HD), BF16),
-        in_specs=[SMEM, SMEM, SMEM] + [VMEM] * (4 + XS),
+        in_specs=[SMEM] + [VMEM] * (3 + XS),
         out_specs=VMEM,
-        scratch_shapes=[
-            whole,
-            whole,
-            whole,
-            pltpu.VMEM((n // batch, BLK, batch * 8), F32),
-            pltpu.VMEM((BLK, XS * (req * rows // BLK) * 8), F32),
-        ],
-        compiler_params=params(),
-        cost_estimate=cost(3),
+        scratch_shapes=[pltpu.VMEM((BLK, XS * (req * rows // BLK) * 8), F32)],
+        compiler_params=params(),
+        cost_estimate=cost(1),
         name="final",
-    )(me, slot_req, flags, ret, *here, *past)
+    )(flags, *merged, *past)
 
 
 def after(value, *others):
@@ -401,13 +439,22 @@
         ]
         return lax.ppermute(value, "inst", pairs)
 
-    steps_out = ((0, 0, 0), (0, 0, 1), (0, 1, 0), (1, 0, 0))
-    wide = prefix_store.shape[1] // len(steps_out)
+    steps_out = (
+        (2, 0, 0, 0),
+        (2, 0, 0, 1),
+        (1, 0, 1, 0),
+        (1, 0, -1, 0),
+        (1, 1, 0, 0),
+        (1, -1, 0, 0),
+    )
+    head_width = prefix_store.shape[1] // shares
     columns = []
     holders = []
-    for k, (dy, dx, dz) in enumerate(steps_out):
-        part = prefix_store[:, k * wide : (k + 1) * wide]
-        columns.append(move(part, dy, dx, dz) if k else part)
+    first = 0
+    for heads, dy, dx, dz in steps_out:
+        part = prefix_store[:, first * head_width : (first + heads) * head_width]
+        first += heads
+        columns.append(move(part, dy, dx, dz) if holders else part)
         holders.append(index(owned // (XS * ZS) + dy, owned // ZS + dx, owned + dz))
     hold = sum(jnp.where(me == holders[k], k, 0) for k in range(1, len(steps_out)))
     spots = [
@@ -416,37 +463,52 @@
 
     q = queries.reshape(req, rows, HD)
     local, slot_req, counts = prep(page, lengths, pool_size, n * CAP)
+    tokens = prefix_store.shape[0] // n
+    spans = tuple(heads * 2 * tokens for heads, _, _, _ in steps_out)
     pay = pack(spots, slot_req, counts, hold.reshape(1), q, columns)
     asked = lax.all_to_all(pay, "inst", split_axis=0, concat_axis=0, tiled=True)
-    flat = after(q.reshape(req * rows, HD), pay)
-    guests = [flat] + [move(flat, 0, s, 0) for s in range(1, XS)]
     fresh = jnp.pad(new_kv, ((0, 0), (0, 16 - steps), (0, 0)))
     here = local_partials(local, pool, q, fresh)
-    head = CAP * rows + 16
-    piece = jnp.concatenate(
+    piece = gather(spans, jnp.stack(holders).astype(jnp.int32), asked, shares)
+    piece = after(piece, *here)
+
+    tp = lax.axis_index("tp").astype(jnp.int32)
+    cores = 2
+    chips = shares // cores
+    core = tp % cores
+    piece = piece.reshape(chips, cores, -1, HD)
+    mine = lax.dynamic_index_in_dim(piece, core, 1, keepdims=False)
+    other = lax.dynamic_index_in_dim(piece, 1 - core, 1, keepdims=False)
+    other = lax.ppermute(other, "tp", [(t, t ^ 1) for t in range(shares)])
+    both = jnp.stack([mine, other], axis=1)
+    sheets = [
         [
-            lax.dynamic_slice(asked, (h, head, 0), (1, asked.shape[1] - head, HD))
-            for h in holders
-        ],
-        axis=0,
-    ).reshape(shares, -1, HD)
-    piece = lax.all_to_all(
-        after(piece, *guests, *here), "tp", split_axis=0, concat_axis=0, tiled=True
-    )
-    ret = remote_partials(outbox.reshape(-1), pool, asked, rows)
-    planes = [[index(y, x, z) for y in range(ys) for z in range(ZS)] for x in range(XS)]
+            index(y, x, z) * shares + chip * cores + c
+            for y in range(ys)
+            for chip in range(chips)
+            for z in range(ZS)
+        ]
+        for x in range(XS)
+        for c in range(cores)
+    ]
+    flat = after(q.reshape(req * rows, HD), both)
+    guests = [flat] + [move(flat, 0, s, 0) for s in range(1, XS)]
+    whole = (ys, chips, ZS) + both.shape[1:]
+    spread = jnp.broadcast_to(both[None, :, None], whole)
     prefix = lax.all_to_all(
-        jnp.broadcast_to(after(piece, ret)[None], (plane,) + piece.shape),
-        "inst",
+        spread.reshape((-1,) + both.shape[1:]),
+        ("inst", "tp"),
         split_axis=0,
         concat_axis=0,
         tiled=True,
-        axis_index_groups=planes,
-    )
-    back = lax.all_to_all(after(ret, prefix), "inst", split_axis=0, concat_axis=0, tiled=True)
+        axis_index_groups=sheets,
+    ).reshape(whole)
+    ret = remote_partials(outbox.reshape(-1), pool, asked, rows)
+    back = lax.all_to_all(after(ret, prefix, *guests), "inst", split_axis=0, concat_axis=0, tiled=True)
     past = prefix_partials(guests, prefix)
     past = [past[0]] + [move(past[s], 0, -s, 0) for s in range(1, XS)]
-    out = final(me.reshape(1), slot_req, flags, back, here, past)
+    merged = merge(me.reshape(1), slot_req, back, here)
+    out = final(flags, merged, past)
     return out.reshape(req, steps, width)
 
 

time: 108 us -> 102 us (0.944)
  blocking collectives: 13.5 us -> 0 us
  starting transfers between devices: 34.2 us -> 42.6 us
  waiting for transfers between devices: 31.5 us -> 29.7 us
  Pallas kernels: 17.9 us -> 19 us
    ppermute x9 -> x11, waiting for transfers between devices: 24 us -> 4.09 us  [move(): return lax.ppermute(value, 'inst', pairs)]
    all_to_all x1 -> x0, blocking collectives: 13.5 us -> none  [per_device(): lax.all_to_all(jnp.broadcast_to(after(piece, ret)[None], (plane,) + piece...]
    all_to_all x2, waiting for transfers between devices: 0.01 us -> 12.1 us  [the longest x1 9.83 us: per_device(): lax.all_to_all(after(ret, prefix, *guests), 'inst', split_axis=0, concat_...]
    all_to_all x1, waiting for transfers between devices: 7.49 us -> 12.7 us  [per_device(): asked = lax.all_to_all(pay, 'inst', split_axis=0, concat_axis=0, tiled=True)]
    ppermute x0 -> x1, starting transfers between devices: none -> 3.04 us  [per_device(): other = lax.ppermute(other, 'tp', [(t, t ^ 1) for t in range(shares)])]
    all_to_all x1, starting transfers between devices: 5.54 us -> 8.58 us  [per_device(): asked = lax.all_to_all(pay, 'inst', split_axis=0, concat_axis=0, tiled=True)]
    pallas_call x0 -> x2, Pallas kernels: none -> 2.48 us  [the longest x1 1.93 us: merge(): pl.pallas_call(merge_kernel, out_shape=(one, one, one), in_specs=[SMEM, S...]
    ppermute x9 -> x11, starting transfers between devices: 13.4 us -> 15 us  [move(): return lax.ppermute(value, 'inst', pairs)]
  transfers between devices with their start and end apart: 12 -> 15, of which waited for: 8 -> 6; matrix products, arithmetic and copies ran while one was open for 1% -> 1% of each run, Pallas kernels for 13% -> 15%
where the time goes in v3:
time: 102 us
  starting transfers between devices  42.6 us (42%)
  waiting for transfers between devices  29.7 us (29%)
  Pallas kernels  19 us (19%)
  local copies, waits for them, and re-layouts  9.2 us (9%)
  between operations  1.11 us (1%)
    ppermute x11, starting transfers between devices, move(): return lax.ppermute(value, 'inst', pairs)  15 us
    all_to_all x1, waiting for transfers between devices, per_device(): asked = lax.all_to_all(pay, 'inst', split_axis=0, concat_axis=0, tiled=True)  12.7 us
    all_to_all x1, waiting for transfers between devices, per_device(): lax.all_to_all(after(ret, prefix, *guests), 'inst', split_axis=0, concat_...  9.83 us
    all_to_all x1, starting transfers between devices, per_device(): asked = lax.all_to_all(pay, 'inst', split_axis=0, concat_axis=0, tiled=True)  8.58 us
    all_to_all x1, starting transfers between devices, per_device(): lax.all_to_all(after(ret, prefix, *guests), 'inst', split_axis=0, concat_...  8.02 us
    all_to_all x1, starting transfers between devices, per_device(): lax.all_to_all(spread.reshape((-1,) + both.shape[1:]), ('inst', 'tp'), sp...  7.92 us
    pallas_call x1, Pallas kernels, remote_partials(): pl.pallas_call(remote_kernel, out_shape=jax.ShapeDtypeStruct((n, CAP * ro...  5.71 us
    unnamed x19, local copies, waits for them, and re-layouts  5.08 us
  transfers between devices with their start and end apart: 15, of which 6 were waited for; matrix products, arithmetic and copies ran while one was open for 1% of the time, Pallas kernels for 15%

profile of v3, /device:TPU:1, one launch (start us, length us, event | category | flops | bytes accessed | tf_op | source)
XLA Modules:
  0.0 101.7 jit_solution(1166928356653307397)
XLA Ops:
  0.0 1.4 %fusion.1 = (bf16[512,512]{1,0:T(8,128)(2,1)S(1)}, bf16[512,512]{1,0:T(8,128)(2,1)S(1)}) fusion(bf16[512,2048]{1,0:T(8,128)(2,1)} %param.15), kind=kLoop, calls=%fused_computation.4 | loop fusion | bytes 2097152 | tf_op jit(solution)/shard_map/slice | solution.py:455
  1.4 2.6 %collective-permute-start = (bf16[512,512]{1,0:T(8,128)(2,1)S(1)}, bf16[512,512]{1,0:T(8,128)(2,1)S(1)}, u32[]{:S(2)}, u32[]{:S(2)}) collective-permute-start(bf16[512,512]{1,0:T(8,128)(2,1)S(1)} %get-tuple-element.41), channel_id=1, source_target_pairs={{0,8},{8,0},{16,24},{24,16},{32,40},{40,32},{48,56},{56,48},{64,72... | collective-permute-start | bytes 1572872 | tf_op jit(solution)/shard_map/ppermute | solution.py:440
  6.1 1.5 %collective-permute-start.2 = (bf16[512,256]{1,0:T(8,128)(2,1)}, bf16[512,256]{1,0:T(8,128)(2,1)S(1)}, u32[]{:S(2)}, u32[]{:S(2)}) collective-permute-start(bf16[512,256]{1,0:T(8,128)(2,1)} %get-tuple-element.38), channel_id=1, source_target_pairs={{0,48},{8,56},{16,0},{24,8},{32,16},{40,24},{48,32},{56,40},{64,11... | collective-permute-start | bytes 786440 | tf_op jit(solution)/shard_map/ppermute | solution.py:440
  7.5 1.3 %collective-permute-start.3 = (bf16[512,256]{1,0:T(8,128)(2,1)S(1)}, bf16[512,256]{1,0:T(8,128)(2,1)S(1)}, u32[]{:S(2)}, u32[]{:S(2)}) collective-permute-start(bf16[512,256]{1,0:T(8,128)(2,1)S(1)} %get-tuple-element.40), channel_id=1, source_target_pairs={{0,64},{8,72},{16,80},{24,88},{32,96},{40,104},{48,112},{56,120},{... | collective-permute-start | bytes 786440 | tf_op jit(solution)/shard_map/ppermute | solution.py:440
  8.8 1.4 %collective-permute-start.4 = (bf16[512,256]{1,0:T(8,128)(2,1)S(1)}, bf16[512,256]{1,0:T(8,128)(2,1)S(1)}, u32[]{:S(2)}, u32[]{:S(2)}) collective-permute-start(bf16[512,256]{1,0:T(8,128)(2,1)S(1)} %get-tuple-element.37), channel_id=1, source_target_pairs={{0,192},{8,200},{16,208},{24,216},{32,224},{40,232},{48,240},{56,2... | collective-permute-start | bytes 786440 | tf_op jit(solution)/shard_map/ppermute | solution.py:440
  11.2 2.3 %prep.1 = (s32[3,16]{1,0:T(4,128)S(1)}, s32[64]{0:T(128)S(1)}, s32[64]{0:T(128)S(1)}) custom-call(s32[8,32]{1,0:T(8,128)S(1)} %copy-done.2, s32[8]{0:T(128)S(1)} %copy-done.4), custom_call_target="tpu_custom_call" | custom-call | bytes 9000000 | tf_op jit(solution)/shard_map/prep/pallas_call | solution.py:95
  13.5 1.4 %collective-permute-done.3.refs_4_ = bf16[512,256]{1,0:T(8,128)(2,1)S(1)} collective-permute-done((bf16[512,256]{1,0:T(8,128)(2,1)S(1)}, bf16[512,256]{1,0:T(8,128)(2,1)S(1)}, u32[]{:S(2)}, u32[]{:S(2)}) %collective-permute-start.3) | collective-permute-done | bytes 262176 | tf_op jit(solution)/shard_map/ppermute | solution.py:440
  15.0 1.8 %pack.1 = bf16[32,144,128]{2,1,0:T(8,128)(2,1)} custom-call(s32[64]{0:T(128)S(1)} %get-tuple-element.21.slot_req, s32[64]{0:T(128)S(1)} %get-tuple-element.22.counts, s32[1]{0:T(128)} %bitcast.2.hold, bf16[8,32,128]{2,1,0:T(8,128)(2,1)S(1)} %reshape.28.q, bf16[512,512]{1,0:T(8,128)(2,1)S(1)} %get-tuple-element.42.refs_0_, ...), custom_call_target="tpu_custom_call" | custom-call | bytes 4500000 | tf_op jit(solution)/shard_map/pack/pallas_call | solution.py:140
  16.7 8.6 %all-to-all-start = ((bf16[32,144,128]{2,1,0:T(8,128)(2,1)}), bf16[32,144,128]{2,1,0:T(8,128)(2,1)S(1)}, u32[]{:S(2)}, u32[]{:S(2)}) async-start(bf16[32,144,128]{2,1,0:T(8,128)(2,1)} %pack.1), calls=%async_computation | async-start | bytes 2359296 | tf_op jit(solution)/shard_map/all_to_all | solution.py:469
  25.4 2.5 %copy-done = bf16[80,128,256]{2,1,0:T(8,128)(2,1)S(1)} copy-done((bf16[80,128,256]{2,1,0:T(8,128)(2,1)S(1)}, bf16[80,128,256]{2,1,0:T(8,128)(2,1)}, u32[]{:S(2)}) %copy-start) | copy-done | bytes 5242904
  27.9 1.9 %local_partials.1 = (f32[8,32,128]{2,1,0:T(8,128)S(1)}, f32[8,32,128]{2,1,0:T(8,128)S(1)}, f32[8,32,128]{2,1,0:T(8,128)S(1)}) custom-call(s32[3,16]{1,0:T(4,128)S(1)} %get-tuple-element.23.local, bf16[80,128,256]{2,1,0:T(8,128)(2,1)S(1)} %copy-done, bf16[8,32,128]{2,1,0:T(8,128)(2,1)S(1)} %reshape.28.q, bf16[8,16,256]{2,1,0:T(8,128)(2,1)S(1)} %pad.4.fresh), custom_call_target="tpu_custom_call" | custom-call | bytes 18000000 | tf_op jit(solution)/shard_map/local_partials/pallas_call | solution.py:257
  29.9 12.7 %all-to-all-done.pay.asked = bf16[32,144,128]{2,1,0:T(8,128)(2,1)S(1)} async-done(((bf16[32,144,128]{2,1,0:T(8,128)(2,1)}), bf16[32,144,128]{2,1,0:T(8,128)(2,1)S(1)}, u32[]{:S(2)}, u32[]{:S(2)}) %all-to-all-start) | async-done | bytes 1179680 | tf_op jit(solution)/shard_map/all_to_all | solution.py:469
  43.2 3.0 %collective-permute-start.5 = (bf16[4,32,128]{2,1,0:T(8,128)(2,1)S(1)}, bf16[4,32,128]{2,1,0:T(8,128)(2,1)S(1)}, u32[]{:S(2)}, u32[]{:S(2)}) collective-permute-start(bf16[4,32,128]{2,1,0:T(8,128)(2,1)S(1)} %get-tuple-element.44), channel_id=1, source_target_pairs={{0,1},{1,0},{2,3},{3,2},{4,5},{5,4},{6,7},{7,6},{8,9},{9,8},{10,11... | collective-permute-start | bytes 98312 | tf_op jit(solution)/shard_map/ppermute | solution.py:482
  48.0 7.9 %all-to-all-start.1 = ((bf16[32,2,32,128]{3,2,1,0:T(8,128)(2,1)}), bf16[32,2,32,128]{3,2,1,0:T(8,128)(2,1)S(1)}, u32[]{:S(2)}, u32[]{:S(2)}) async-start(bf16[32,2,32,128]{3,2,1,0:T(8,128)(2,1)} %bitcast.12), calls=%async_computation.1 | async-start | bytes 1048576 | tf_op jit(solution)/shard_map/all_to_all | solution.py:498
  56.4 1.8 %collective-permute-start.7 = (bf16[256,128]{1,0:T(8,128)(2,1)S(1)}, bf16[256,128]{1,0:T(8,128)(2,1)S(1)}, u32[]{:S(2)}, u32[]{:S(2)}) collective-permute-start(bf16[256,128]{1,0:T(8,128)(2,1)S(1)} %reshape_reshape.3.q0), channel_id=1, source_target_pairs={{0,32},{8,40},{16,48},{24,56},{32,0},{40,8},{48,16},{56,24},{64,96... | collective-permute-start | bytes 196616 | tf_op jit(solution)/shard_map/ppermute | solution.py:440
  59.6 2.5 %copy-done.1 = bf16[80,128,256]{2,1,0:T(8,128)(2,1)S(1)} copy-done((bf16[80,128,256]{2,1,0:T(8,128)(2,1)S(1)}, bf16[80,128,256]{2,1,0:T(8,128)(2,1)}, u32[]{:S(2)}) %copy-start.1) | copy-done | bytes 5242904
  62.1 5.7 %remote_partials.1 = f32[32,72,128]{2,1,0:T(8,128)} custom-call(s32[64]{0:T(128)S(1)} %reshape.26.outbox, bf16[80,128,256]{2,1,0:T(8,128)(2,1)S(1)} %copy-done.1, bf16[32,144,128]{2,1,0:T(8,128)(2,1)S(1)} %all-to-all-done.pay.asked), custom_call_target="tpu_custom_call" | custom-call | bytes 18000000 | tf_op jit(solution)/shard_map/remote_partials/pallas_call | solution.py:209
  67.8 2.2 %all-to-all-done.1 = bf16[32,2,32,128]{3,2,1,0:T(8,128)(2,1)S(1)} async-done(((bf16[32,2,32,128]{3,2,1,0:T(8,128)(2,1)}), bf16[32,2,32,128]{3,2,1,0:T(8,128)(2,1)S(1)}, u32[]{:S(2)}, u32[]{:S(2)}) %all-to-all-start.1) | async-done | bytes 524320 | tf_op jit(solution)/shard_map/all_to_all | solution.py:498
  70.0 8.0 %all-to-all-start.2 = ((f32[32,72,128]{2,1,0:T(8,128)}), f32[32,72,128]{2,1,0:T(8,128)S(1)}, u32[]{:S(2)}, u32[]{:S(2)}) async-start(f32[32,72,128]{2,1,0:T(8,128)} %remote_partials.1), calls=%async_computation.2 | async-start | bytes 2359296 | tf_op jit(solution)/shard_map/all_to_all | solution.py:507
  78.1 3.8 %prefix_partials.1 = (f32[272,128]{1,0:T(8,128)S(1)}, f32[272,128]{1,0:T(8,128)S(1)}, f32[272,128]{1,0:T(8,128)S(1)}, f32[272,128]{1,0:T(8,128)S(1)}) custom-call(bf16[256,128]{1,0:T(8,128)(2,1)S(1)} %reshape_reshape.3.q0, bf16[256,128]{1,0:T(8,128)(2,1)S(1)} %collective-permute-done.6.q1, bf16[256,128]{1,0:T(8,128)(2,1)S(1)} %collective-permute-done.7.q2, ...), custom_call_target="tpu_custom_call" | custom-call | bytes 18000000 | tf_op jit(solution)/shard_map/prefix_partials/pallas_call | solution.py:312
  81.8 2.5 %collective-permute-start.9 = (f32[272,128]{1,0:T(8,128)S(1)}, f32[272,128]{1,0:T(8,128)S(1)}, u32[]{:S(2)}, u32[]{:S(2)}) collective-permute-start(f32[272,128]{1,0:T(8,128)S(1)} %get-tuple-element.34), channel_id=1, source_target_pairs={{0,48},{8,56},{16,0},{24,8},{32,16},{40,24},{48,32},{56,40},{64,11... | collective-permute-start | bytes 417800 | tf_op jit(solution)/shard_map/ppermute | solution.py:440
  85.5 9.8 %all-to-all-done.2.ret = f32[32,72,128]{2,1,0:T(8,128)S(1)} async-done(((f32[32,72,128]{2,1,0:T(8,128)}), f32[32,72,128]{2,1,0:T(8,128)S(1)}, u32[]{:S(2)}, u32[]{:S(2)}) %all-to-all-start.2) | async-done | bytes 1179680 | tf_op jit(solution)/shard_map/all_to_all | solution.py:507
  95.3 1.9 %merge.1 = (f32[8,32,128]{2,1,0:T(8,128)S(1)}, f32[8,32,128]{2,1,0:T(8,128)S(1)}, f32[8,32,128]{2,1,0:T(8,128)S(1)}) custom-call(s32[1]{0:T(128)} %bitcast.me, s32[64]{0:T(128)S(1)} %get-tuple-element.21.slot_req, f32[32,72,128]{2,1,0:T(8,128)S(1)} %all-to-all-done.2.ret, f32[8,32,128]{2,1,0:T(8,128)S(1)} %get-tuple-element.24.lo, ...), custom_call_target="tpu_custom_call" | custom-call | bytes 6000000 | tf_op jit(solution)/shard_map/merge/pallas_call | solution.py:361
  97.3 2.6 %collective-permute-done.11.p3 = f32[272,128]{1,0:T(8,128)S(1)} collective-permute-done((f32[272,128]{1,0:T(8,128)S(1)}, f32[272,128]{1,0:T(8,128)S(1)}, u32[]{:S(2)}, u32[]{:S(2)}) %collective-permute-start.11) | collective-permute-done | bytes 139296 | tf_op jit(solution)/shard_map/ppermute | solution.py:440
  (44 shorter events, 9.4 us)
Async XLA Ops:
  0.0 4.0 %copy-start.5 = (bf16[512,2048]{1,0:T(8,128)(2,1)S(1)}, bf16[512,2048]{1,0:T(8,128)(2,1)}, u32[]{:S(2)}) copy-start(bf16[512,2048]{1,0:T(8,128)(2,1)} %param.15) | copy-start | bytes 6291460
  0.0 11.1 %copy-start.6 = (bf16[8,4,1024]{2,1,0:T(4,128)(2,1)S(1)}, bf16[8,4,1024]{2,1,0:T(4,128)(2,1)}, u32[]{:S(2)}) copy-start(bf16[8,4,1024]{2,1,0:T(4,128)(2,1)} %param.9) | copy-start | bytes 196612
  0.0 11.2 %copy-start.2 = (s32[8,32]{1,0:T(8,128)S(1)}, s32[8,32]{1,0:T(8,128)}, u32[]{:S(2)}) copy-start(s32[8,32]{1,0:T(8,128)} %page.1) | copy-start | bytes 3076
  0.0 11.2 %copy-start.4 = (s32[8]{0:T(128)S(1)}, s32[8]{0:T(128)}, u32[]{:S(2)}) copy-start(s32[8]{0:T(128)} %lens.1) | copy-start | bytes 100
  1.4 13.5 %collective-permute-start = (bf16[512,512]{1,0:T(8,128)(2,1)S(1)}, bf16[512,512]{1,0:T(8,128)(2,1)S(1)}, u32[]{:S(2)}, u32[]{:S(2)}) collective-permute-start(bf16[512,512]{1,0:T(8,128)(2,1)S(1)} %get-tuple-element.41), channel_id=1, source_target_pairs={{0,8},{8,0},{16,24},{24,16},{32,40},{40,32},{48,56},{56,48},{64,72... | collective-permute-start | bytes 1572872 | tf_op jit(solution)/shard_map/ppermute | solution.py:440
  4.9 8.6 %collective-permute-start.1 = (bf16[512,256]{1,0:T(8,128)(2,1)}, bf16[512,256]{1,0:T(8,128)(2,1)S(1)}, u32[]{:S(2)}, u32[]{:S(2)}) collective-permute-start(bf16[512,256]{1,0:T(8,128)(2,1)} %get-tuple-element.39), channel_id=1, source_target_pairs={{0,16},{8,24},{16,32},{24,40},{32,48},{40,56},{48,0},{56,8},{64,80... | collective-permute-start | bytes 786440 | tf_op jit(solution)/shard_map/ppermute | solution.py:440
  6.1 7.4 %collective-permute-start.2 = (bf16[512,256]{1,0:T(8,128)(2,1)}, bf16[512,256]{1,0:T(8,128)(2,1)S(1)}, u32[]{:S(2)}, u32[]{:S(2)}) collective-permute-start(bf16[512,256]{1,0:T(8,128)(2,1)} %get-tuple-element.38), channel_id=1, source_target_pairs={{0,48},{8,56},{16,0},{24,8},{32,16},{40,24},{48,32},{56,40},{64,11... | collective-permute-start | bytes 786440 | tf_op jit(solution)/shard_map/ppermute | solution.py:440
  7.5 7.4 %collective-permute-start.3 = (bf16[512,256]{1,0:T(8,128)(2,1)S(1)}, bf16[512,256]{1,0:T(8,128)(2,1)S(1)}, u32[]{:S(2)}, u32[]{:S(2)}) collective-permute-start(bf16[512,256]{1,0:T(8,128)(2,1)S(1)} %get-tuple-element.40), channel_id=1, source_target_pairs={{0,64},{8,72},{16,80},{24,88},{32,96},{40,104},{48,112},{56,120},{... | collective-permute-start | bytes 786440 | tf_op jit(solution)/shard_map/ppermute | solution.py:440
  8.8 6.1 %collective-permute-start.4 = (bf16[512,256]{1,0:T(8,128)(2,1)S(1)}, bf16[512,256]{1,0:T(8,128)(2,1)S(1)}, u32[]{:S(2)}, u32[]{:S(2)}) collective-permute-start(bf16[512,256]{1,0:T(8,128)(2,1)S(1)} %get-tuple-element.37), channel_id=1, source_target_pairs={{0,192},{8,200},{16,208},{24,216},{32,224},{40,232},{48,240},{56,2... | collective-permute-start | bytes 786440 | tf_op jit(solution)/shard_map/ppermute | solution.py:440
  15.0 10.4 %copy-start.7 = (bf16[8,4,256]{2,1,0:T(4,128)(2,1)S(1)}, bf16[8,4,256]{2,1,0:T(4,128)(2,1)}, u32[]{:S(2)}) copy-start(bf16[8,4,256]{2,1,0:T(4,128)(2,1)} %param.10) | copy-start | bytes 49156
  16.7 25.9 %all-to-all-start = ((bf16[32,144,128]{2,1,0:T(8,128)(2,1)}), bf16[32,144,128]{2,1,0:T(8,128)(2,1)S(1)}, u32[]{:S(2)}, u32[]{:S(2)}) async-start(bf16[32,144,128]{2,1,0:T(8,128)(2,1)} %pack.1), calls=%async_computation | async-start | bytes 2359296 | tf_op jit(solution)/shard_map/all_to_all | solution.py:469
  25.4 2.5 %copy-start = (bf16[80,128,256]{2,1,0:T(8,128)(2,1)S(1)}, bf16[80,128,256]{2,1,0:T(8,128)(2,1)}, u32[]{:S(2)}) copy-start(bf16[80,128,256]{2,1,0:T(8,128)(2,1)} %pool.3) | copy-start | bytes 15728644
  29.8 29.6 %copy-start.8 = (s32[1,32,2]{1,2,0:T(2,128)S(1)}, s32[1,32,2]{1,2,0:T(2,128)}, u32[]{:S(2)}) copy-start(s32[1,32,2]{1,2,0:T(2,128)} %param.14) | copy-start | bytes 772
  43.2 3.9 %collective-permute-start.5 = (bf16[4,32,128]{2,1,0:T(8,128)(2,1)S(1)}, bf16[4,32,128]{2,1,0:T(8,128)(2,1)S(1)}, u32[]{:S(2)}, u32[]{:S(2)}) collective-permute-start(bf16[4,32,128]{2,1,0:T(8,128)(2,1)S(1)} %get-tuple-element.44), channel_id=1, source_target_pairs={{0,1},{1,0},{2,3},{3,2},{4,5},{5,4},{6,7},{7,6},{8,9},{9,8},{10,11... | collective-permute-start | bytes 98312 | tf_op jit(solution)/shard_map/ppermute | solution.py:482
  48.0 22.0 %all-to-all-start.1 = ((bf16[32,2,32,128]{3,2,1,0:T(8,128)(2,1)}), bf16[32,2,32,128]{3,2,1,0:T(8,128)(2,1)S(1)}, u32[]{:S(2)}, u32[]{:S(2)}) async-start(bf16[32,2,32,128]{3,2,1,0:T(8,128)(2,1)} %bitcast.12), calls=%async_computation.1 | async-start | bytes 1048576 | tf_op jit(solution)/shard_map/all_to_all | solution.py:498
  56.0 11.8 %collective-permute-start.6 = (bf16[256,128]{1,0:T(8,128)(2,1)S(1)}, bf16[256,128]{1,0:T(8,128)(2,1)S(1)}, u32[]{:S(2)}, u32[]{:S(2)}) collective-permute-start(bf16[256,128]{1,0:T(8,128)(2,1)S(1)} %reshape_reshape.3.q0), channel_id=1, source_target_pairs={{0,16},{8,24},{16,32},{24,40},{32,48},{40,56},{48,0},{56,8},{64,80... | collective-permute-start | bytes 196616 | tf_op jit(solution)/shard_map/ppermute | solution.py:440
  56.4 11.4 %collective-permute-start.7 = (bf16[256,128]{1,0:T(8,128)(2,1)S(1)}, bf16[256,128]{1,0:T(8,128)(2,1)S(1)}, u32[]{:S(2)}, u32[]{:S(2)}) collective-permute-start(bf16[256,128]{1,0:T(8,128)(2,1)S(1)} %reshape_reshape.3.q0), channel_id=1, source_target_pairs={{0,32},{8,40},{16,48},{24,56},{32,0},{40,8},{48,16},{56,24},{64,96... | collective-permute-start | bytes 196616 | tf_op jit(solution)/shard_map/ppermute | solution.py:440
  58.1 9.7 %collective-permute-start.8 = (bf16[256,128]{1,0:T(8,128)(2,1)S(1)}, bf16[256,128]{1,0:T(8,128)(2,1)S(1)}, u32[]{:S(2)}, u32[]{:S(2)}) collective-permute-start(bf16[256,128]{1,0:T(8,128)(2,1)S(1)} %reshape_reshape.3.q0), channel_id=1, source_target_pairs={{0,48},{8,56},{16,0},{24,8},{32,16},{40,24},{48,32},{56,40},{64,11... | collective-permute-start | bytes 196616 | tf_op jit(solution)/shard_map/ppermute | solution.py:440
  59.6 2.5 %copy-start.1 = (bf16[80,128,256]{2,1,0:T(8,128)(2,1)S(1)}, bf16[80,128,256]{2,1,0:T(8,128)(2,1)}, u32[]{:S(2)}) copy-start(bf16[80,128,256]{2,1,0:T(8,128)(2,1)} %pool.3) | copy-start | bytes 15728644
  70.0 29.9 %copy-start.3 = (s32[8]{0:T(128)S(1)}, s32[8]{0:T(128)}, u32[]{:S(2)}) copy-start(s32[8]{0:T(128)} %flags.1) | copy-start | bytes 100
  70.0 25.3 %all-to-all-start.2 = ((f32[32,72,128]{2,1,0:T(8,128)}), f32[32,72,128]{2,1,0:T(8,128)S(1)}, u32[]{:S(2)}, u32[]{:S(2)}) async-start(f32[32,72,128]{2,1,0:T(8,128)} %remote_partials.1), calls=%async_computation.2 | async-start | bytes 2359296 | tf_op jit(solution)/shard_map/all_to_all | solution.py:507
  81.8 15.4 %collective-permute-start.9 = (f32[272,128]{1,0:T(8,128)S(1)}, f32[272,128]{1,0:T(8,128)S(1)}, u32[]{:S(2)}, u32[]{:S(2)}) collective-permute-start(f32[272,128]{1,0:T(8,128)S(1)} %get-tuple-element.34), channel_id=1, source_target_pairs={{0,48},{8,56},{16,0},{24,8},{32,16},{40,24},{48,32},{56,40},{64,11... | collective-permute-start | bytes 417800 | tf_op jit(solution)/shard_map/ppermute | solution.py:440
  84.3 12.9 %collective-permute-start.10 = (f32[272,128]{1,0:T(8,128)S(1)}, f32[272,128]{1,0:T(8,128)S(1)}, u32[]{:S(2)}, u32[]{:S(2)}) collective-permute-start(f32[272,128]{1,0:T(8,128)S(1)} %get-tuple-element.35), channel_id=1, source_target_pairs={{0,32},{8,40},{16,48},{24,56},{32,0},{40,8},{48,16},{56,24},{64,96... | collective-permute-start | bytes 417800 | tf_op jit(solution)/shard_map/ppermute | solution.py:440
  84.9 15.0 %collective-permute-start.11 = (f32[272,128]{1,0:T(8,128)S(1)}, f32[272,128]{1,0:T(8,128)S(1)}, u32[]{:S(2)}, u32[]{:S(2)}) collective-permute-start(f32[272,128]{1,0:T(8,128)S(1)} %get-tuple-element.36), channel_id=1, source_target_pairs={{0,16},{8,24},{16,32},{24,40},{32,48},{40,56},{48,0},{56,8},{64,80... | collective-permute-start | bytes 417800 | tf_op jit(solution)/shard_map/ppermute | solution.py:440

commit v4 on v3

--- a/solution.py
+++ b/solution.py
@@ -148,21 +148,22 @@
     )(slot_req, counts, hold, q, *columns)
 
 
-def gather_kernel(spans, holders, asked, out):
+def gather_kernel(units, holders, asked, out):
+    tokens = out.shape[1] // 2
+    head = asked.shape[1] - units[0] * tokens
     first = 0
-    head = asked.shape[1] - spans[0]
-    flat = out.shape[1]
-    for k, span in enumerate(spans):
-        for h in range(span // flat):
-            at = head + h * flat
-            out[first] = asked[holders[k], at : at + flat, :]
+    for k, count in enumerate(units):
+        for j in range(count):
+            half = (first % 2) * tokens
+            at = head + j * tokens
+            out[first // 2, half : half + tokens, :] = asked[holders[k], at : at + tokens, :]
             first += 1
 
 
-def gather(spans, holders, asked, shares):
-    return pl.pallas_call(
-        functools.partial(gather_kernel, spans),
-        out_shape=jax.ShapeDtypeStruct((shares, sum(spans) // shares, HD), BF16),
+def gather(units, holders, asked, tokens):
+    return pl.pallas_call(
+        functools.partial(gather_kernel, units),
+        out_shape=jax.ShapeDtypeStruct((sum(units) // 2, 2 * tokens, HD), BF16),
         in_specs=[SMEM, VMEM],
         out_specs=VMEM,
         compiler_params=params(),
@@ -440,20 +441,19 @@
         return lax.ppermute(value, "inst", pairs)
 
     steps_out = (
-        (2, 0, 0, 0),
-        (2, 0, 0, 1),
-        (1, 0, 1, 0),
-        (1, 0, -1, 0),
-        (1, 1, 0, 0),
-        (1, -1, 0, 0),
+        (3, 0, 0, 0),
+        (3, 0, 0, 1),
+        (3, 0, 1, 0),
+        (3, 0, -1, 0),
+        (2, 1, 0, 0),
+        (2, -1, 0, 0),
     )
-    head_width = prefix_store.shape[1] // shares
     columns = []
     holders = []
     first = 0
-    for heads, dy, dx, dz in steps_out:
-        part = prefix_store[:, first * head_width : (first + heads) * head_width]
-        first += heads
+    for units, dy, dx, dz in steps_out:
+        part = prefix_store[:, first * HD : (first + units) * HD]
+        first += units
         columns.append(move(part, dy, dx, dz) if holders else part)
         holders.append(index(owned // (XS * ZS) + dy, owned // ZS + dx, owned + dz))
     hold = sum(jnp.where(me == holders[k], k, 0) for k in range(1, len(steps_out)))
@@ -464,12 +464,13 @@
     q = queries.reshape(req, rows, HD)
     local, slot_req, counts = prep(page, lengths, pool_size, n * CAP)
     tokens = prefix_store.shape[0] // n
-    spans = tuple(heads * 2 * tokens for heads, _, _, _ in steps_out)
+    tokens = prefix_store.shape[0] // n
+    units = tuple(step[0] for step in steps_out)
     pay = pack(spots, slot_req, counts, hold.reshape(1), q, columns)
     asked = lax.all_to_all(pay, "inst", split_axis=0, concat_axis=0, tiled=True)
     fresh = jnp.pad(new_kv, ((0, 0), (0, 16 - steps), (0, 0)))
     here = local_partials(local, pool, q, fresh)
-    piece = gather(spans, jnp.stack(holders).astype(jnp.int32), asked, shares)
+    piece = gather(units, jnp.stack(holders).astype(jnp.int32), asked, tokens)
     piece = after(piece, *here)
 
     tp = lax.axis_index("tp").astype(jnp.int32)

time: 102 us -> 100 us (0.980)
  starting transfers between devices: 42.6 us -> 40.4 us
  local copies, waits for them, and re-layouts: 9.2 us -> 11 us
  waiting for transfers between devices: 29.7 us -> 28 us
    all_to_all x1, starting transfers between devices: 8.58 us -> 5.25 us  [per_device(): asked = lax.all_to_all(pay, 'inst', split_axis=0, concat_axis=0, tiled=True)]
    all_to_all x1, waiting for transfers between devices: 12.7 us -> 10.5 us  [per_device(): asked = lax.all_to_all(pay, 'inst', split_axis=0, concat_axis=0, tiled=True)]
    slice x2, local copies, waits for them, and re-layouts: 2.28 us -> 4.1 us  [per_device(): part = prefix_store[:, first * HD:(first + units) * HD]]
    unnamed x19 -> x17, local copies, waits for them, and re-layouts: 5.08 us -> 5.08 us
  transfers between devices with their start and end apart: 15 -> 15, of which waited for: 6 -> 6; matrix products, arithmetic and copies ran while one was open for 1% -> 2% of each run, Pallas kernels for 15% -> 16%
where the time goes in v4:
time: 100 us; the launch traced here: 99.5 us
  starting transfers between devices  40.4 us (40%)
  waiting for transfers between devices  28 us (28%)
  Pallas kernels  18.9 us (19%)
  local copies, waits for them, and re-layouts  11 us (11%)
  between operations  1.1 us (1%)
    ppermute x11, starting transfers between devices, move(): return lax.ppermute(value, 'inst', pairs)  14.9 us
    all_to_all x1, waiting for transfers between devices, per_device(): asked = lax.all_to_all(pay, 'inst', split_axis=0, concat_axis=0, tiled=True)  10.5 us
    all_to_all x1, waiting for transfers between devices, per_device(): lax.all_to_all(after(ret, prefix, *guests), 'inst', split_axis=0, concat_...  9.84 us
    all_to_all x1, starting transfers between devices, per_device(): lax.all_to_all(spread.reshape((-1,) + both.shape[1:]), ('inst', 'tp'), sp...  8.35 us
    all_to_all x1, starting transfers between devices, per_device(): lax.all_to_all(after(ret, prefix, *guests), 'inst', split_axis=0, concat_...  7.99 us
    pallas_call x1, Pallas kernels, remote_partials(): pl.pallas_call(remote_kernel, out_shape=jax.ShapeDtypeStruct((n, CAP * ro...  5.7 us
    all_to_all x1, starting transfers between devices, per_device(): asked = lax.all_to_all(pay, 'inst', split_axis=0, concat_axis=0, tiled=True)  5.25 us
    unnamed x17, local copies, waits for them, and re-layouts  5.08 us
  transfers between devices with their start and end apart: 15, of which 6 were waited for; matrix products, arithmetic and copies ran while one was open for 2% of the time, Pallas kernels for 16%

profile of v4, /device:TPU:1, one launch (start us, length us, event | category | flops | bytes accessed | tf_op | source)
XLA Modules:
  0.0 99.5 jit_solution(15100996314375628386)
XLA Ops:
  0.0 2.3 %fusion.1 = (bf16[512,384]{1,0:T(8,128)(2,1)S(1)}, bf16[512,384]{1,0:T(8,128)(2,1)S(1)}, bf16[512,384]{1,0:T(8,128)(2,1)}, bf16[512,384]{1,0:T(8,128)(2,1)S(1)}) fusion(bf16[512,2048]{1,0:T(8,128)(2,1)} %param.15), kind=kLoop, calls=%fused_computation.4 | loop fusion | bytes 3145728 | tf_op jit(solution)/shard_map/slice | solution.py:455
  2.3 2.5 %collective-permute-start = (bf16[512,384]{1,0:T(8,128)(2,1)}, bf16[512,384]{1,0:T(8,128)(2,1)S(1)}, u32[]{:S(2)}, u32[]{:S(2)}) collective-permute-start(bf16[512,384]{1,0:T(8,128)(2,1)} %get-tuple-element.41), channel_id=1, source_target_pairs={{0,8},{8,0},{16,24},{24,16},{32,40},{40,32},{48,56},{56,48},{64,72... | collective-permute-start | bytes 1179656 | tf_op jit(solution)/shard_map/ppermute | solution.py:441
  6.0 1.5 %collective-permute-start.2 = (bf16[512,384]{1,0:T(8,128)(2,1)S(1)}, bf16[512,384]{1,0:T(8,128)(2,1)S(1)}, u32[]{:S(2)}, u32[]{:S(2)}) collective-permute-start(bf16[512,384]{1,0:T(8,128)(2,1)S(1)} %get-tuple-element.39), channel_id=1, source_target_pairs={{0,48},{8,56},{16,0},{24,8},{32,16},{40,24},{48,32},{56,40},{64,11... | collective-permute-start | bytes 1179656 | tf_op jit(solution)/shard_map/ppermute | solution.py:441
  7.5 1.8 %fusion = (bf16[512,256]{1,0:T(8,128)(2,1)S(1)}, bf16[512,256]{1,0:T(8,128)(2,1)}) fusion(bf16[512,2048]{1,0:T(8,128)(2,1)} %param.15), kind=kLoop, calls=%fused_computation.3 | loop fusion | bytes 1048576 | tf_op jit(solution)/shard_map/slice | solution.py:455
  10.6 1.4 %collective-permute-start.4 = (bf16[512,256]{1,0:T(8,128)(2,1)S(1)}, bf16[512,256]{1,0:T(8,128)(2,1)S(1)}, u32[]{:S(2)}, u32[]{:S(2)}) collective-permute-start(bf16[512,256]{1,0:T(8,128)(2,1)S(1)} %get-tuple-element.37), channel_id=1, source_target_pairs={{0,192},{8,200},{16,208},{24,216},{32,224},{40,232},{48,240},{56,2... | collective-permute-start | bytes 786440 | tf_op jit(solution)/shard_map/ppermute | solution.py:441
  12.9 2.2 %prep.1 = (s32[3,16]{1,0:T(4,128)S(1)}, s32[64]{0:T(128)S(1)}, s32[64]{0:T(128)S(1)}) custom-call(s32[8,32]{1,0:T(8,128)S(1)} %copy-done.2, s32[8]{0:T(128)S(1)} %copy-done.4), custom_call_target="tpu_custom_call" | custom-call | bytes 9000000 | tf_op jit(solution)/shard_map/prep/pallas_call | solution.py:95
  15.1 2.0 %collective-permute-done.3.refs_4_ = bf16[512,256]{1,0:T(8,128)(2,1)S(1)} collective-permute-done((bf16[512,256]{1,0:T(8,128)(2,1)}, bf16[512,256]{1,0:T(8,128)(2,1)S(1)}, u32[]{:S(2)}, u32[]{:S(2)}) %collective-permute-start.3) | collective-permute-done | bytes 262176 | tf_op jit(solution)/shard_map/ppermute | solution.py:441
  17.1 1.7 %pack.1 = bf16[32,128,128]{2,1,0:T(8,128)(2,1)} custom-call(s32[64]{0:T(128)S(1)} %get-tuple-element.21.slot_req, s32[64]{0:T(128)S(1)} %get-tuple-element.22.counts, s32[1]{0:T(128)} %bitcast.2.hold, bf16[8,32,128]{2,1,0:T(8,128)(2,1)S(1)} %reshape.28.q, bf16[512,384]{1,0:T(8,128)(2,1)S(1)} %get-tuple-element.42.refs_0_, ...), custom_call_target="tpu_custom_call" | custom-call | bytes 4500000 | tf_op jit(solution)/shard_map/pack/pallas_call | solution.py:140
  18.8 5.2 %all-to-all-start = ((bf16[32,128,128]{2,1,0:T(8,128)(2,1)}), bf16[32,128,128]{2,1,0:T(8,128)(2,1)S(1)}, u32[]{:S(2)}, u32[]{:S(2)}) async-start(bf16[32,128,128]{2,1,0:T(8,128)(2,1)} %pack.1), calls=%async_computation | async-start | bytes 2097152 | tf_op jit(solution)/shard_map/all_to_all | solution.py:470
  24.1 2.5 %copy-done = bf16[80,128,256]{2,1,0:T(8,128)(2,1)S(1)} copy-done((bf16[80,128,256]{2,1,0:T(8,128)(2,1)S(1)}, bf16[80,128,256]{2,1,0:T(8,128)(2,1)}, u32[]{:S(2)}) %copy-start) | copy-done | bytes 5242904
  26.6 1.9 %local_partials.1 = (f32[8,32,128]{2,1,0:T(8,128)S(1)}, f32[8,32,128]{2,1,0:T(8,128)S(1)}, f32[8,32,128]{2,1,0:T(8,128)S(1)}) custom-call(s32[3,16]{1,0:T(4,128)S(1)} %get-tuple-element.23.local, bf16[80,128,256]{2,1,0:T(8,128)(2,1)S(1)} %copy-done, bf16[8,32,128]{2,1,0:T(8,128)(2,1)S(1)} %reshape.28.q, bf16[8,16,256]{2,1,0:T(8,128)(2,1)S(1)} %pad.4.fresh), custom_call_target="tpu_custom_call" | custom-call | bytes 18000000 | tf_op jit(solution)/shard_map/local_partials/pallas_call | solution.py:258
  28.6 10.5 %all-to-all-done.pay.asked = bf16[32,128,128]{2,1,0:T(8,128)(2,1)S(1)} async-done(((bf16[32,128,128]{2,1,0:T(8,128)(2,1)}), bf16[32,128,128]{2,1,0:T(8,128)(2,1)S(1)}, u32[]{:S(2)}, u32[]{:S(2)}) %all-to-all-start) | async-done | bytes 1048608 | tf_op jit(solution)/shard_map/all_to_all | solution.py:470
  39.7 3.9 %collective-permute-start.5 = (bf16[4,32,128]{2,1,0:T(8,128)(2,1)S(1)}, bf16[4,32,128]{2,1,0:T(8,128)(2,1)S(1)}, u32[]{:S(2)}, u32[]{:S(2)}) collective-permute-start(bf16[4,32,128]{2,1,0:T(8,128)(2,1)S(1)} %get-tuple-element.44), channel_id=1, source_target_pairs={{0,1},{1,0},{2,3},{3,2},{4,5},{5,4},{6,7},{7,6},{8,9},{9,8},{10,11... | collective-permute-start | bytes 98312 | tf_op jit(solution)/shard_map/ppermute | solution.py:483
  45.4 8.3 %all-to-all-start.1 = ((bf16[32,2,32,128]{3,2,1,0:T(8,128)(2,1)}), bf16[32,2,32,128]{3,2,1,0:T(8,128)(2,1)S(1)}, u32[]{:S(2)}, u32[]{:S(2)}) async-start(bf16[32,2,32,128]{3,2,1,0:T(8,128)(2,1)} %bitcast.12), calls=%async_computation.1 | async-start | bytes 1048576 | tf_op jit(solution)/shard_map/all_to_all | solution.py:499
  54.2 1.7 %collective-permute-start.7 = (bf16[256,128]{1,0:T(8,128)(2,1)S(1)}, bf16[256,128]{1,0:T(8,128)(2,1)S(1)}, u32[]{:S(2)}, u32[]{:S(2)}) collective-permute-start(bf16[256,128]{1,0:T(8,128)(2,1)S(1)} %reshape_reshape.3.q0), channel_id=1, source_target_pairs={{0,32},{8,40},{16,48},{24,56},{32,0},{40,8},{48,16},{56,24},{64,96... | collective-permute-start | bytes 196616 | tf_op jit(solution)/shard_map/ppermute | solution.py:441
  57.4 2.5 %copy-done.1 = bf16[80,128,256]{2,1,0:T(8,128)(2,1)S(1)} copy-done((bf16[80,128,256]{2,1,0:T(8,128)(2,1)S(1)}, bf16[80,128,256]{2,1,0:T(8,128)(2,1)}, u32[]{:S(2)}) %copy-start.1) | copy-done | bytes 5242904
  59.9 5.7 %remote_partials.1 = f32[32,72,128]{2,1,0:T(8,128)} custom-call(s32[64]{0:T(128)S(1)} %reshape.26.outbox, bf16[80,128,256]{2,1,0:T(8,128)(2,1)S(1)} %copy-done.1, bf16[32,128,128]{2,1,0:T(8,128)(2,1)S(1)} %all-to-all-done.pay.asked), custom_call_target="tpu_custom_call" | custom-call | bytes 18000000 | tf_op jit(solution)/shard_map/remote_partials/pallas_call | solution.py:210
  65.6 2.3 %all-to-all-done.1 = bf16[32,2,32,128]{3,2,1,0:T(8,128)(2,1)S(1)} async-done(((bf16[32,2,32,128]{3,2,1,0:T(8,128)(2,1)}), bf16[32,2,32,128]{3,2,1,0:T(8,128)(2,1)S(1)}, u32[]{:S(2)}, u32[]{:S(2)}) %all-to-all-start.1) | async-done | bytes 524320 | tf_op jit(solution)/shard_map/all_to_all | solution.py:499
  67.9 8.0 %all-to-all-start.2 = ((f32[32,72,128]{2,1,0:T(8,128)}), f32[32,72,128]{2,1,0:T(8,128)S(1)}, u32[]{:S(2)}, u32[]{:S(2)}) async-start(f32[32,72,128]{2,1,0:T(8,128)} %remote_partials.1), calls=%async_computation.2 | async-start | bytes 2359296 | tf_op jit(solution)/shard_map/all_to_all | solution.py:508
  75.9 3.8 %prefix_partials.1 = (f32[272,128]{1,0:T(8,128)S(1)}, f32[272,128]{1,0:T(8,128)S(1)}, f32[272,128]{1,0:T(8,128)S(1)}, f32[272,128]{1,0:T(8,128)S(1)}) custom-call(bf16[256,128]{1,0:T(8,128)(2,1)S(1)} %reshape_reshape.3.q0, bf16[256,128]{1,0:T(8,128)(2,1)S(1)} %collective-permute-done.6.q1, bf16[256,128]{1,0:T(8,128)(2,1)S(1)} %collective-permute-done.7.q2, ...), custom_call_target="tpu_custom_call" | custom-call | bytes 18000000 | tf_op jit(solution)/shard_map/prefix_partials/pallas_call | solution.py:313
  79.6 2.5 %collective-permute-start.9 = (f32[272,128]{1,0:T(8,128)S(1)}, f32[272,128]{1,0:T(8,128)S(1)}, u32[]{:S(2)}, u32[]{:S(2)}) collective-permute-start(f32[272,128]{1,0:T(8,128)S(1)} %get-tuple-element.34), channel_id=1, source_target_pairs={{0,48},{8,56},{16,0},{24,8},{32,16},{40,24},{48,32},{56,40},{64,11... | collective-permute-start | bytes 417800 | tf_op jit(solution)/shard_map/ppermute | solution.py:441
  83.3 9.8 %all-to-all-done.2.ret = f32[32,72,128]{2,1,0:T(8,128)S(1)} async-done(((f32[32,72,128]{2,1,0:T(8,128)}), f32[32,72,128]{2,1,0:T(8,128)S(1)}, u32[]{:S(2)}, u32[]{:S(2)}) %all-to-all-start.2) | async-done | bytes 1179680 | tf_op jit(solution)/shard_map/all_to_all | solution.py:508
  93.1 1.9 %merge.1 = (f32[8,32,128]{2,1,0:T(8,128)S(1)}, f32[8,32,128]{2,1,0:T(8,128)S(1)}, f32[8,32,128]{2,1,0:T(8,128)S(1)}) custom-call(s32[1]{0:T(128)} %bitcast.me, s32[64]{0:T(128)S(1)} %get-tuple-element.21.slot_req, f32[32,72,128]{2,1,0:T(8,128)S(1)} %all-to-all-done.2.ret, f32[8,32,128]{2,1,0:T(8,128)S(1)} %get-tuple-element.24.lo, ...), custom_call_target="tpu_custom_call" | custom-call | bytes 6000000 | tf_op jit(solution)/shard_map/merge/pallas_call | solution.py:362
  95.1 2.6 %collective-permute-done.11.p3 = f32[272,128]{1,0:T(8,128)S(1)} collective-permute-done((f32[272,128]{1,0:T(8,128)S(1)}, f32[272,128]{1,0:T(8,128)S(1)}, u32[]{:S(2)}, u32[]{:S(2)}) %collective-permute-start.11) | collective-permute-done | bytes 139296 | tf_op jit(solution)/shard_map/ppermute | solution.py:441
  (42 shorter events, 9.8 us)
Async XLA Ops:
  0.0 12.8 %copy-start.5 = (bf16[8,4,1024]{2,1,0:T(4,128)(2,1)S(1)}, bf16[8,4,1024]{2,1,0:T(4,128)(2,1)}, u32[]{:S(2)}) copy-start(bf16[8,4,1024]{2,1,0:T(4,128)(2,1)} %param.9) | copy-start | bytes 196612
  0.0 12.9 %copy-start.2 = (s32[8,32]{1,0:T(8,128)S(1)}, s32[8,32]{1,0:T(8,128)}, u32[]{:S(2)}) copy-start(s32[8,32]{1,0:T(8,128)} %page.1) | copy-start | bytes 3076
  0.0 12.9 %copy-start.4 = (s32[8]{0:T(128)S(1)}, s32[8]{0:T(128)}, u32[]{:S(2)}) copy-start(s32[8]{0:T(128)} %lens.1) | copy-start | bytes 100
  2.3 14.7 %collective-permute-start = (bf16[512,384]{1,0:T(8,128)(2,1)}, bf16[512,384]{1,0:T(8,128)(2,1)S(1)}, u32[]{:S(2)}, u32[]{:S(2)}) collective-permute-start(bf16[512,384]{1,0:T(8,128)(2,1)} %get-tuple-element.41), channel_id=1, source_target_pairs={{0,8},{8,0},{16,24},{24,16},{32,40},{40,32},{48,56},{56,48},{64,72... | collective-permute-start | bytes 1179656 | tf_op jit(solution)/shard_map/ppermute | solution.py:441
  4.8 12.3 %collective-permute-start.1 = (bf16[512,384]{1,0:T(8,128)(2,1)S(1)}, bf16[512,384]{1,0:T(8,128)(2,1)S(1)}, u32[]{:S(2)}, u32[]{:S(2)}) collective-permute-start(bf16[512,384]{1,0:T(8,128)(2,1)S(1)} %get-tuple-element.40), channel_id=1, source_target_pairs={{0,16},{8,24},{16,32},{24,40},{32,48},{40,56},{48,0},{56,8},{64,80... | collective-permute-start | bytes 1179656 | tf_op jit(solution)/shard_map/ppermute | solution.py:441
  6.0 11.1 %collective-permute-start.2 = (bf16[512,384]{1,0:T(8,128)(2,1)S(1)}, bf16[512,384]{1,0:T(8,128)(2,1)S(1)}, u32[]{:S(2)}, u32[]{:S(2)}) collective-permute-start(bf16[512,384]{1,0:T(8,128)(2,1)S(1)} %get-tuple-element.39), channel_id=1, source_target_pairs={{0,48},{8,56},{16,0},{24,8},{32,16},{40,24},{48,32},{56,40},{64,11... | collective-permute-start | bytes 1179656 | tf_op jit(solution)/shard_map/ppermute | solution.py:441
  9.3 7.8 %collective-permute-start.3 = (bf16[512,256]{1,0:T(8,128)(2,1)}, bf16[512,256]{1,0:T(8,128)(2,1)S(1)}, u32[]{:S(2)}, u32[]{:S(2)}) collective-permute-start(bf16[512,256]{1,0:T(8,128)(2,1)} %get-tuple-element.38), channel_id=1, source_target_pairs={{0,64},{8,72},{16,80},{24,88},{32,96},{40,104},{48,112},{56,120},{... | collective-permute-start | bytes 786440 | tf_op jit(solution)/shard_map/ppermute | solution.py:441
  10.6 6.5 %collective-permute-start.4 = (bf16[512,256]{1,0:T(8,128)(2,1)S(1)}, bf16[512,256]{1,0:T(8,128)(2,1)S(1)}, u32[]{:S(2)}, u32[]{:S(2)}) collective-permute-start(bf16[512,256]{1,0:T(8,128)(2,1)S(1)} %get-tuple-element.37), channel_id=1, source_target_pairs={{0,192},{8,200},{16,208},{24,216},{32,224},{40,232},{48,240},{56,2... | collective-permute-start | bytes 786440 | tf_op jit(solution)/shard_map/ppermute | solution.py:441
  17.1 7.0 %copy-start.6 = (bf16[8,4,256]{2,1,0:T(4,128)(2,1)S(1)}, bf16[8,4,256]{2,1,0:T(4,128)(2,1)}, u32[]{:S(2)}) copy-start(bf16[8,4,256]{2,1,0:T(4,128)(2,1)} %param.10) | copy-start | bytes 49156
  18.8 20.3 %all-to-all-start = ((bf16[32,128,128]{2,1,0:T(8,128)(2,1)}), bf16[32,128,128]{2,1,0:T(8,128)(2,1)S(1)}, u32[]{:S(2)}, u32[]{:S(2)}) async-start(bf16[32,128,128]{2,1,0:T(8,128)(2,1)} %pack.1), calls=%async_computation | async-start | bytes 2097152 | tf_op jit(solution)/shard_map/all_to_all | solution.py:470
  24.1 2.5 %copy-start = (bf16[80,128,256]{2,1,0:T(8,128)(2,1)S(1)}, bf16[80,128,256]{2,1,0:T(8,128)(2,1)}, u32[]{:S(2)}) copy-start(bf16[80,128,256]{2,1,0:T(8,128)(2,1)} %pool.3) | copy-start | bytes 15728644
  28.5 28.6 %copy-start.7 = (s32[1,32,2]{1,2,0:T(2,128)S(1)}, s32[1,32,2]{1,2,0:T(2,128)}, u32[]{:S(2)}) copy-start(s32[1,32,2]{1,2,0:T(2,128)} %param.14) | copy-start | bytes 772
  39.7 4.8 %collective-permute-start.5 = (bf16[4,32,128]{2,1,0:T(8,128)(2,1)S(1)}, bf16[4,32,128]{2,1,0:T(8,128)(2,1)S(1)}, u32[]{:S(2)}, u32[]{:S(2)}) collective-permute-start(bf16[4,32,128]{2,1,0:T(8,128)(2,1)S(1)} %get-tuple-element.44), channel_id=1, source_target_pairs={{0,1},{1,0},{2,3},{3,2},{4,5},{5,4},{6,7},{7,6},{8,9},{9,8},{10,11... | collective-permute-start | bytes 98312 | tf_op jit(solution)/shard_map/ppermute | solution.py:483
  45.4 22.5 %all-to-all-start.1 = ((bf16[32,2,32,128]{3,2,1,0:T(8,128)(2,1)}), bf16[32,2,32,128]{3,2,1,0:T(8,128)(2,1)S(1)}, u32[]{:S(2)}, u32[]{:S(2)}) async-start(bf16[32,2,32,128]{3,2,1,0:T(8,128)(2,1)} %bitcast.12), calls=%async_computation.1 | async-start | bytes 1048576 | tf_op jit(solution)/shard_map/all_to_all | solution.py:499
  53.8 11.8 %collective-permute-start.6 = (bf16[256,128]{1,0:T(8,128)(2,1)S(1)}, bf16[256,128]{1,0:T(8,128)(2,1)S(1)}, u32[]{:S(2)}, u32[]{:S(2)}) collective-permute-start(bf16[256,128]{1,0:T(8,128)(2,1)S(1)} %reshape_reshape.3.q0), channel_id=1, source_target_pairs={{0,16},{8,24},{16,32},{24,40},{32,48},{40,56},{48,0},{56,8},{64,80... | collective-permute-start | bytes 196616 | tf_op jit(solution)/shard_map/ppermute | solution.py:441
  54.2 11.4 %collective-permute-start.7 = (bf16[256,128]{1,0:T(8,128)(2,1)S(1)}, bf16[256,128]{1,0:T(8,128)(2,1)S(1)}, u32[]{:S(2)}, u32[]{:S(2)}) collective-permute-start(bf16[256,128]{1,0:T(8,128)(2,1)S(1)} %reshape_reshape.3.q0), channel_id=1, source_target_pairs={{0,32},{8,40},{16,48},{24,56},{32,0},{40,8},{48,16},{56,24},{64,96... | collective-permute-start | bytes 196616 | tf_op jit(solution)/shard_map/ppermute | solution.py:441
  55.9 9.6 %collective-permute-start.8 = (bf16[256,128]{1,0:T(8,128)(2,1)S(1)}, bf16[256,128]{1,0:T(8,128)(2,1)S(1)}, u32[]{:S(2)}, u32[]{:S(2)}) collective-permute-start(bf16[256,128]{1,0:T(8,128)(2,1)S(1)} %reshape_reshape.3.q0), channel_id=1, source_target_pairs={{0,48},{8,56},{16,0},{24,8},{32,16},{40,24},{48,32},{56,40},{64,11... | collective-permute-start | bytes 196616 | tf_op jit(solution)/shard_map/ppermute | solution.py:441
  57.4 2.5 %copy-start.1 = (bf16[80,128,256]{2,1,0:T(8,128)(2,1)S(1)}, bf16[80,128,256]{2,1,0:T(8,128)(2,1)}, u32[]{:S(2)}) copy-start(bf16[80,128,256]{2,1,0:T(8,128)(2,1)} %pool.3) | copy-start | bytes 15728644
  67.8 29.8 %copy-start.3 = (s32[8]{0:T(128)S(1)}, s32[8]{0:T(128)}, u32[]{:S(2)}) copy-start(s32[8]{0:T(128)} %flags.1) | copy-start | bytes 100
  67.9 25.3 %all-to-all-start.2 = ((f32[32,72,128]{2,1,0:T(8,128)}), f32[32,72,128]{2,1,0:T(8,128)S(1)}, u32[]{:S(2)}, u32[]{:S(2)}) async-start(f32[32,72,128]{2,1,0:T(8,128)} %remote_partials.1), calls=%async_computation.2 | async-start | bytes 2359296 | tf_op jit(solution)/shard_map/all_to_all | solution.py:508
  79.6 15.4 %collective-permute-start.9 = (f32[272,128]{1,0:T(8,128)S(1)}, f32[272,128]{1,0:T(8,128)S(1)}, u32[]{:S(2)}, u32[]{:S(2)}) collective-permute-start(f32[272,128]{1,0:T(8,128)S(1)} %get-tuple-element.34), channel_id=1, source_target_pairs={{0,48},{8,56},{16,0},{24,8},{32,16},{40,24},{48,32},{56,40},{64,11... | collective-permute-start | bytes 417800 | tf_op jit(solution)/shard_map/ppermute | solution.py:441
  82.1 13.0 %collective-permute-start.10 = (f32[272,128]{1,0:T(8,128)S(1)}, f32[272,128]{1,0:T(8,128)S(1)}, u32[]{:S(2)}, u32[]{:S(2)}) collective-permute-start(f32[272,128]{1,0:T(8,128)S(1)} %get-tuple-element.35), channel_id=1, source_target_pairs={{0,32},{8,40},{16,48},{24,56},{32,0},{40,8},{48,16},{56,24},{64,96... | collective-permute-start | bytes 417800 | tf_op jit(solution)/shard_map/ppermute | solution.py:441
  82.7 15.0 %collective-permute-start.11 = (f32[272,128]{1,0:T(8,128)S(1)}, f32[272,128]{1,0:T(8,128)S(1)}, u32[]{:S(2)}, u32[]{:S(2)}) collective-permute-start(f32[272,128]{1,0:T(8,128)S(1)} %get-tuple-element.36), channel_id=1, source_target_pairs={{0,16},{8,24},{16,32},{24,40},{32,48},{40,56},{48,0},{56,8},{64,80... | collective-permute-start | bytes 417800 | tf_op jit(solution)/shard_map/ppermute | solution.py:441

commit v5 on v4

--- a/solution.py
+++ b/solution.py
@@ -148,28 +148,40 @@
     )(slot_req, counts, hold, q, *columns)
 
 
-def gather_kernel(units, holders, asked, out):
-    tokens = out.shape[1] // 2
+def chip_of(position, core, chips):
+    return (position + (chips // 2) * core) % chips
+
+
+def gather_kernel(units, core, holders, asked, mine, other):
+    chips, double, _ = mine.shape
+    tokens = double // 2
     head = asked.shape[1] - units[0] * tokens
-    first = 0
-    for k, count in enumerate(units):
-        for j in range(count):
-            half = (first % 2) * tokens
-            at = head + j * tokens
-            out[first // 2, half : half + tokens, :] = asked[holders[k], at : at + tokens, :]
-            first += 1
-
-
-def gather(units, holders, asked, tokens):
+    found = [(k, j) for k, count in enumerate(units) for j in range(count)]
+    for c in range(2):
+
+        @pl.when(core[0] == c)
+        def _():
+            for out, parity in ((mine, c), (other, 1 - c)):
+                for position in range(chips):
+                    for part in range(2):
+                        k, j = found[(chip_of(position, parity, chips) * 2 + parity) * 2 + part]
+                        at = head + j * tokens
+                        out[position, part * tokens : (part + 1) * tokens, :] = asked[
+                            holders[k], at : at + tokens, :
+                        ]
+
+
+def gather(units, core, holders, asked, tokens):
+    one = jax.ShapeDtypeStruct((sum(units) // 4, 2 * tokens, HD), BF16)
     return pl.pallas_call(
         functools.partial(gather_kernel, units),
-        out_shape=jax.ShapeDtypeStruct((sum(units) // 2, 2 * tokens, HD), BF16),
-        in_specs=[SMEM, VMEM],
-        out_specs=VMEM,
+        out_shape=(one, one),
+        in_specs=[SMEM, SMEM, VMEM],
+        out_specs=(VMEM, VMEM),
         compiler_params=params(),
         cost_estimate=cost(0.5),
         name="gather",
-    )(holders, asked)
+    )(core, holders, asked)
 
 
 def remote_kernel(outbox, pool, pay, ret):
@@ -470,23 +482,20 @@
     asked = lax.all_to_all(pay, "inst", split_axis=0, concat_axis=0, tiled=True)
     fresh = jnp.pad(new_kv, ((0, 0), (0, 16 - steps), (0, 0)))
     here = local_partials(local, pool, q, fresh)
-    piece = gather(units, jnp.stack(holders).astype(jnp.int32), asked, tokens)
-    piece = after(piece, *here)
-
-    tp = lax.axis_index("tp").astype(jnp.int32)
+
     cores = 2
     chips = shares // cores
-    core = tp % cores
-    piece = piece.reshape(chips, cores, -1, HD)
-    mine = lax.dynamic_index_in_dim(piece, core, 1, keepdims=False)
-    other = lax.dynamic_index_in_dim(piece, 1 - core, 1, keepdims=False)
-    other = lax.ppermute(other, "tp", [(t, t ^ 1) for t in range(shares)])
+    core = lax.axis_index("tp").astype(jnp.int32) % cores
+    mine, other = gather(
+        units, core.reshape(1), jnp.stack(holders).astype(jnp.int32), asked, tokens
+    )
+    other = lax.ppermute(after(other, *here), "tp", [(t, t ^ 1) for t in range(shares)])
     both = jnp.stack([mine, other], axis=1)
     sheets = [
         [
-            index(y, x, z) * shares + chip * cores + c
+            index(y + (ys // 2) * c, x, z) * shares + chip_of(p, c, chips) * cores + c
             for y in range(ys)
-            for chip in range(chips)
+            for p in range(chips)
             for z in range(ZS)
         ]
         for x in range(XS)

time: 100 us -> 98.7 us (0.987)
  waiting for transfers between devices: 28 us -> 25.8 us
    all_to_all x1, starting transfers between devices: 8.35 us -> 11.5 us  [per_device(): lax.all_to_all(spread.reshape((-1,) + both.shape[1:]), ('inst', 'tp'), sp...]
    all_to_all x1, waiting for transfers between devices: 2.27 us -> 0.01 us  [per_device(): lax.all_to_all(spread.reshape((-1,) + both.shape[1:]), ('inst', 'tp'), sp...]
    all_to_all x1, starting transfers between devices: 7.99 us -> 6.15 us  [per_device(): lax.all_to_all(after(ret, prefix, *guests), 'inst', split_axis=0, concat_...]
  transfers between devices with their start and end apart: 15 -> 15, of which waited for: 6 -> 5; matrix products, arithmetic and copies ran while one was open for 2% -> 2% of each run, Pallas kernels for 16% -> 16%
where the time goes in v5:
time: 98.7 us; the launch traced here: 98.2 us
  starting transfers between devices  41.2 us (42%)
  waiting for transfers between devices  25.8 us (26%)
  Pallas kernels  19 us (19%)
  local copies, waits for them, and re-layouts  11 us (11%)
  between operations  1.09 us (1%)
    ppermute x11, starting transfers between devices, move(): return lax.ppermute(value, 'inst', pairs)  14.4 us
    all_to_all x1, starting transfers between devices, per_device(): lax.all_to_all(spread.reshape((-1,) + both.shape[1:]), ('inst', 'tp'), sp...  11.5 us
    all_to_all x1, waiting for transfers between devices, per_device(): lax.all_to_all(after(ret, prefix, *guests), 'inst', split_axis=0, concat_...  10.8 us
    all_to_all x1, waiting for transfers between devices, per_device(): asked = lax.all_to_all(pay, 'inst', split_axis=0, concat_axis=0, tiled=True)  10.5 us
    all_to_all x1, starting transfers between devices, per_device(): lax.all_to_all(after(ret, prefix, *guests), 'inst', split_axis=0, concat_...  6.15 us
    pallas_call x1, Pallas kernels, remote_partials(): pl.pallas_call(remote_kernel, out_shape=jax.ShapeDtypeStruct((n, CAP * ro...  5.7 us
    all_to_all x1, starting transfers between devices, per_device(): asked = lax.all_to_all(pay, 'inst', split_axis=0, concat_axis=0, tiled=True)  5.25 us
    unnamed x17, local copies, waits for them, and re-layouts  5.08 us
  transfers between devices with their start and end apart: 15, of which 5 were waited for; matrix products, arithmetic and copies ran while one was open for 2% of the time, Pallas kernels for 16%

profile of v5, /device:TPU:1, one launch (start us, length us, event | category | flops | bytes accessed | tf_op | source)
XLA Modules:
  0.0 98.2 jit_solution(14028025423462827053)
XLA Ops:
  0.0 2.3 %fusion.1 = (bf16[512,384]{1,0:T(8,128)(2,1)S(1)}, bf16[512,384]{1,0:T(8,128)(2,1)S(1)}, bf16[512,384]{1,0:T(8,128)(2,1)}, bf16[512,384]{1,0:T(8,128)(2,1)S(1)}) fusion(bf16[512,2048]{1,0:T(8,128)(2,1)} %param.15), kind=kLoop, calls=%fused_computation.2 | loop fusion | bytes 3145728 | tf_op jit(solution)/shard_map/slice | solution.py:467
  2.3 2.5 %collective-permute-start = (bf16[512,384]{1,0:T(8,128)(2,1)}, bf16[512,384]{1,0:T(8,128)(2,1)S(1)}, u32[]{:S(2)}, u32[]{:S(2)}) collective-permute-start(bf16[512,384]{1,0:T(8,128)(2,1)} %get-tuple-element.45), channel_id=1, source_target_pairs={{0,8},{8,0},{16,24},{24,16},{32,40},{40,32},{48,56},{56,48},{64,72... | collective-permute-start | bytes 1179656 | tf_op jit(solution)/shard_map/ppermute | solution.py:453
  6.0 1.5 %collective-permute-start.2 = (bf16[512,384]{1,0:T(8,128)(2,1)S(1)}, bf16[512,384]{1,0:T(8,128)(2,1)S(1)}, u32[]{:S(2)}, u32[]{:S(2)}) collective-permute-start(bf16[512,384]{1,0:T(8,128)(2,1)S(1)} %get-tuple-element.43), channel_id=1, source_target_pairs={{0,48},{8,56},{16,0},{24,8},{32,16},{40,24},{48,32},{56,40},{64,11... | collective-permute-start | bytes 1179656 | tf_op jit(solution)/shard_map/ppermute | solution.py:453
  7.5 1.8 %fusion = (bf16[512,256]{1,0:T(8,128)(2,1)S(1)}, bf16[512,256]{1,0:T(8,128)(2,1)}) fusion(bf16[512,2048]{1,0:T(8,128)(2,1)} %param.15), kind=kLoop, calls=%fused_computation.1 | loop fusion | bytes 1048576 | tf_op jit(solution)/shard_map/slice | solution.py:467
  9.3 1.3 %collective-permute-start.3 = (bf16[512,256]{1,0:T(8,128)(2,1)}, bf16[512,256]{1,0:T(8,128)(2,1)S(1)}, u32[]{:S(2)}, u32[]{:S(2)}) collective-permute-start(bf16[512,256]{1,0:T(8,128)(2,1)} %get-tuple-element.42), channel_id=1, source_target_pairs={{0,64},{8,72},{16,80},{24,88},{32,96},{40,104},{48,112},{56,120},{... | collective-permute-start | bytes 786440 | tf_op jit(solution)/shard_map/ppermute | solution.py:453
  10.6 1.4 %collective-permute-start.4 = (bf16[512,256]{1,0:T(8,128)(2,1)S(1)}, bf16[512,256]{1,0:T(8,128)(2,1)S(1)}, u32[]{:S(2)}, u32[]{:S(2)}) collective-permute-start(bf16[512,256]{1,0:T(8,128)(2,1)S(1)} %get-tuple-element.41), channel_id=1, source_target_pairs={{0,192},{8,200},{16,208},{24,216},{32,224},{40,232},{48,240},{56,2... | collective-permute-start | bytes 786440 | tf_op jit(solution)/shard_map/ppermute | solution.py:453
  12.9 2.3 %prep.1 = (s32[3,16]{1,0:T(4,128)S(1)}, s32[64]{0:T(128)S(1)}, s32[64]{0:T(128)S(1)}) custom-call(s32[8,32]{1,0:T(8,128)S(1)} %copy-done.2, s32[8]{0:T(128)S(1)} %copy-done.4), custom_call_target="tpu_custom_call" | custom-call | bytes 9000000 | tf_op jit(solution)/shard_map/prep/pallas_call | solution.py:95
  15.2 1.9 %collective-permute-done.3.refs_4_ = bf16[512,256]{1,0:T(8,128)(2,1)S(1)} collective-permute-done((bf16[512,256]{1,0:T(8,128)(2,1)}, bf16[512,256]{1,0:T(8,128)(2,1)S(1)}, u32[]{:S(2)}, u32[]{:S(2)}) %collective-permute-start.3) | collective-permute-done | bytes 262176 | tf_op jit(solution)/shard_map/ppermute | solution.py:453
  17.1 1.7 %pack.1 = bf16[32,128,128]{2,1,0:T(8,128)(2,1)} custom-call(s32[64]{0:T(128)S(1)} %get-tuple-element.23.slot_req, s32[64]{0:T(128)S(1)} %get-tuple-element.24.counts, s32[1]{0:T(128)} %bitcast.2.hold, bf16[8,32,128]{2,1,0:T(8,128)(2,1)S(1)} %reshape.28.q, bf16[512,384]{1,0:T(8,128)(2,1)S(1)} %get-tuple-element.46.refs_0_, ...), custom_call_target="tpu_custom_call" | custom-call | bytes 4500000 | tf_op jit(solution)/shard_map/pack/pallas_call | solution.py:140
  18.8 5.2 %all-to-all-start = ((bf16[32,128,128]{2,1,0:T(8,128)(2,1)}), bf16[32,128,128]{2,1,0:T(8,128)(2,1)S(1)}, u32[]{:S(2)}, u32[]{:S(2)}) async-start(bf16[32,128,128]{2,1,0:T(8,128)(2,1)} %pack.1), calls=%async_computation | async-start | bytes 2097152 | tf_op jit(solution)/shard_map/all_to_all | solution.py:482
  24.1 2.5 %copy-done = bf16[80,128,256]{2,1,0:T(8,128)(2,1)S(1)} copy-done((bf16[80,128,256]{2,1,0:T(8,128)(2,1)S(1)}, bf16[80,128,256]{2,1,0:T(8,128)(2,1)}, u32[]{:S(2)}) %copy-start) | copy-done | bytes 5242904
  26.6 1.9 %local_partials.1 = (f32[8,32,128]{2,1,0:T(8,128)S(1)}, f32[8,32,128]{2,1,0:T(8,128)S(1)}, f32[8,32,128]{2,1,0:T(8,128)S(1)}) custom-call(s32[3,16]{1,0:T(4,128)S(1)} %get-tuple-element.27.local, bf16[80,128,256]{2,1,0:T(8,128)(2,1)S(1)} %copy-done, bf16[8,32,128]{2,1,0:T(8,128)(2,1)S(1)} %reshape.28.q, bf16[8,16,256]{2,1,0:T(8,128)(2,1)S(1)} %pad.4.fresh), custom_call_target="tpu_custom_call" | custom-call | bytes 18000000 | tf_op jit(solution)/shard_map/local_partials/pallas_call | solution.py:270
  28.6 10.5 %all-to-all-done.pay.asked = bf16[32,128,128]{2,1,0:T(8,128)(2,1)S(1)} async-done(((bf16[32,128,128]{2,1,0:T(8,128)(2,1)}), bf16[32,128,128]{2,1,0:T(8,128)(2,1)S(1)}, u32[]{:S(2)}, u32[]{:S(2)}) %all-to-all-start) | async-done | bytes 1048608 | tf_op jit(solution)/shard_map/all_to_all | solution.py:482
  39.7 3.9 %collective-permute-start.5 = (bf16[4,32,128]{2,1,0:T(8,128)(2,1)S(1)}, bf16[4,32,128]{2,1,0:T(8,128)(2,1)S(1)}, u32[]{:S(2)}, u32[]{:S(2)}) collective-permute-start(bf16[4,32,128]{2,1,0:T(8,128)(2,1)S(1)} %get-tuple-element.31), channel_id=1, source_target_pairs={{0,1},{1,0},{2,3},{3,2},{4,5},{5,4},{6,7},{7,6},{8,9},{9,8},{10,11... | collective-permute-start | bytes 98312 | tf_op jit(solution)/shard_map/ppermute | solution.py:492
  45.4 11.5 %all-to-all-start.1 = ((bf16[32,2,32,128]{3,2,1,0:T(8,128)(2,1)}), bf16[32,2,32,128]{3,2,1,0:T(8,128)(2,1)S(1)}, u32[]{:S(2)}, u32[]{:S(2)}) async-start(bf16[32,2,32,128]{3,2,1,0:T(8,128)(2,1)} %bitcast.12), calls=%async_computation.1 | async-start | bytes 1048576 | tf_op jit(solution)/shard_map/all_to_all | solution.py:508
  57.3 1.7 %collective-permute-start.7 = (bf16[256,128]{1,0:T(8,128)(2,1)S(1)}, bf16[256,128]{1,0:T(8,128)(2,1)S(1)}, u32[]{:S(2)}, u32[]{:S(2)}) collective-permute-start(bf16[256,128]{1,0:T(8,128)(2,1)S(1)} %reshape_reshape.3.q0), channel_id=1, source_target_pairs={{0,32},{8,40},{16,48},{24,56},{32,0},{40,8},{48,16},{56,24},{64,96... | collective-permute-start | bytes 196616 | tf_op jit(solution)/shard_map/ppermute | solution.py:453
  60.0 2.5 %copy-done.1 = bf16[80,128,256]{2,1,0:T(8,128)(2,1)S(1)} copy-done((bf16[80,128,256]{2,1,0:T(8,128)(2,1)S(1)}, bf16[80,128,256]{2,1,0:T(8,128)(2,1)}, u32[]{:S(2)}) %copy-start.1) | copy-done | bytes 5242904
  62.5 5.7 %remote_partials.1 = f32[32,72,128]{2,1,0:T(8,128)} custom-call(s32[64]{0:T(128)S(1)} %reshape.26.outbox, bf16[80,128,256]{2,1,0:T(8,128)(2,1)S(1)} %copy-done.1, bf16[32,128,128]{2,1,0:T(8,128)(2,1)S(1)} %all-to-all-done.pay.asked), custom_call_target="tpu_custom_call" | custom-call | bytes 18000000 | tf_op jit(solution)/shard_map/remote_partials/pallas_call | solution.py:222
  68.3 6.1 %all-to-all-start.2 = ((f32[32,72,128]{2,1,0:T(8,128)}), f32[32,72,128]{2,1,0:T(8,128)S(1)}, u32[]{:S(2)}, u32[]{:S(2)}) async-start(f32[32,72,128]{2,1,0:T(8,128)} %remote_partials.1), calls=%async_computation.2 | async-start | bytes 2359296 | tf_op jit(solution)/shard_map/all_to_all | solution.py:517
  74.4 3.8 %prefix_partials.1 = (f32[272,128]{1,0:T(8,128)S(1)}, f32[272,128]{1,0:T(8,128)S(1)}, f32[272,128]{1,0:T(8,128)S(1)}, f32[272,128]{1,0:T(8,128)S(1)}) custom-call(bf16[256,128]{1,0:T(8,128)(2,1)S(1)} %reshape_reshape.3.q0, bf16[256,128]{1,0:T(8,128)(2,1)S(1)} %collective-permute-done.6.q1, bf16[256,128]{1,0:T(8,128)(2,1)S(1)} %collective-permute-done.7.q2, ...), custom_call_target="tpu_custom_call" | custom-call | bytes 18000000 | tf_op jit(solution)/shard_map/prefix_partials/pallas_call | solution.py:325
  78.2 2.5 %collective-permute-start.9 = (f32[272,128]{1,0:T(8,128)S(1)}, f32[272,128]{1,0:T(8,128)S(1)}, u32[]{:S(2)}, u32[]{:S(2)}) collective-permute-start(f32[272,128]{1,0:T(8,128)S(1)} %get-tuple-element.38), channel_id=1, source_target_pairs={{0,48},{8,56},{16,0},{24,8},{32,16},{40,24},{48,32},{56,40},{64,11... | collective-permute-start | bytes 417800 | tf_op jit(solution)/shard_map/ppermute | solution.py:453
  81.8 10.8 %all-to-all-done.2.ret = f32[32,72,128]{2,1,0:T(8,128)S(1)} async-done(((f32[32,72,128]{2,1,0:T(8,128)}), f32[32,72,128]{2,1,0:T(8,128)S(1)}, u32[]{:S(2)}, u32[]{:S(2)}) %all-to-all-start.2) | async-done | bytes 1179680 | tf_op jit(solution)/shard_map/all_to_all | solution.py:517
  92.6 1.9 %merge.1 = (f32[8,32,128]{2,1,0:T(8,128)S(1)}, f32[8,32,128]{2,1,0:T(8,128)S(1)}, f32[8,32,128]{2,1,0:T(8,128)S(1)}) custom-call(s32[1]{0:T(128)} %bitcast.me, s32[64]{0:T(128)S(1)} %get-tuple-element.23.slot_req, f32[32,72,128]{2,1,0:T(8,128)S(1)} %all-to-all-done.2.ret, f32[8,32,128]{2,1,0:T(8,128)S(1)} %get-tuple-element.28.lo, ...), custom_call_target="tpu_custom_call" | custom-call | bytes 6000000 | tf_op jit(solution)/shard_map/merge/pallas_call | solution.py:374
  94.6 1.8 %collective-permute-done.11.p3 = f32[272,128]{1,0:T(8,128)S(1)} collective-permute-done((f32[272,128]{1,0:T(8,128)S(1)}, f32[272,128]{1,0:T(8,128)S(1)}, u32[]{:S(2)}, u32[]{:S(2)}) %collective-permute-start.11) | collective-permute-done | bytes 139296 | tf_op jit(solution)/shard_map/ppermute | solution.py:453
  (42 shorter events, 8.1 us)
Async XLA Ops:
  0.0 12.8 %copy-start.5 = (bf16[8,4,1024]{2,1,0:T(4,128)(2,1)S(1)}, bf16[8,4,1024]{2,1,0:T(4,128)(2,1)}, u32[]{:S(2)}) copy-start(bf16[8,4,1024]{2,1,0:T(4,128)(2,1)} %param.9) | copy-start | bytes 196612
  0.0 12.9 %copy-start.2 = (s32[8,32]{1,0:T(8,128)S(1)}, s32[8,32]{1,0:T(8,128)}, u32[]{:S(2)}) copy-start(s32[8,32]{1,0:T(8,128)} %page.1) | copy-start | bytes 3076
  0.0 12.9 %copy-start.4 = (s32[8]{0:T(128)S(1)}, s32[8]{0:T(128)}, u32[]{:S(2)}) copy-start(s32[8]{0:T(128)} %lens.1) | copy-start | bytes 100
  2.3 14.7 %collective-permute-start = (bf16[512,384]{1,0:T(8,128)(2,1)}, bf16[512,384]{1,0:T(8,128)(2,1)S(1)}, u32[]{:S(2)}, u32[]{:S(2)}) collective-permute-start(bf16[512,384]{1,0:T(8,128)(2,1)} %get-tuple-element.45), channel_id=1, source_target_pairs={{0,8},{8,0},{16,24},{24,16},{32,40},{40,32},{48,56},{56,48},{64,72... | collective-permute-start | bytes 1179656 | tf_op jit(solution)/shard_map/ppermute | solution.py:453
  4.8 12.3 %collective-permute-start.1 = (bf16[512,384]{1,0:T(8,128)(2,1)S(1)}, bf16[512,384]{1,0:T(8,128)(2,1)S(1)}, u32[]{:S(2)}, u32[]{:S(2)}) collective-permute-start(bf16[512,384]{1,0:T(8,128)(2,1)S(1)} %get-tuple-element.44), channel_id=1, source_target_pairs={{0,16},{8,24},{16,32},{24,40},{32,48},{40,56},{48,0},{56,8},{64,80... | collective-permute-start | bytes 1179656 | tf_op jit(solution)/shard_map/ppermute | solution.py:453
  6.0 11.1 %collective-permute-start.2 = (bf16[512,384]{1,0:T(8,128)(2,1)S(1)}, bf16[512,384]{1,0:T(8,128)(2,1)S(1)}, u32[]{:S(2)}, u32[]{:S(2)}) collective-permute-start(bf16[512,384]{1,0:T(8,128)(2,1)S(1)} %get-tuple-element.43), channel_id=1, source_target_pairs={{0,48},{8,56},{16,0},{24,8},{32,16},{40,24},{48,32},{56,40},{64,11... | collective-permute-start | bytes 1179656 | tf_op jit(solution)/shard_map/ppermute | solution.py:453
  9.3 7.8 %collective-permute-start.3 = (bf16[512,256]{1,0:T(8,128)(2,1)}, bf16[512,256]{1,0:T(8,128)(2,1)S(1)}, u32[]{:S(2)}, u32[]{:S(2)}) collective-permute-start(bf16[512,256]{1,0:T(8,128)(2,1)} %get-tuple-element.42), channel_id=1, source_target_pairs={{0,64},{8,72},{16,80},{24,88},{32,96},{40,104},{48,112},{56,120},{... | collective-permute-start | bytes 786440 | tf_op jit(solution)/shard_map/ppermute | solution.py:453
  10.6 6.5 %collective-permute-start.4 = (bf16[512,256]{1,0:T(8,128)(2,1)S(1)}, bf16[512,256]{1,0:T(8,128)(2,1)S(1)}, u32[]{:S(2)}, u32[]{:S(2)}) collective-permute-start(bf16[512,256]{1,0:T(8,128)(2,1)S(1)} %get-tuple-element.41), channel_id=1, source_target_pairs={{0,192},{8,200},{16,208},{24,216},{32,224},{40,232},{48,240},{56,2... | collective-permute-start | bytes 786440 | tf_op jit(solution)/shard_map/ppermute | solution.py:453
  17.1 7.0 %copy-start.6 = (bf16[8,4,256]{2,1,0:T(4,128)(2,1)S(1)}, bf16[8,4,256]{2,1,0:T(4,128)(2,1)}, u32[]{:S(2)}) copy-start(bf16[8,4,256]{2,1,0:T(4,128)(2,1)} %param.10) | copy-start | bytes 49156
  18.8 20.3 %all-to-all-start = ((bf16[32,128,128]{2,1,0:T(8,128)(2,1)}), bf16[32,128,128]{2,1,0:T(8,128)(2,1)S(1)}, u32[]{:S(2)}, u32[]{:S(2)}) async-start(bf16[32,128,128]{2,1,0:T(8,128)(2,1)} %pack.1), calls=%async_computation | async-start | bytes 2097152 | tf_op jit(solution)/shard_map/all_to_all | solution.py:482
  24.1 2.5 %copy-start = (bf16[80,128,256]{2,1,0:T(8,128)(2,1)S(1)}, bf16[80,128,256]{2,1,0:T(8,128)(2,1)}, u32[]{:S(2)}) copy-start(bf16[80,128,256]{2,1,0:T(8,128)(2,1)} %pool.3) | copy-start | bytes 15728644
  28.5 31.3 %copy-start.7 = (s32[1,32,2]{1,2,0:T(2,128)S(1)}, s32[1,32,2]{1,2,0:T(2,128)}, u32[]{:S(2)}) copy-start(s32[1,32,2]{1,2,0:T(2,128)} %param.14) | copy-start | bytes 772
  39.7 4.8 %collective-permute-start.5 = (bf16[4,32,128]{2,1,0:T(8,128)(2,1)S(1)}, bf16[4,32,128]{2,1,0:T(8,128)(2,1)S(1)}, u32[]{:S(2)}, u32[]{:S(2)}) collective-permute-start(bf16[4,32,128]{2,1,0:T(8,128)(2,1)S(1)} %get-tuple-element.31), channel_id=1, source_target_pairs={{0,1},{1,0},{2,3},{3,2},{4,5},{5,4},{6,7},{7,6},{8,9},{9,8},{10,11... | collective-permute-start | bytes 98312 | tf_op jit(solution)/shard_map/ppermute | solution.py:492
  45.4 22.8 %all-to-all-start.1 = ((bf16[32,2,32,128]{3,2,1,0:T(8,128)(2,1)}), bf16[32,2,32,128]{3,2,1,0:T(8,128)(2,1)S(1)}, u32[]{:S(2)}, u32[]{:S(2)}) async-start(bf16[32,2,32,128]{3,2,1,0:T(8,128)(2,1)} %bitcast.12), calls=%async_computation.1 | async-start | bytes 1048576 | tf_op jit(solution)/shard_map/all_to_all | solution.py:508
  56.9 11.3 %collective-permute-start.6 = (bf16[256,128]{1,0:T(8,128)(2,1)S(1)}, bf16[256,128]{1,0:T(8,128)(2,1)S(1)}, u32[]{:S(2)}, u32[]{:S(2)}) collective-permute-start(bf16[256,128]{1,0:T(8,128)(2,1)S(1)} %reshape_reshape.3.q0), channel_id=1, source_target_pairs={{0,16},{8,24},{16,32},{24,40},{32,48},{40,56},{48,0},{56,8},{64,80... | collective-permute-start | bytes 196616 | tf_op jit(solution)/shard_map/ppermute | solution.py:453
  57.3 10.9 %collective-permute-start.7 = (bf16[256,128]{1,0:T(8,128)(2,1)S(1)}, bf16[256,128]{1,0:T(8,128)(2,1)S(1)}, u32[]{:S(2)}, u32[]{:S(2)}) collective-permute-start(bf16[256,128]{1,0:T(8,128)(2,1)S(1)} %reshape_reshape.3.q0), channel_id=1, source_target_pairs={{0,32},{8,40},{16,48},{24,56},{32,0},{40,8},{48,16},{56,24},{64,96... | collective-permute-start | bytes 196616 | tf_op jit(solution)/shard_map/ppermute | solution.py:453
  59.0 9.2 %collective-permute-start.8 = (bf16[256,128]{1,0:T(8,128)(2,1)S(1)}, bf16[256,128]{1,0:T(8,128)(2,1)S(1)}, u32[]{:S(2)}, u32[]{:S(2)}) collective-permute-start(bf16[256,128]{1,0:T(8,128)(2,1)S(1)} %reshape_reshape.3.q0), channel_id=1, source_target_pairs={{0,48},{8,56},{16,0},{24,8},{32,16},{40,24},{48,32},{56,40},{64,11... | collective-permute-start | bytes 196616 | tf_op jit(solution)/shard_map/ppermute | solution.py:453
  60.0 2.5 %copy-start.1 = (bf16[80,128,256]{2,1,0:T(8,128)(2,1)S(1)}, bf16[80,128,256]{2,1,0:T(8,128)(2,1)}, u32[]{:S(2)}) copy-start(bf16[80,128,256]{2,1,0:T(8,128)(2,1)} %pool.3) | copy-start | bytes 15728644
  68.2 28.1 %copy-start.3 = (s32[8]{0:T(128)S(1)}, s32[8]{0:T(128)}, u32[]{:S(2)}) copy-start(s32[8]{0:T(128)} %flags.1) | copy-start | bytes 100
  68.3 24.4 %all-to-all-start.2 = ((f32[32,72,128]{2,1,0:T(8,128)}), f32[32,72,128]{2,1,0:T(8,128)S(1)}, u32[]{:S(2)}, u32[]{:S(2)}) async-start(f32[32,72,128]{2,1,0:T(8,128)} %remote_partials.1), calls=%async_computation.2 | async-start | bytes 2359296 | tf_op jit(solution)/shard_map/all_to_all | solution.py:517
  78.2 16.4 %collective-permute-start.9 = (f32[272,128]{1,0:T(8,128)S(1)}, f32[272,128]{1,0:T(8,128)S(1)}, u32[]{:S(2)}, u32[]{:S(2)}) collective-permute-start(f32[272,128]{1,0:T(8,128)S(1)} %get-tuple-element.38), channel_id=1, source_target_pairs={{0,48},{8,56},{16,0},{24,8},{32,16},{40,24},{48,32},{56,40},{64,11... | collective-permute-start | bytes 417800 | tf_op jit(solution)/shard_map/ppermute | solution.py:453
  80.7 13.9 %collective-permute-start.10 = (f32[272,128]{1,0:T(8,128)S(1)}, f32[272,128]{1,0:T(8,128)S(1)}, u32[]{:S(2)}, u32[]{:S(2)}) collective-permute-start(f32[272,128]{1,0:T(8,128)S(1)} %get-tuple-element.39), channel_id=1, source_target_pairs={{0,32},{8,40},{16,48},{24,56},{32,0},{40,8},{48,16},{56,24},{64,96... | collective-permute-start | bytes 417800 | tf_op jit(solution)/shard_map/ppermute | solution.py:453
  81.3 15.1 %collective-permute-start.11 = (f32[272,128]{1,0:T(8,128)S(1)}, f32[272,128]{1,0:T(8,128)S(1)}, u32[]{:S(2)}, u32[]{:S(2)}) collective-permute-start(f32[272,128]{1,0:T(8,128)S(1)} %get-tuple-element.40), channel_id=1, source_target_pairs={{0,16},{8,24},{16,32},{24,40},{32,48},{40,56},{48,0},{56,8},{64,80... | collective-permute-start | bytes 417800 | tf_op jit(solution)/shard_map/ppermute | solution.py:453

commit v6 on v5

--- a/solution.py
+++ b/solution.py
@@ -108,40 +108,52 @@
 
 
 def pack_kernel(spots, slot_req, counts, hold, q, *refs):
-    sources, pay = refs[:-1], refs[-1]
+    sources, (pay, made, sems) = refs[:-3], refs[-3:]
     rows = q.shape[1]
     body = CAP * rows
     upper = lax.broadcasted_iota(jnp.int32, (16, HD), 0) < 8
     tokens = sources[0].shape[0] // len(spots)
     most = sources[0].shape[1] // HD
-    for d in range(len(spots)):
-        for c in range(CAP):
-            pay[d, c * rows : (c + 1) * rows, :] = q[slot_req[CAP * d + c]]
-        tile = jnp.where(upper, counts[CAP * d], counts[CAP * d + 1])
-        pay[d, body : body + 16, :] = tile.astype(F32).astype(BF16)
-    for k, source in enumerate(sources):
-
-        @pl.when(hold[0] == k)
-        def _():
-            for d, spot in enumerate(spots):
-                for j in range(most):
-                    at = body + 16 + j * tokens
-                    col = (j % (source.shape[1] // HD)) * HD
-                    pay[d, at : at + tokens, :] = source[
-                        spot * tokens : (spot + 1) * tokens, col : col + HD
-                    ]
+    groups = sems.shape[0]
+    each = len(spots) // groups
+    copies = []
+    for g in range(groups):
+        members = range(g * each, (g + 1) * each)
+        for d in members:
+            for c in range(CAP):
+                made[d, c * rows : (c + 1) * rows, :] = q[slot_req[CAP * d + c]]
+            tile = jnp.where(upper, counts[CAP * d], counts[CAP * d + 1])
+            made[d, body : body + 16, :] = tile.astype(F32).astype(BF16)
+        for k, source in enumerate(sources):
+
+            @pl.when(hold[0] == k)
+            def _():
+                for d in members:
+                    for j in range(most):
+                        at = body + 16 + j * tokens
+                        col = (j % (source.shape[1] // HD)) * HD
+                        made[d, at : at + tokens, :] = source[
+                            spots[d] * tokens : (spots[d] + 1) * tokens, col : col + HD
+                        ]
+
+        part = pl.ds(g * each, each)
+        copies.append(pltpu.make_async_copy(made.at[part], pay.at[part], sems.at[g]))
+        copies[-1].start()
+    for copy in copies:
+        copy.wait()
 
 
 def pack(spots, slot_req, counts, hold, q, columns):
     n = len(spots)
     rows = q.shape[1]
     held, wide = columns[0].shape
-    height = CAP * rows + 16 + (wide // HD) * (held // n)
+    shape = (n, CAP * rows + 16 + (wide // HD) * (held // n), HD)
     return pl.pallas_call(
         functools.partial(pack_kernel, spots),
-        out_shape=jax.ShapeDtypeStruct((n, height, HD), BF16),
+        out_shape=jax.ShapeDtypeStruct(shape, BF16),
         in_specs=[SMEM, SMEM, SMEM, VMEM] + [VMEM] * len(columns),
-        out_specs=VMEM,
+        out_specs=pl.BlockSpec(memory_space=pl.ANY),
+        scratch_shapes=[pltpu.VMEM(shape, BF16), pltpu.SemaphoreType.DMA((4,))],
         compiler_params=params(),
         cost_estimate=cost(1.5),
         name="pack",
@@ -278,11 +290,13 @@
     )(local, pool, q, fresh)
 
 
-def prefix_kernel(q0, q1, q2, q3, kv, p0, p1, p2, p3, q, out_o, out_m, out_l):
+def prefix_kernel(count, *refs):
+    sources, kv, targets = refs[:count], refs[count], refs[count + 1 : 2 * count + 1]
+    q, out_o, out_m, out_l = refs[2 * count + 1 :]
     chips, cores, double = kv.shape[1], kv.shape[3], kv.shape[4]
     tokens = double // 2
-    part = q0.shape[0]
-    for s, source in enumerate((q0, q1, q2, q3)):
+    part = sources[0].shape[0]
+    for s, source in enumerate(sources):
         q[s * part : (s + 1) * part, :] = source[...]
     out_o[...] = jnp.zeros_like(out_o)
     out_l[...] = jnp.zeros_like(out_l)
@@ -310,7 +324,7 @@
 
     lax.fori_loop(0, chips, pair, 0)
     lane = lax.broadcasted_iota(jnp.int32, (BLK, HD), 1)
-    for s, target in enumerate((p0, p1, p2, p3)):
+    for s, target in enumerate(targets):
         target[:part, :] = out_o[s * part : (s + 1) * part, :]
         for k in range(part // BLK):
             at = s * part + k * BLK
@@ -321,15 +335,15 @@
 def prefix_partials(queries, kv):
     part = queries[0].shape[0]
     one = jax.ShapeDtypeStruct((part + 8 * (part // BLK), HD), F32)
-    whole = pltpu.VMEM((XS * part, HD), F32)
-    return pl.pallas_call(
-        prefix_kernel,
-        out_shape=(one,) * XS,
-        in_specs=[VMEM] * (XS + 1),
-        out_specs=(VMEM,) * XS,
-        scratch_shapes=[pltpu.VMEM((XS * part, HD), BF16), whole, whole, whole],
-        compiler_params=params(),
-        cost_estimate=cost(6),
+    whole = pltpu.VMEM((len(queries) * part, HD), F32)
+    return pl.pallas_call(
+        functools.partial(prefix_kernel, len(queries)),
+        out_shape=(one,) * len(queries),
+        in_specs=[VMEM] * (len(queries) + 1),
+        out_specs=(VMEM,) * len(queries),
+        scratch_shapes=[pltpu.VMEM((len(queries) * part, HD), BF16), whole, whole, whole],
+        compiler_params=params(),
+        cost_estimate=cost(len(queries)),
         name="prefix_partials",
     )(*queries, kv)
 
@@ -515,8 +529,10 @@
     ).reshape(whole)
     ret = remote_partials(outbox.reshape(-1), pool, asked, rows)
     back = lax.all_to_all(after(ret, prefix, *guests), "inst", split_axis=0, concat_axis=0, tiled=True)
-    past = prefix_partials(guests, prefix)
-    past = [past[0]] + [move(past[s], 0, -s, 0) for s in range(1, XS)]
+    past = prefix_partials(guests[1:], prefix)
+    sent = [move(past[s - 1], 0, -s, 0) for s in range(1, XS)]
+    own = prefix_partials([after(flat, past[0])], prefix)
+    past = [own[0]] + sent
     merged = merge(me.reshape(1), slot_req, back, here)
     out = final(flags, merged, past)
     return out.reshape(req, steps, width)

time: 98.7 us -> 97.9 us (level)
  waiting for transfers between devices: 25.8 us -> 24.5 us
  Pallas kernels: 19 us -> 20.1 us
    all_to_all x1, waiting for transfers between devices: 10.8 us -> 9.57 us  [per_device(): lax.all_to_all(after(ret, prefix, *guests), 'inst', split_axis=0, concat_...]
    pallas_call x1 -> x2, Pallas kernels: 3.77 us -> 4.97 us  [prefix_partials(): pl.pallas_call(functools.partial(prefix_kernel, len(queries)), out_shape=...]
    unnamed x17 -> x19, local copies, waits for them, and re-layouts: 5.08 us -> 5.09 us
  transfers between devices with their start and end apart: 15 -> 15, of which waited for: 5 -> 5; matrix products, arithmetic and copies ran while one was open for 2% -> 2% of each run, Pallas kernels for 16% -> 17%
where the time goes in v6:
time: 97.9 us; the launch traced here: 97.4 us
  starting transfers between devices  41.3 us (42%)
  waiting for transfers between devices  24.5 us (25%)
  Pallas kernels  20.1 us (21%)
  local copies, waits for them, and re-layouts  10.4 us (11%)
  between operations  1.11 us (1%)
    ppermute x11, starting transfers between devices, move(): return lax.ppermute(value, 'inst', pairs)  14.5 us
    all_to_all x1, starting transfers between devices, per_device(): lax.all_to_all(spread.reshape((-1,) + both.shape[1:]), ('inst', 'tp'), sp...  11.4 us
    all_to_all x1, waiting for transfers between devices, per_device(): asked = lax.all_to_all(pay, 'inst', split_axis=0, concat_axis=0, tiled=True)  10.4 us
    all_to_all x1, waiting for transfers between devices, per_device(): lax.all_to_all(after(ret, prefix, *guests), 'inst', split_axis=0, concat_...  9.57 us
    all_to_all x1, starting transfers between devices, per_device(): lax.all_to_all(after(ret, prefix, *guests), 'inst', split_axis=0, concat_...  6 us
    pallas_call x1, Pallas kernels, remote_partials(): pl.pallas_call(remote_kernel, out_shape=jax.ShapeDtypeStruct((n, CAP * ro...  5.71 us
    all_to_all x1, starting transfers between devices, per_device(): asked = lax.all_to_all(pay, 'inst', split_axis=0, concat_axis=0, tiled=True)  5.38 us
    unnamed x19, local copies, waits for them, and re-layouts  5.09 us
  transfers between devices with their start and end apart: 15, of which 5 were waited for; matrix products, arithmetic and copies ran while one was open for 2% of the time, Pallas kernels for 17%

profile of v6, /device:TPU:1, one launch (start us, length us, event | category | flops | bytes accessed | tf_op | source)
XLA Modules:
  0.0 97.4 jit_solution(14382338199221228845)
XLA Ops:
  0.0 1.6 %fusion.1 = (bf16[512,384]{1,0:T(8,128)(2,1)S(1)}, bf16[512,384]{1,0:T(8,128)(2,1)S(1)}, bf16[512,384]{1,0:T(8,128)(2,1)S(1)}, bf16[512,384]{1,0:T(8,128)(2,1)S(1)}) fusion(bf16[512,2048]{1,0:T(8,128)(2,1)} %param.15), kind=kLoop, calls=%fused_computation.2 | loop fusion | bytes 3145728 | tf_op jit(solution)/shard_map/slice | solution.py:481
  1.6 2.6 %collective-permute-start = (bf16[512,384]{1,0:T(8,128)(2,1)S(1)}, bf16[512,384]{1,0:T(8,128)(2,1)S(1)}, u32[]{:S(2)}, u32[]{:S(2)}) collective-permute-start(bf16[512,384]{1,0:T(8,128)(2,1)S(1)} %get-tuple-element.45), channel_id=1, source_target_pairs={{0,8},{8,0},{16,24},{24,16},{32,40},{40,32},{48,56},{56,48},{64,72... | collective-permute-start | bytes 1179656 | tf_op jit(solution)/shard_map/ppermute | solution.py:467
  5.4 1.5 %collective-permute-start.2 = (bf16[512,384]{1,0:T(8,128)(2,1)S(1)}, bf16[512,384]{1,0:T(8,128)(2,1)S(1)}, u32[]{:S(2)}, u32[]{:S(2)}) collective-permute-start(bf16[512,384]{1,0:T(8,128)(2,1)S(1)} %get-tuple-element.43), channel_id=1, source_target_pairs={{0,48},{8,56},{16,0},{24,8},{32,16},{40,24},{48,32},{56,40},{64,11... | collective-permute-start | bytes 1179656 | tf_op jit(solution)/shard_map/ppermute | solution.py:467
  6.8 1.9 %fusion = (bf16[512,256]{1,0:T(8,128)(2,1)}, bf16[512,256]{1,0:T(8,128)(2,1)}) fusion(bf16[512,2048]{1,0:T(8,128)(2,1)} %param.15), kind=kLoop, calls=%fused_computation.1 | loop fusion | bytes 1048576 | tf_op jit(solution)/shard_map/slice | solution.py:481
  10.0 1.4 %collective-permute-start.4 = (bf16[512,256]{1,0:T(8,128)(2,1)}, bf16[512,256]{1,0:T(8,128)(2,1)S(1)}, u32[]{:S(2)}, u32[]{:S(2)}) collective-permute-start(bf16[512,256]{1,0:T(8,128)(2,1)} %get-tuple-element.41), channel_id=1, source_target_pairs={{0,192},{8,200},{16,208},{24,216},{32,224},{40,232},{48,240},{56,2... | collective-permute-start | bytes 786440 | tf_op jit(solution)/shard_map/ppermute | solution.py:467
  12.3 2.3 %prep.1 = (s32[3,16]{1,0:T(4,128)S(1)}, s32[64]{0:T(128)S(1)}, s32[64]{0:T(128)S(1)}) custom-call(s32[8,32]{1,0:T(8,128)S(1)} %copy-done.2, s32[8]{0:T(128)S(1)} %copy-done.4), custom_call_target="tpu_custom_call" | custom-call | bytes 9000000 | tf_op jit(solution)/shard_map/prep/pallas_call | solution.py:95
  14.6 1.9 %collective-permute-done.3.refs_4_ = bf16[512,256]{1,0:T(8,128)(2,1)S(1)} collective-permute-done((bf16[512,256]{1,0:T(8,128)(2,1)}, bf16[512,256]{1,0:T(8,128)(2,1)S(1)}, u32[]{:S(2)}, u32[]{:S(2)}) %collective-permute-start.3) | collective-permute-done | bytes 262176 | tf_op jit(solution)/shard_map/ppermute | solution.py:467
  16.5 1.6 %pack.1 = bf16[32,128,128]{2,1,0:T(8,128)(2,1)} custom-call(s32[64]{0:T(128)S(1)} %get-tuple-element.23.slot_req, s32[64]{0:T(128)S(1)} %get-tuple-element.24.counts, s32[1]{0:T(128)} %bitcast.2.hold, bf16[8,32,128]{2,1,0:T(8,128)(2,1)S(1)} %reshape.28.q, bf16[512,384]{1,0:T(8,128)(2,1)S(1)} %get-tuple-element.46.refs_0_, ...), custom_call_target="tpu_custom_call" | custom-call | bytes 4500000 | tf_op jit(solution)/shard_map/pack/pallas_call | solution.py:151
  18.2 5.4 %all-to-all-start = ((bf16[32,128,128]{2,1,0:T(8,128)(2,1)}), bf16[32,128,128]{2,1,0:T(8,128)(2,1)S(1)}, u32[]{:S(2)}, u32[]{:S(2)}) async-start(bf16[32,128,128]{2,1,0:T(8,128)(2,1)} %pack.1), calls=%async_computation | async-start | bytes 2097152 | tf_op jit(solution)/shard_map/all_to_all | solution.py:496
  23.6 2.5 %copy-done = bf16[80,128,256]{2,1,0:T(8,128)(2,1)S(1)} copy-done((bf16[80,128,256]{2,1,0:T(8,128)(2,1)S(1)}, bf16[80,128,256]{2,1,0:T(8,128)(2,1)}, u32[]{:S(2)}) %copy-start) | copy-done | bytes 5242904
  26.1 1.9 %local_partials.1 = (f32[8,32,128]{2,1,0:T(8,128)S(1)}, f32[8,32,128]{2,1,0:T(8,128)S(1)}, f32[8,32,128]{2,1,0:T(8,128)S(1)}) custom-call(s32[3,16]{1,0:T(4,128)S(1)} %get-tuple-element.27.local, bf16[80,128,256]{2,1,0:T(8,128)(2,1)S(1)} %copy-done, bf16[8,32,128]{2,1,0:T(8,128)(2,1)S(1)} %reshape.28.q, bf16[8,16,256]{2,1,0:T(8,128)(2,1)S(1)} %pad.4.fresh), custom_call_target="tpu_custom_call" | custom-call | bytes 18000000 | tf_op jit(solution)/shard_map/local_partials/pallas_call | solution.py:282
  28.1 10.4 %all-to-all-done.pay.asked = bf16[32,128,128]{2,1,0:T(8,128)(2,1)S(1)} async-done(((bf16[32,128,128]{2,1,0:T(8,128)(2,1)}), bf16[32,128,128]{2,1,0:T(8,128)(2,1)S(1)}, u32[]{:S(2)}, u32[]{:S(2)}) %all-to-all-start) | async-done | bytes 1048608 | tf_op jit(solution)/shard_map/all_to_all | solution.py:496
  39.1 4.0 %collective-permute-start.5 = (bf16[4,32,128]{2,1,0:T(8,128)(2,1)S(1)}, bf16[4,32,128]{2,1,0:T(8,128)(2,1)S(1)}, u32[]{:S(2)}, u32[]{:S(2)}) collective-permute-start(bf16[4,32,128]{2,1,0:T(8,128)(2,1)S(1)} %get-tuple-element.31), channel_id=1, source_target_pairs={{0,1},{1,0},{2,3},{3,2},{4,5},{5,4},{6,7},{7,6},{8,9},{9,8},{10,11... | collective-permute-start | bytes 98312 | tf_op jit(solution)/shard_map/ppermute | solution.py:506
  44.9 11.4 %all-to-all-start.1 = ((bf16[32,2,32,128]{3,2,1,0:T(8,128)(2,1)}), bf16[32,2,32,128]{3,2,1,0:T(8,128)(2,1)S(1)}, u32[]{:S(2)}, u32[]{:S(2)}) async-start(bf16[32,2,32,128]{3,2,1,0:T(8,128)(2,1)} %bitcast.12), calls=%async_computation.1 | async-start | bytes 1048576 | tf_op jit(solution)/shard_map/all_to_all | solution.py:522
  56.8 1.7 %collective-permute-start.7 = (bf16[256,128]{1,0:T(8,128)(2,1)S(1)}, bf16[256,128]{1,0:T(8,128)(2,1)S(1)}, u32[]{:S(2)}, u32[]{:S(2)}) collective-permute-start(bf16[256,128]{1,0:T(8,128)(2,1)S(1)} %reshape_reshape.3.refs_0_), channel_id=1, source_target_pairs={{0,32},{8,40},{16,48},{24,56},{32,0},{40,8},{48,16},{56,24},{64,96... | collective-permute-start | bytes 196616 | tf_op jit(solution)/shard_map/ppermute | solution.py:467
  59.5 2.5 %copy-done.1 = bf16[80,128,256]{2,1,0:T(8,128)(2,1)S(1)} copy-done((bf16[80,128,256]{2,1,0:T(8,128)(2,1)S(1)}, bf16[80,128,256]{2,1,0:T(8,128)(2,1)}, u32[]{:S(2)}) %copy-start.1) | copy-done | bytes 5242904
  62.0 5.7 %remote_partials.1 = f32[32,72,128]{2,1,0:T(8,128)} custom-call(s32[64]{0:T(128)S(1)} %reshape.26.outbox, bf16[80,128,256]{2,1,0:T(8,128)(2,1)S(1)} %copy-done.1, bf16[32,128,128]{2,1,0:T(8,128)(2,1)S(1)} %all-to-all-done.pay.asked), custom_call_target="tpu_custom_call" | custom-call | bytes 18000000 | tf_op jit(solution)/shard_map/remote_partials/pallas_call | solution.py:234
  67.7 6.0 %all-to-all-start.2 = ((f32[32,72,128]{2,1,0:T(8,128)}), f32[32,72,128]{2,1,0:T(8,128)S(1)}, u32[]{:S(2)}, u32[]{:S(2)}) async-start(f32[32,72,128]{2,1,0:T(8,128)} %remote_partials.1), calls=%async_computation.2 | async-start | bytes 2359296 | tf_op jit(solution)/shard_map/all_to_all | solution.py:531
  73.7 3.1 %prefix_partials.2 = (f32[272,128]{1,0:T(8,128)S(1)}, f32[272,128]{1,0:T(8,128)S(1)}, f32[272,128]{1,0:T(8,128)S(1)}) custom-call(bf16[256,128]{1,0:T(8,128)(2,1)S(1)} %collective-permute-done.6.refs_0_, bf16[256,128]{1,0:T(8,128)(2,1)S(1)} %collective-permute-done.7.refs_1_, bf16[256,128]{1,0:T(8,128)(2,1)S(1)} %collective-permute-done.8.refs_2_, ...), custom_call_target="tpu_custom_call" | custom-call | bytes 9000000 | tf_op jit(solution)/shard_map/prefix_partials/pallas_call | solution.py:339
  76.8 2.5 %collective-permute-start.9 = (f32[272,128]{1,0:T(8,128)S(1)}, f32[272,128]{1,0:T(8,128)S(1)}, u32[]{:S(2)}, u32[]{:S(2)}) collective-permute-start(f32[272,128]{1,0:T(8,128)S(1)} %get-tuple-element.37), channel_id=1, source_target_pairs={{0,48},{8,56},{16,0},{24,8},{32,16},{40,24},{48,32},{56,40},{64,11... | collective-permute-start | bytes 417800 | tf_op jit(solution)/shard_map/ppermute | solution.py:467
  80.4 1.9 %prefix_partials.3.p0 = f32[272,128]{1,0:T(8,128)S(1)} custom-call(bf16[256,128]{1,0:T(8,128)(2,1)S(1)} %reshape_reshape.3.refs_0_, bf16[4,4,2,2,32,128]{5,4,3,2,1,0:T(8,128)(2,1)S(1)} %bitcast.20), custom_call_target="tpu_custom_call" | custom-call | bytes 3000000 | tf_op jit(solution)/shard_map/prefix_partials/pallas_call | solution.py:339
  82.3 9.6 %all-to-all-done.2.ret = f32[32,72,128]{2,1,0:T(8,128)S(1)} async-done(((f32[32,72,128]{2,1,0:T(8,128)}), f32[32,72,128]{2,1,0:T(8,128)S(1)}, u32[]{:S(2)}, u32[]{:S(2)}) %all-to-all-start.2) | async-done | bytes 1179680 | tf_op jit(solution)/shard_map/all_to_all | solution.py:531
  91.9 1.9 %merge.1 = (f32[8,32,128]{2,1,0:T(8,128)S(1)}, f32[8,32,128]{2,1,0:T(8,128)S(1)}, f32[8,32,128]{2,1,0:T(8,128)S(1)}) custom-call(s32[1]{0:T(128)} %bitcast.me, s32[64]{0:T(128)S(1)} %get-tuple-element.23.slot_req, f32[32,72,128]{2,1,0:T(8,128)S(1)} %all-to-all-done.2.ret, f32[8,32,128]{2,1,0:T(8,128)S(1)} %get-tuple-element.28.lo, ...), custom_call_target="tpu_custom_call" | custom-call | bytes 6000000 | tf_op jit(solution)/shard_map/merge/pallas_call | solution.py:388
  93.9 1.8 %collective-permute-done.11.p3 = f32[272,128]{1,0:T(8,128)S(1)} collective-permute-done((f32[272,128]{1,0:T(8,128)S(1)}, f32[272,128]{1,0:T(8,128)S(1)}, u32[]{:S(2)}, u32[]{:S(2)}) %collective-permute-start.11) | collective-permute-done | bytes 139296 | tf_op jit(solution)/shard_map/ppermute | solution.py:467
  (45 shorter events, 9.4 us)
Async XLA Ops:
  0.0 12.3 %copy-start.5 = (bf16[8,4,1024]{2,1,0:T(4,128)(2,1)S(1)}, bf16[8,4,1024]{2,1,0:T(4,128)(2,1)}, u32[]{:S(2)}) copy-start(bf16[8,4,1024]{2,1,0:T(4,128)(2,1)} %param.9) | copy-start | bytes 196612
  0.0 12.3 %copy-start.2 = (s32[8,32]{1,0:T(8,128)S(1)}, s32[8,32]{1,0:T(8,128)}, u32[]{:S(2)}) copy-start(s32[8,32]{1,0:T(8,128)} %page.1) | copy-start | bytes 3076
  0.0 12.3 %copy-start.4 = (s32[8]{0:T(128)S(1)}, s32[8]{0:T(128)}, u32[]{:S(2)}) copy-start(s32[8]{0:T(128)} %lens.1) | copy-start | bytes 100
  1.6 14.9 %collective-permute-start = (bf16[512,384]{1,0:T(8,128)(2,1)S(1)}, bf16[512,384]{1,0:T(8,128)(2,1)S(1)}, u32[]{:S(2)}, u32[]{:S(2)}) collective-permute-start(bf16[512,384]{1,0:T(8,128)(2,1)S(1)} %get-tuple-element.45), channel_id=1, source_target_pairs={{0,8},{8,0},{16,24},{24,16},{32,40},{40,32},{48,56},{56,48},{64,72... | collective-permute-start | bytes 1179656 | tf_op jit(solution)/shard_map/ppermute | solution.py:467
  4.1 12.4 %collective-permute-start.1 = (bf16[512,384]{1,0:T(8,128)(2,1)S(1)}, bf16[512,384]{1,0:T(8,128)(2,1)S(1)}, u32[]{:S(2)}, u32[]{:S(2)}) collective-permute-start(bf16[512,384]{1,0:T(8,128)(2,1)S(1)} %get-tuple-element.44), channel_id=1, source_target_pairs={{0,16},{8,24},{16,32},{24,40},{32,48},{40,56},{48,0},{56,8},{64,80... | collective-permute-start | bytes 1179656 | tf_op jit(solution)/shard_map/ppermute | solution.py:467
  5.4 11.2 %collective-permute-start.2 = (bf16[512,384]{1,0:T(8,128)(2,1)S(1)}, bf16[512,384]{1,0:T(8,128)(2,1)S(1)}, u32[]{:S(2)}, u32[]{:S(2)}) collective-permute-start(bf16[512,384]{1,0:T(8,128)(2,1)S(1)} %get-tuple-element.43), channel_id=1, source_target_pairs={{0,48},{8,56},{16,0},{24,8},{32,16},{40,24},{48,32},{56,40},{64,11... | collective-permute-start | bytes 1179656 | tf_op jit(solution)/shard_map/ppermute | solution.py:467
  8.7 7.8 %collective-permute-start.3 = (bf16[512,256]{1,0:T(8,128)(2,1)}, bf16[512,256]{1,0:T(8,128)(2,1)S(1)}, u32[]{:S(2)}, u32[]{:S(2)}) collective-permute-start(bf16[512,256]{1,0:T(8,128)(2,1)} %get-tuple-element.42), channel_id=1, source_target_pairs={{0,64},{8,72},{16,80},{24,88},{32,96},{40,104},{48,112},{56,120},{... | collective-permute-start | bytes 786440 | tf_op jit(solution)/shard_map/ppermute | solution.py:467
  10.0 6.5 %collective-permute-start.4 = (bf16[512,256]{1,0:T(8,128)(2,1)}, bf16[512,256]{1,0:T(8,128)(2,1)S(1)}, u32[]{:S(2)}, u32[]{:S(2)}) collective-permute-start(bf16[512,256]{1,0:T(8,128)(2,1)} %get-tuple-element.41), channel_id=1, source_target_pairs={{0,192},{8,200},{16,208},{24,216},{32,224},{40,232},{48,240},{56,2... | collective-permute-start | bytes 786440 | tf_op jit(solution)/shard_map/ppermute | solution.py:467
  16.5 7.1 %copy-start.7 = (bf16[8,4,256]{2,1,0:T(4,128)(2,1)S(1)}, bf16[8,4,256]{2,1,0:T(4,128)(2,1)}, u32[]{:S(2)}) copy-start(bf16[8,4,256]{2,1,0:T(4,128)(2,1)} %param.10) | copy-start | bytes 49156
  18.2 20.4 %all-to-all-start = ((bf16[32,128,128]{2,1,0:T(8,128)(2,1)}), bf16[32,128,128]{2,1,0:T(8,128)(2,1)S(1)}, u32[]{:S(2)}, u32[]{:S(2)}) async-start(bf16[32,128,128]{2,1,0:T(8,128)(2,1)} %pack.1), calls=%async_computation | async-start | bytes 2097152 | tf_op jit(solution)/shard_map/all_to_all | solution.py:496
  23.6 2.5 %copy-start = (bf16[80,128,256]{2,1,0:T(8,128)(2,1)S(1)}, bf16[80,128,256]{2,1,0:T(8,128)(2,1)}, u32[]{:S(2)}) copy-start(bf16[80,128,256]{2,1,0:T(8,128)(2,1)} %pool.3) | copy-start | bytes 15728644
  28.0 28.3 %copy-start.6 = (bf16[8,4,1024]{2,1,0:T(4,128)(2,1)S(1)}, bf16[8,4,1024]{2,1,0:T(4,128)(2,1)}, u32[]{:S(2)}) copy-start(bf16[8,4,1024]{2,1,0:T(4,128)(2,1)} %param.9) | copy-start | bytes 196612
  28.0 31.2 %copy-start.8 = (s32[1,32,2]{1,2,0:T(2,128)S(1)}, s32[1,32,2]{1,2,0:T(2,128)}, u32[]{:S(2)}) copy-start(s32[1,32,2]{1,2,0:T(2,128)} %param.14) | copy-start | bytes 772
  39.1 4.9 %collective-permute-start.5 = (bf16[4,32,128]{2,1,0:T(8,128)(2,1)S(1)}, bf16[4,32,128]{2,1,0:T(8,128)(2,1)S(1)}, u32[]{:S(2)}, u32[]{:S(2)}) collective-permute-start(bf16[4,32,128]{2,1,0:T(8,128)(2,1)S(1)} %get-tuple-element.31), channel_id=1, source_target_pairs={{0,1},{1,0},{2,3},{3,2},{4,5},{5,4},{6,7},{7,6},{8,9},{9,8},{10,11... | collective-permute-start | bytes 98312 | tf_op jit(solution)/shard_map/ppermute | solution.py:506
  44.9 22.8 %all-to-all-start.1 = ((bf16[32,2,32,128]{3,2,1,0:T(8,128)(2,1)}), bf16[32,2,32,128]{3,2,1,0:T(8,128)(2,1)S(1)}, u32[]{:S(2)}, u32[]{:S(2)}) async-start(bf16[32,2,32,128]{3,2,1,0:T(8,128)(2,1)} %bitcast.12), calls=%async_computation.1 | async-start | bytes 1048576 | tf_op jit(solution)/shard_map/all_to_all | solution.py:522
  56.4 11.3 %collective-permute-start.6 = (bf16[256,128]{1,0:T(8,128)(2,1)S(1)}, bf16[256,128]{1,0:T(8,128)(2,1)S(1)}, u32[]{:S(2)}, u32[]{:S(2)}) collective-permute-start(bf16[256,128]{1,0:T(8,128)(2,1)S(1)} %reshape_reshape.3.refs_0_), channel_id=1, source_target_pairs={{0,16},{8,24},{16,32},{24,40},{32,48},{40,56},{48,0},{56,8},{64,80... | collective-permute-start | bytes 196616 | tf_op jit(solution)/shard_map/ppermute | solution.py:467
  56.8 10.9 %collective-permute-start.7 = (bf16[256,128]{1,0:T(8,128)(2,1)S(1)}, bf16[256,128]{1,0:T(8,128)(2,1)S(1)}, u32[]{:S(2)}, u32[]{:S(2)}) collective-permute-start(bf16[256,128]{1,0:T(8,128)(2,1)S(1)} %reshape_reshape.3.refs_0_), channel_id=1, source_target_pairs={{0,32},{8,40},{16,48},{24,56},{32,0},{40,8},{48,16},{56,24},{64,96... | collective-permute-start | bytes 196616 | tf_op jit(solution)/shard_map/ppermute | solution.py:467
  58.4 9.2 %collective-permute-start.8 = (bf16[256,128]{1,0:T(8,128)(2,1)S(1)}, bf16[256,128]{1,0:T(8,128)(2,1)S(1)}, u32[]{:S(2)}, u32[]{:S(2)}) collective-permute-start(bf16[256,128]{1,0:T(8,128)(2,1)S(1)} %reshape_reshape.3.refs_0_), channel_id=1, source_target_pairs={{0,48},{8,56},{16,0},{24,8},{32,16},{40,24},{48,32},{56,40},{64,11... | collective-permute-start | bytes 196616 | tf_op jit(solution)/shard_map/ppermute | solution.py:467
  59.5 2.5 %copy-start.1 = (bf16[80,128,256]{2,1,0:T(8,128)(2,1)S(1)}, bf16[80,128,256]{2,1,0:T(8,128)(2,1)}, u32[]{:S(2)}) copy-start(bf16[80,128,256]{2,1,0:T(8,128)(2,1)} %pool.3) | copy-start | bytes 15728644
  67.7 24.2 %all-to-all-start.2 = ((f32[32,72,128]{2,1,0:T(8,128)}), f32[32,72,128]{2,1,0:T(8,128)S(1)}, u32[]{:S(2)}, u32[]{:S(2)}) async-start(f32[32,72,128]{2,1,0:T(8,128)} %remote_partials.1), calls=%async_computation.2 | async-start | bytes 2359296 | tf_op jit(solution)/shard_map/all_to_all | solution.py:531
  73.7 22.0 %copy-start.3 = (s32[8]{0:T(128)S(1)}, s32[8]{0:T(128)}, u32[]{:S(2)}) copy-start(s32[8]{0:T(128)} %flags.1) | copy-start | bytes 100
  76.8 17.1 %collective-permute-start.9 = (f32[272,128]{1,0:T(8,128)S(1)}, f32[272,128]{1,0:T(8,128)S(1)}, u32[]{:S(2)}, u32[]{:S(2)}) collective-permute-start(f32[272,128]{1,0:T(8,128)S(1)} %get-tuple-element.37), channel_id=1, source_target_pairs={{0,48},{8,56},{16,0},{24,8},{32,16},{40,24},{48,32},{56,40},{64,11... | collective-permute-start | bytes 417800 | tf_op jit(solution)/shard_map/ppermute | solution.py:467
  79.3 14.6 %collective-permute-start.10 = (f32[272,128]{1,0:T(8,128)S(1)}, f32[272,128]{1,0:T(8,128)S(1)}, u32[]{:S(2)}, u32[]{:S(2)}) collective-permute-start(f32[272,128]{1,0:T(8,128)S(1)} %get-tuple-element.39), channel_id=1, source_target_pairs={{0,32},{8,40},{16,48},{24,56},{32,0},{40,8},{48,16},{56,24},{64,96... | collective-permute-start | bytes 417800 | tf_op jit(solution)/shard_map/ppermute | solution.py:467
  79.8 15.8 %collective-permute-start.11 = (f32[272,128]{1,0:T(8,128)S(1)}, f32[272,128]{1,0:T(8,128)S(1)}, u32[]{:S(2)}, u32[]{:S(2)}) collective-permute-start(f32[272,128]{1,0:T(8,128)S(1)} %get-tuple-element.40), channel_id=1, source_target_pairs={{0,16},{8,24},{16,32},{24,40},{32,48},{40,56},{48,0},{56,8},{64,80... | collective-permute-start | bytes 417800 | tf_op jit(solution)/shard_map/ppermute | solution.py:467

commit v7 on v6

--- a/solution.py
+++ b/solution.py
@@ -196,7 +196,7 @@
     )(core, holders, asked)
 
 
-def remote_kernel(outbox, pool, pay, ret):
+def remote_kernel(outbox, pool, pay, back, ret, sems):
     n = pay.shape[0]
     rows = (ret.shape[1] - 8) // CAP
     each = BLK // rows
@@ -224,18 +224,30 @@
         turned = jnp.concatenate(stats, axis=0).T[:8]
         for i in range(each):
             ret[g * each + i, CAP * rows : CAP * rows + 8, :] = turned
+        leave(g).start()
         return carry
 
+    def leave(g):
+        part = pl.ds(g * each, each)
+        return pltpu.make_async_copy(ret.at[part], back.at[part], sems.at[g])
+
+    def left(g, carry):
+        leave(g).wait()
+        return carry
+
     lax.fori_loop(0, n // each, group, 0)
+    lax.fori_loop(0, n // each, left, 0)
 
 
 def remote_partials(outbox, pool, pay, rows):
     n = pay.shape[0]
+    shape = (n, CAP * rows + 8, HD)
     return pl.pallas_call(
         remote_kernel,
-        out_shape=jax.ShapeDtypeStruct((n, CAP * rows + 8, HD), F32),
+        out_shape=jax.ShapeDtypeStruct(shape, F32),
         in_specs=[SMEM, VMEM, VMEM],
-        out_specs=VMEM,
+        out_specs=pl.BlockSpec(memory_space=pl.ANY),
+        scratch_shapes=[pltpu.VMEM(shape, F32), pltpu.SemaphoreType.DMA((n * rows // BLK,))],
         compiler_params=params(),
         cost_estimate=cost(6),
         name="remote_partials",
@@ -474,13 +486,15 @@
         (2, 1, 0, 0),
         (2, -1, 0, 0),
     )
-    columns = []
-    holders = []
+    parts = []
     first = 0
-    for units, dy, dx, dz in steps_out:
-        part = prefix_store[:, first * HD : (first + units) * HD]
+    for units, _, _, _ in steps_out:
+        parts.append(prefix_store[:, first * HD : (first + units) * HD] if first else None)
         first += units
-        columns.append(move(part, dy, dx, dz) if holders else part)
+    columns = [after(prefix_store, *parts[1:])[:, : steps_out[0][0] * HD]]
+    holders = [owned]
+    for part, (_, dy, dx, dz) in zip(parts[1:], steps_out[1:]):
+        columns.append(move(part, dy, dx, dz))
         holders.append(index(owned // (XS * ZS) + dy, owned // ZS + dx, owned + dz))
     hold = sum(jnp.where(me == holders[k], k, 0) for k in range(1, len(steps_out)))
     spots = [

time: 97.9 us -> 97.8 us (level)
  waiting for transfers between devices: 24.5 us -> 23.5 us
    ppermute x11, waiting for transfers between devices: 3.69 us -> 2.7 us  [move(): return lax.ppermute(value, 'inst', pairs)]
    slice x2 -> x3, local copies, waits for them, and re-layouts: 3.43 us -> 4.33 us  [the longest x2 3.29 us: per_device(): prefix_store[:, first * HD:(first + units) * HD]]
    unnamed x19 -> x17, local copies, waits for them, and re-layouts: 5.09 us -> 5.08 us
  transfers between devices with their start and end apart: 15 -> 15, of which waited for: 5 -> 5; matrix products, arithmetic and copies ran while one was open for 2% -> 3% of each run, Pallas kernels for 17% -> 17%
where the time goes in v7:
time: 97.8 us; the launch traced here: 97.3 us
  starting transfers between devices  41.6 us (43%)
  waiting for transfers between devices  23.5 us (24%)
  Pallas kernels  19.8 us (20%)
  local copies, waits for them, and re-layouts  11.3 us (12%)
  between operations  1.12 us (1%)
    ppermute x11, starting transfers between devices, move(): return lax.ppermute(value, 'inst', pairs)  14.5 us
    all_to_all x1, starting transfers between devices, per_device(): lax.all_to_all(spread.reshape((-1,) + both.shape[1:]), ('inst', 'tp'), sp...  11.4 us
    all_to_all x1, waiting for transfers between devices, per_device(): asked = lax.all_to_all(pay, 'inst', split_axis=0, concat_axis=0, tiled=True)  10.4 us
    all_to_all x1, waiting for transfers between devices, per_device(): lax.all_to_all(after(ret, prefix, *guests), 'inst', split_axis=0, concat_...  9.55 us
    all_to_all x1, starting transfers between devices, per_device(): lax.all_to_all(after(ret, prefix, *guests), 'inst', split_axis=0, concat_...  6.29 us
    pallas_call x1, Pallas kernels, remote_partials(): pl.pallas_call(remote_kernel, out_shape=jax.ShapeDtypeStruct(shape, F32),...  5.41 us
    all_to_all x1, starting transfers between devices, per_device(): asked = lax.all_to_all(pay, 'inst', split_axis=0, concat_axis=0, tiled=True)  5.38 us
    unnamed x17, local copies, waits for them, and re-layouts  5.08 us
  transfers between devices with their start and end apart: 15, of which 5 were waited for; matrix products, arithmetic and copies ran while one was open for 3% of the time, Pallas kernels for 17%

profile of v7, /device:TPU:1, one launch (start us, length us, event | category | flops | bytes accessed | tf_op | source)
XLA Modules:
  0.0 97.3 jit_solution(14661284615584794376)
XLA Ops:
  0.0 1.4 %fusion.1 = (bf16[512,384]{1,0:T(8,128)(2,1)S(1)}, bf16[512,384]{1,0:T(8,128)(2,1)S(1)}, bf16[512,384]{1,0:T(8,128)(2,1)S(1)}) fusion(bf16[512,2048]{1,0:T(8,128)(2,1)} %param.15), kind=kLoop, calls=%fused_computation.2 | loop fusion | bytes 2359296 | tf_op jit(solution)/shard_map/slice | solution.py:492
  1.4 2.6 %collective-permute-start = (bf16[512,384]{1,0:T(8,128)(2,1)S(1)}, bf16[512,384]{1,0:T(8,128)(2,1)S(1)}, u32[]{:S(2)}, u32[]{:S(2)}) collective-permute-start(bf16[512,384]{1,0:T(8,128)(2,1)S(1)} %get-tuple-element.47), channel_id=1, source_target_pairs={{0,8},{8,0},{16,24},{24,16},{32,40},{40,32},{48,56},{56,48},{64,72... | collective-permute-start | bytes 1179656 | tf_op jit(solution)/shard_map/ppermute | solution.py:479
  5.2 1.5 %collective-permute-start.2 = (bf16[512,384]{1,0:T(8,128)(2,1)S(1)}, bf16[512,384]{1,0:T(8,128)(2,1)S(1)}, u32[]{:S(2)}, u32[]{:S(2)}) collective-permute-start(bf16[512,384]{1,0:T(8,128)(2,1)S(1)} %get-tuple-element.45), channel_id=1, source_target_pairs={{0,48},{8,56},{16,0},{24,8},{32,16},{40,24},{48,32},{56,40},{64,11... | collective-permute-start | bytes 1179656 | tf_op jit(solution)/shard_map/ppermute | solution.py:479
  6.7 1.9 %fusion = (bf16[512,256]{1,0:T(8,128)(2,1)}, bf16[512,256]{1,0:T(8,128)(2,1)}) fusion(bf16[512,2048]{1,0:T(8,128)(2,1)} %param.15), kind=kLoop, calls=%fused_computation.1 | loop fusion | bytes 1048576 | tf_op jit(solution)/shard_map/slice | solution.py:492
  8.5 1.3 %collective-permute-start.3 = (bf16[512,256]{1,0:T(8,128)(2,1)}, bf16[512,256]{1,0:T(8,128)(2,1)S(1)}, u32[]{:S(2)}, u32[]{:S(2)}) collective-permute-start(bf16[512,256]{1,0:T(8,128)(2,1)} %get-tuple-element.44), channel_id=1, source_target_pairs={{0,64},{8,72},{16,80},{24,88},{32,96},{40,104},{48,112},{56,120},{... | collective-permute-start | bytes 786440 | tf_op jit(solution)/shard_map/ppermute | solution.py:479
  9.8 1.4 %collective-permute-start.4 = (bf16[512,256]{1,0:T(8,128)(2,1)}, bf16[512,256]{1,0:T(8,128)(2,1)S(1)}, u32[]{:S(2)}, u32[]{:S(2)}) collective-permute-start(bf16[512,256]{1,0:T(8,128)(2,1)} %get-tuple-element.43), channel_id=1, source_target_pairs={{0,192},{8,200},{16,208},{24,216},{32,224},{40,232},{48,240},{56,2... | collective-permute-start | bytes 786440 | tf_op jit(solution)/shard_map/ppermute | solution.py:479
  13.2 2.2 %prep.1 = (s32[3,16]{1,0:T(4,128)S(1)}, s32[64]{0:T(128)S(1)}, s32[64]{0:T(128)S(1)}) custom-call(s32[8,32]{1,0:T(8,128)S(1)} %copy-done.2, s32[8]{0:T(128)S(1)} %copy-done.4), custom_call_target="tpu_custom_call" | custom-call | bytes 9000000 | tf_op jit(solution)/shard_map/prep/pallas_call | solution.py:95
  16.4 1.6 %pack.1 = bf16[32,128,128]{2,1,0:T(8,128)(2,1)} custom-call(s32[64]{0:T(128)S(1)} %get-tuple-element.24.slot_req, s32[64]{0:T(128)S(1)} %get-tuple-element.25.counts, s32[1]{0:T(128)} %bitcast.2.hold, bf16[8,32,128]{2,1,0:T(8,128)(2,1)S(1)} %reshape.28.q, bf16[512,384]{1,0:T(8,128)(2,1)S(1)} %slice.23.refs_0_, ...), custom_call_target="tpu_custom_call" | custom-call | bytes 4500000 | tf_op jit(solution)/shard_map/pack/pallas_call | solution.py:151
  18.0 5.4 %all-to-all-start = ((bf16[32,128,128]{2,1,0:T(8,128)(2,1)}), bf16[32,128,128]{2,1,0:T(8,128)(2,1)S(1)}, u32[]{:S(2)}, u32[]{:S(2)}) async-start(bf16[32,128,128]{2,1,0:T(8,128)(2,1)} %pack.1), calls=%async_computation | async-start | bytes 2097152 | tf_op jit(solution)/shard_map/all_to_all | solution.py:510
  23.5 2.5 %copy-done = bf16[80,128,256]{2,1,0:T(8,128)(2,1)S(1)} copy-done((bf16[80,128,256]{2,1,0:T(8,128)(2,1)S(1)}, bf16[80,128,256]{2,1,0:T(8,128)(2,1)}, u32[]{:S(2)}) %copy-start) | copy-done | bytes 5242904
  26.0 1.9 %local_partials.1 = (f32[8,32,128]{2,1,0:T(8,128)S(1)}, f32[8,32,128]{2,1,0:T(8,128)S(1)}, f32[8,32,128]{2,1,0:T(8,128)S(1)}) custom-call(s32[3,16]{1,0:T(4,128)S(1)} %get-tuple-element.29.local, bf16[80,128,256]{2,1,0:T(8,128)(2,1)S(1)} %copy-done, bf16[8,32,128]{2,1,0:T(8,128)(2,1)S(1)} %reshape.28.q, bf16[8,16,256]{2,1,0:T(8,128)(2,1)S(1)} %pad.4.fresh), custom_call_target="tpu_custom_call" | custom-call | bytes 18000000 | tf_op jit(solution)/shard_map/local_partials/pallas_call | solution.py:294
  28.0 10.4 %all-to-all-done.pay.asked = bf16[32,128,128]{2,1,0:T(8,128)(2,1)S(1)} async-done(((bf16[32,128,128]{2,1,0:T(8,128)(2,1)}), bf16[32,128,128]{2,1,0:T(8,128)(2,1)S(1)}, u32[]{:S(2)}, u32[]{:S(2)}) %all-to-all-start) | async-done | bytes 1048608 | tf_op jit(solution)/shard_map/all_to_all | solution.py:510
  39.0 4.0 %collective-permute-start.5 = (bf16[4,32,128]{2,1,0:T(8,128)(2,1)S(1)}, bf16[4,32,128]{2,1,0:T(8,128)(2,1)S(1)}, u32[]{:S(2)}, u32[]{:S(2)}) collective-permute-start(bf16[4,32,128]{2,1,0:T(8,128)(2,1)S(1)} %get-tuple-element.33), channel_id=1, source_target_pairs={{0,1},{1,0},{2,3},{3,2},{4,5},{5,4},{6,7},{7,6},{8,9},{9,8},{10,11... | collective-permute-start | bytes 98312 | tf_op jit(solution)/shard_map/ppermute | solution.py:520
  44.8 11.4 %all-to-all-start.1 = ((bf16[32,2,32,128]{3,2,1,0:T(8,128)(2,1)}), bf16[32,2,32,128]{3,2,1,0:T(8,128)(2,1)S(1)}, u32[]{:S(2)}, u32[]{:S(2)}) async-start(bf16[32,2,32,128]{3,2,1,0:T(8,128)(2,1)} %bitcast.11), calls=%async_computation.1 | async-start | bytes 1048576 | tf_op jit(solution)/shard_map/all_to_all | solution.py:536
  56.6 1.7 %collective-permute-start.7 = (bf16[256,128]{1,0:T(8,128)(2,1)S(1)}, bf16[256,128]{1,0:T(8,128)(2,1)S(1)}, u32[]{:S(2)}, u32[]{:S(2)}) collective-permute-start(bf16[256,128]{1,0:T(8,128)(2,1)S(1)} %reshape_reshape.3.refs_0_), channel_id=1, source_target_pairs={{0,32},{8,40},{16,48},{24,56},{32,0},{40,8},{48,16},{56,24},{64,96... | collective-permute-start | bytes 196616 | tf_op jit(solution)/shard_map/ppermute | solution.py:479
  59.3 2.5 %copy-done.1 = bf16[80,128,256]{2,1,0:T(8,128)(2,1)S(1)} copy-done((bf16[80,128,256]{2,1,0:T(8,128)(2,1)S(1)}, bf16[80,128,256]{2,1,0:T(8,128)(2,1)}, u32[]{:S(2)}) %copy-start.1) | copy-done | bytes 5242904
  61.8 5.4 %remote_partials.1 = f32[32,72,128]{2,1,0:T(8,128)} custom-call(s32[64]{0:T(128)S(1)} %reshape.26.outbox, bf16[80,128,256]{2,1,0:T(8,128)(2,1)S(1)} %copy-done.1, bf16[32,128,128]{2,1,0:T(8,128)(2,1)S(1)} %all-to-all-done.pay.asked), custom_call_target="tpu_custom_call" | custom-call | bytes 18000000 | tf_op jit(solution)/shard_map/remote_partials/pallas_call | solution.py:245
  67.3 6.3 %all-to-all-start.2 = ((f32[32,72,128]{2,1,0:T(8,128)}), f32[32,72,128]{2,1,0:T(8,128)S(1)}, u32[]{:S(2)}, u32[]{:S(2)}) async-start(f32[32,72,128]{2,1,0:T(8,128)} %remote_partials.1), calls=%async_computation.2 | async-start | bytes 2359296 | tf_op jit(solution)/shard_map/all_to_all | solution.py:545
  73.6 3.1 %prefix_partials.2 = (f32[272,128]{1,0:T(8,128)S(1)}, f32[272,128]{1,0:T(8,128)S(1)}, f32[272,128]{1,0:T(8,128)S(1)}) custom-call(bf16[256,128]{1,0:T(8,128)(2,1)S(1)} %collective-permute-done.6.refs_0_, bf16[256,128]{1,0:T(8,128)(2,1)S(1)} %collective-permute-done.7.refs_1_, bf16[256,128]{1,0:T(8,128)(2,1)S(1)} %collective-permute-done.8.refs_2_, ...), custom_call_target="tpu_custom_call" | custom-call | bytes 9000000 | tf_op jit(solution)/shard_map/prefix_partials/pallas_call | solution.py:351
  76.7 2.5 %collective-permute-start.9 = (f32[272,128]{1,0:T(8,128)S(1)}, f32[272,128]{1,0:T(8,128)S(1)}, u32[]{:S(2)}, u32[]{:S(2)}) collective-permute-start(f32[272,128]{1,0:T(8,128)S(1)} %get-tuple-element.39), channel_id=1, source_target_pairs={{0,48},{8,56},{16,0},{24,8},{32,16},{40,24},{48,32},{56,40},{64,11... | collective-permute-start | bytes 417800 | tf_op jit(solution)/shard_map/ppermute | solution.py:479
  80.3 1.9 %prefix_partials.3.p0 = f32[272,128]{1,0:T(8,128)S(1)} custom-call(bf16[256,128]{1,0:T(8,128)(2,1)S(1)} %reshape_reshape.3.refs_0_, bf16[4,4,2,2,32,128]{5,4,3,2,1,0:T(8,128)(2,1)S(1)} %bitcast.19), custom_call_target="tpu_custom_call" | custom-call | bytes 3000000 | tf_op jit(solution)/shard_map/prefix_partials/pallas_call | solution.py:351
  82.2 9.5 %all-to-all-done.2.ret = f32[32,72,128]{2,1,0:T(8,128)S(1)} async-done(((f32[32,72,128]{2,1,0:T(8,128)}), f32[32,72,128]{2,1,0:T(8,128)S(1)}, u32[]{:S(2)}, u32[]{:S(2)}) %all-to-all-start.2) | async-done | bytes 1179680 | tf_op jit(solution)/shard_map/all_to_all | solution.py:545
  91.8 1.9 %merge.1 = (f32[8,32,128]{2,1,0:T(8,128)S(1)}, f32[8,32,128]{2,1,0:T(8,128)S(1)}, f32[8,32,128]{2,1,0:T(8,128)S(1)}) custom-call(s32[1]{0:T(128)} %bitcast.me, s32[64]{0:T(128)S(1)} %get-tuple-element.24.slot_req, f32[32,72,128]{2,1,0:T(8,128)S(1)} %all-to-all-done.2.ret, f32[8,32,128]{2,1,0:T(8,128)S(1)} %get-tuple-element.30.lo, ...), custom_call_target="tpu_custom_call" | custom-call | bytes 6000000 | tf_op jit(solution)/shard_map/merge/pallas_call | solution.py:400
  93.7 1.8 %collective-permute-done.11.p3 = f32[272,128]{1,0:T(8,128)S(1)} collective-permute-done((f32[272,128]{1,0:T(8,128)S(1)}, f32[272,128]{1,0:T(8,128)S(1)}, u32[]{:S(2)}, u32[]{:S(2)}) %collective-permute-start.11) | collective-permute-done | bytes 139296 | tf_op jit(solution)/shard_map/ppermute | solution.py:479
  (44 shorter events, 10.0 us)
Async XLA Ops:
  0.0 12.1 %copy-start.5 = (bf16[8,4,1024]{2,1,0:T(4,128)(2,1)S(1)}, bf16[8,4,1024]{2,1,0:T(4,128)(2,1)}, u32[]{:S(2)}) copy-start(bf16[8,4,1024]{2,1,0:T(4,128)(2,1)} %param.9) | copy-start | bytes 196612
  0.0 13.2 %copy-start.2 = (s32[8,32]{1,0:T(8,128)S(1)}, s32[8,32]{1,0:T(8,128)}, u32[]{:S(2)}) copy-start(s32[8,32]{1,0:T(8,128)} %page.1) | copy-start | bytes 3076
  0.0 13.2 %copy-start.4 = (s32[8]{0:T(128)S(1)}, s32[8]{0:T(128)}, u32[]{:S(2)}) copy-start(s32[8]{0:T(128)} %lens.1) | copy-start | bytes 100
  1.4 14.9 %collective-permute-start = (bf16[512,384]{1,0:T(8,128)(2,1)S(1)}, bf16[512,384]{1,0:T(8,128)(2,1)S(1)}, u32[]{:S(2)}, u32[]{:S(2)}) collective-permute-start(bf16[512,384]{1,0:T(8,128)(2,1)S(1)} %get-tuple-element.47), channel_id=1, source_target_pairs={{0,8},{8,0},{16,24},{24,16},{32,40},{40,32},{48,56},{56,48},{64,72... | collective-permute-start | bytes 1179656 | tf_op jit(solution)/shard_map/ppermute | solution.py:479
  4.0 12.4 %collective-permute-start.1 = (bf16[512,384]{1,0:T(8,128)(2,1)S(1)}, bf16[512,384]{1,0:T(8,128)(2,1)S(1)}, u32[]{:S(2)}, u32[]{:S(2)}) collective-permute-start(bf16[512,384]{1,0:T(8,128)(2,1)S(1)} %get-tuple-element.46), channel_id=1, source_target_pairs={{0,16},{8,24},{16,32},{24,40},{32,48},{40,56},{48,0},{56,8},{64,80... | collective-permute-start | bytes 1179656 | tf_op jit(solution)/shard_map/ppermute | solution.py:479
  5.2 11.2 %collective-permute-start.2 = (bf16[512,384]{1,0:T(8,128)(2,1)S(1)}, bf16[512,384]{1,0:T(8,128)(2,1)S(1)}, u32[]{:S(2)}, u32[]{:S(2)}) collective-permute-start(bf16[512,384]{1,0:T(8,128)(2,1)S(1)} %get-tuple-element.45), channel_id=1, source_target_pairs={{0,48},{8,56},{16,0},{24,8},{32,16},{40,24},{48,32},{56,40},{64,11... | collective-permute-start | bytes 1179656 | tf_op jit(solution)/shard_map/ppermute | solution.py:479
  8.5 7.8 %collective-permute-start.3 = (bf16[512,256]{1,0:T(8,128)(2,1)}, bf16[512,256]{1,0:T(8,128)(2,1)S(1)}, u32[]{:S(2)}, u32[]{:S(2)}) collective-permute-start(bf16[512,256]{1,0:T(8,128)(2,1)} %get-tuple-element.44), channel_id=1, source_target_pairs={{0,64},{8,72},{16,80},{24,88},{32,96},{40,104},{48,112},{56,120},{... | collective-permute-start | bytes 786440 | tf_op jit(solution)/shard_map/ppermute | solution.py:479
  9.8 6.5 %collective-permute-start.4 = (bf16[512,256]{1,0:T(8,128)(2,1)}, bf16[512,256]{1,0:T(8,128)(2,1)S(1)}, u32[]{:S(2)}, u32[]{:S(2)}) collective-permute-start(bf16[512,256]{1,0:T(8,128)(2,1)} %get-tuple-element.43), channel_id=1, source_target_pairs={{0,192},{8,200},{16,208},{24,216},{32,224},{40,232},{48,240},{56,2... | collective-permute-start | bytes 786440 | tf_op jit(solution)/shard_map/ppermute | solution.py:479
  16.4 7.1 %copy-start.6 = (bf16[8,4,256]{2,1,0:T(4,128)(2,1)S(1)}, bf16[8,4,256]{2,1,0:T(4,128)(2,1)}, u32[]{:S(2)}) copy-start(bf16[8,4,256]{2,1,0:T(4,128)(2,1)} %param.10) | copy-start | bytes 49156
  18.0 20.4 %all-to-all-start = ((bf16[32,128,128]{2,1,0:T(8,128)(2,1)}), bf16[32,128,128]{2,1,0:T(8,128)(2,1)S(1)}, u32[]{:S(2)}, u32[]{:S(2)}) async-start(bf16[32,128,128]{2,1,0:T(8,128)(2,1)} %pack.1), calls=%async_computation | async-start | bytes 2097152 | tf_op jit(solution)/shard_map/all_to_all | solution.py:510
  23.5 2.5 %copy-start = (bf16[80,128,256]{2,1,0:T(8,128)(2,1)S(1)}, bf16[80,128,256]{2,1,0:T(8,128)(2,1)}, u32[]{:S(2)}) copy-start(bf16[80,128,256]{2,1,0:T(8,128)(2,1)} %pool.3) | copy-start | bytes 15728644
  27.9 31.3 %copy-start.7 = (s32[1,32,2]{1,2,0:T(2,128)S(1)}, s32[1,32,2]{1,2,0:T(2,128)}, u32[]{:S(2)}) copy-start(s32[1,32,2]{1,2,0:T(2,128)} %param.14) | copy-start | bytes 772
  39.0 4.9 %collective-permute-start.5 = (bf16[4,32,128]{2,1,0:T(8,128)(2,1)S(1)}, bf16[4,32,128]{2,1,0:T(8,128)(2,1)S(1)}, u32[]{:S(2)}, u32[]{:S(2)}) collective-permute-start(bf16[4,32,128]{2,1,0:T(8,128)(2,1)S(1)} %get-tuple-element.33), channel_id=1, source_target_pairs={{0,1},{1,0},{2,3},{3,2},{4,5},{5,4},{6,7},{7,6},{8,9},{9,8},{10,11... | collective-permute-start | bytes 98312 | tf_op jit(solution)/shard_map/ppermute | solution.py:520
  44.8 22.5 %all-to-all-start.1 = ((bf16[32,2,32,128]{3,2,1,0:T(8,128)(2,1)}), bf16[32,2,32,128]{3,2,1,0:T(8,128)(2,1)S(1)}, u32[]{:S(2)}, u32[]{:S(2)}) async-start(bf16[32,2,32,128]{3,2,1,0:T(8,128)(2,1)} %bitcast.11), calls=%async_computation.1 | async-start | bytes 1048576 | tf_op jit(solution)/shard_map/all_to_all | solution.py:536
  56.2 11.0 %collective-permute-start.6 = (bf16[256,128]{1,0:T(8,128)(2,1)S(1)}, bf16[256,128]{1,0:T(8,128)(2,1)S(1)}, u32[]{:S(2)}, u32[]{:S(2)}) collective-permute-start(bf16[256,128]{1,0:T(8,128)(2,1)S(1)} %reshape_reshape.3.refs_0_), channel_id=1, source_target_pairs={{0,16},{8,24},{16,32},{24,40},{32,48},{40,56},{48,0},{56,8},{64,80... | collective-permute-start | bytes 196616 | tf_op jit(solution)/shard_map/ppermute | solution.py:479
  56.6 10.6 %collective-permute-start.7 = (bf16[256,128]{1,0:T(8,128)(2,1)S(1)}, bf16[256,128]{1,0:T(8,128)(2,1)S(1)}, u32[]{:S(2)}, u32[]{:S(2)}) collective-permute-start(bf16[256,128]{1,0:T(8,128)(2,1)S(1)} %reshape_reshape.3.refs_0_), channel_id=1, source_target_pairs={{0,32},{8,40},{16,48},{24,56},{32,0},{40,8},{48,16},{56,24},{64,96... | collective-permute-start | bytes 196616 | tf_op jit(solution)/shard_map/ppermute | solution.py:479
  58.3 8.9 %collective-permute-start.8 = (bf16[256,128]{1,0:T(8,128)(2,1)S(1)}, bf16[256,128]{1,0:T(8,128)(2,1)S(1)}, u32[]{:S(2)}, u32[]{:S(2)}) collective-permute-start(bf16[256,128]{1,0:T(8,128)(2,1)S(1)} %reshape_reshape.3.refs_0_), channel_id=1, source_target_pairs={{0,48},{8,56},{16,0},{24,8},{32,16},{40,24},{48,32},{56,40},{64,11... | collective-permute-start | bytes 196616 | tf_op jit(solution)/shard_map/ppermute | solution.py:479
  59.3 2.5 %copy-start.1 = (bf16[80,128,256]{2,1,0:T(8,128)(2,1)S(1)}, bf16[80,128,256]{2,1,0:T(8,128)(2,1)}, u32[]{:S(2)}) copy-start(bf16[80,128,256]{2,1,0:T(8,128)(2,1)} %pool.3) | copy-start | bytes 15728644
  67.3 24.5 %all-to-all-start.2 = ((f32[32,72,128]{2,1,0:T(8,128)}), f32[32,72,128]{2,1,0:T(8,128)S(1)}, u32[]{:S(2)}, u32[]{:S(2)}) async-start(f32[32,72,128]{2,1,0:T(8,128)} %remote_partials.1), calls=%async_computation.2 | async-start | bytes 2359296 | tf_op jit(solution)/shard_map/all_to_all | solution.py:545
  73.6 22.0 %copy-start.3 = (s32[8]{0:T(128)S(1)}, s32[8]{0:T(128)}, u32[]{:S(2)}) copy-start(s32[8]{0:T(128)} %flags.1) | copy-start | bytes 100
  76.7 17.1 %collective-permute-start.9 = (f32[272,128]{1,0:T(8,128)S(1)}, f32[272,128]{1,0:T(8,128)S(1)}, u32[]{:S(2)}, u32[]{:S(2)}) collective-permute-start(f32[272,128]{1,0:T(8,128)S(1)} %get-tuple-element.39), channel_id=1, source_target_pairs={{0,48},{8,56},{16,0},{24,8},{32,16},{40,24},{48,32},{56,40},{64,11... | collective-permute-start | bytes 417800 | tf_op jit(solution)/shard_map/ppermute | solution.py:479
  79.1 14.6 %collective-permute-start.10 = (f32[272,128]{1,0:T(8,128)S(1)}, f32[272,128]{1,0:T(8,128)S(1)}, u32[]{:S(2)}, u32[]{:S(2)}) collective-permute-start(f32[272,128]{1,0:T(8,128)S(1)} %get-tuple-element.41), channel_id=1, source_target_pairs={{0,32},{8,40},{16,48},{24,56},{32,0},{40,8},{48,16},{56,24},{64,96... | collective-permute-start | bytes 417800 | tf_op jit(solution)/shard_map/ppermute | solution.py:479
  79.7 15.8 %collective-permute-start.11 = (f32[272,128]{1,0:T(8,128)S(1)}, f32[272,128]{1,0:T(8,128)S(1)}, u32[]{:S(2)}, u32[]{:S(2)}) collective-permute-start(f32[272,128]{1,0:T(8,128)S(1)} %get-tuple-element.42), channel_id=1, source_target_pairs={{0,16},{8,24},{16,32},{24,40},{32,48},{40,56},{48,0},{56,8},{64,80... | collective-permute-start | bytes 417800 | tf_op jit(solution)/shard_map/ppermute | solution.py:479

commit v8 on v7

--- a/solution.py
+++ b/solution.py
@@ -22,7 +22,7 @@
 
 
 def params():
-    return pltpu.CompilerParams(vmem_limit_bytes=16 * 1024 * 1024)
+    return pltpu.CompilerParams(vmem_limit_bytes=8 * 1024 * 1024)
 
 
 def cost(us):

time: 97.8 us -> 97.8 us (level)
  no operation moved by 1% of the time
where the time goes in v8:
time: 97.8 us; the launch traced here: 97.3 us
  starting transfers between devices  41.6 us (43%)
  waiting for transfers between devices  23.5 us (24%)
  Pallas kernels  19.8 us (20%)
  local copies, waits for them, and re-layouts  11.3 us (12%)
  between operations  1.12 us (1%)
    ppermute x11, starting transfers between devices, move(): return lax.ppermute(value, 'inst', pairs)  14.5 us
    all_to_all x1, starting transfers between devices, per_device(): lax.all_to_all(spread.reshape((-1,) + both.shape[1:]), ('inst', 'tp'), sp...  11.4 us
    all_to_all x1, waiting for transfers between devices, per_device(): asked = lax.all_to_all(pay, 'inst', split_axis=0, concat_axis=0, tiled=True)  10.4 us
    all_to_all x1, waiting for transfers between devices, per_device(): lax.all_to_all(after(ret, prefix, *guests), 'inst', split_axis=0, concat_...  9.55 us
    all_to_all x1, starting transfers between devices, per_device(): lax.all_to_all(after(ret, prefix, *guests), 'inst', split_axis=0, concat_...  6.29 us
    pallas_call x1, Pallas kernels, remote_partials(): pl.pallas_call(remote_kernel, out_shape=jax.ShapeDtypeStruct(shape, F32),...  5.41 us
    all_to_all x1, starting transfers between devices, per_device(): asked = lax.all_to_all(pay, 'inst', split_axis=0, concat_axis=0, tiled=True)  5.38 us
    unnamed x17, local copies, waits for them, and re-layouts  5.08 us
  transfers between devices with their start and end apart: 15, of which 5 were waited for; matrix products, arithmetic and copies ran while one was open for 3% of the time, Pallas kernels for 17%

profile of v8, /device:TPU:1, one launch (start us, length us, event | category | flops | bytes accessed | tf_op | source)
XLA Modules:
  0.0 97.3 jit_solution(5780967104430785850)
XLA Ops:
  0.0 1.4 %fusion.1 = (bf16[512,384]{1,0:T(8,128)(2,1)S(1)}, bf16[512,384]{1,0:T(8,128)(2,1)S(1)}, bf16[512,384]{1,0:T(8,128)(2,1)S(1)}) fusion(bf16[512,2048]{1,0:T(8,128)(2,1)} %param.15), kind=kLoop, calls=%fused_computation.2 | loop fusion | bytes 2359296 | tf_op jit(solution)/shard_map/slice | solution.py:492
  1.4 2.6 %collective-permute-start = (bf16[512,384]{1,0:T(8,128)(2,1)S(1)}, bf16[512,384]{1,0:T(8,128)(2,1)S(1)}, u32[]{:S(2)}, u32[]{:S(2)}) collective-permute-start(bf16[512,384]{1,0:T(8,128)(2,1)S(1)} %get-tuple-element.47), channel_id=1, source_target_pairs={{0,8},{8,0},{16,24},{24,16},{32,40},{40,32},{48,56},{56,48},{64,72... | collective-permute-start | bytes 1179656 | tf_op jit(solution)/shard_map/ppermute | solution.py:479
  5.2 1.5 %collective-permute-start.2 = (bf16[512,384]{1,0:T(8,128)(2,1)S(1)}, bf16[512,384]{1,0:T(8,128)(2,1)S(1)}, u32[]{:S(2)}, u32[]{:S(2)}) collective-permute-start(bf16[512,384]{1,0:T(8,128)(2,1)S(1)} %get-tuple-element.45), channel_id=1, source_target_pairs={{0,48},{8,56},{16,0},{24,8},{32,16},{40,24},{48,32},{56,40},{64,11... | collective-permute-start | bytes 1179656 | tf_op jit(solution)/shard_map/ppermute | solution.py:479
  6.7 1.9 %fusion = (bf16[512,256]{1,0:T(8,128)(2,1)}, bf16[512,256]{1,0:T(8,128)(2,1)}) fusion(bf16[512,2048]{1,0:T(8,128)(2,1)} %param.15), kind=kLoop, calls=%fused_computation.1 | loop fusion | bytes 1048576 | tf_op jit(solution)/shard_map/slice | solution.py:492
  8.5 1.3 %collective-permute-start.3 = (bf16[512,256]{1,0:T(8,128)(2,1)}, bf16[512,256]{1,0:T(8,128)(2,1)S(1)}, u32[]{:S(2)}, u32[]{:S(2)}) collective-permute-start(bf16[512,256]{1,0:T(8,128)(2,1)} %get-tuple-element.44), channel_id=1, source_target_pairs={{0,64},{8,72},{16,80},{24,88},{32,96},{40,104},{48,112},{56,120},{... | collective-permute-start | bytes 786440 | tf_op jit(solution)/shard_map/ppermute | solution.py:479
  9.8 1.4 %collective-permute-start.4 = (bf16[512,256]{1,0:T(8,128)(2,1)}, bf16[512,256]{1,0:T(8,128)(2,1)S(1)}, u32[]{:S(2)}, u32[]{:S(2)}) collective-permute-start(bf16[512,256]{1,0:T(8,128)(2,1)} %get-tuple-element.43), channel_id=1, source_target_pairs={{0,192},{8,200},{16,208},{24,216},{32,224},{40,232},{48,240},{56,2... | collective-permute-start | bytes 786440 | tf_op jit(solution)/shard_map/ppermute | solution.py:479
  13.2 2.2 %prep.1 = (s32[3,16]{1,0:T(4,128)S(1)}, s32[64]{0:T(128)S(1)}, s32[64]{0:T(128)S(1)}) custom-call(s32[8,32]{1,0:T(8,128)S(1)} %copy-done.2, s32[8]{0:T(128)S(1)} %copy-done.4), custom_call_target="tpu_custom_call" | custom-call | bytes 9000000 | tf_op jit(solution)/shard_map/prep/pallas_call | solution.py:95
  16.4 1.6 %pack.1 = bf16[32,128,128]{2,1,0:T(8,128)(2,1)} custom-call(s32[64]{0:T(128)S(1)} %get-tuple-element.24.slot_req, s32[64]{0:T(128)S(1)} %get-tuple-element.25.counts, s32[1]{0:T(128)} %bitcast.2.hold, bf16[8,32,128]{2,1,0:T(8,128)(2,1)S(1)} %reshape.28.q, bf16[512,384]{1,0:T(8,128)(2,1)S(1)} %slice.23.refs_0_, ...), custom_call_target="tpu_custom_call" | custom-call | bytes 4500000 | tf_op jit(solution)/shard_map/pack/pallas_call | solution.py:151
  18.0 5.4 %all-to-all-start = ((bf16[32,128,128]{2,1,0:T(8,128)(2,1)}), bf16[32,128,128]{2,1,0:T(8,128)(2,1)S(1)}, u32[]{:S(2)}, u32[]{:S(2)}) async-start(bf16[32,128,128]{2,1,0:T(8,128)(2,1)} %pack.1), calls=%async_computation | async-start | bytes 2097152 | tf_op jit(solution)/shard_map/all_to_all | solution.py:510
  23.5 2.5 %copy-done = bf16[80,128,256]{2,1,0:T(8,128)(2,1)S(1)} copy-done((bf16[80,128,256]{2,1,0:T(8,128)(2,1)S(1)}, bf16[80,128,256]{2,1,0:T(8,128)(2,1)}, u32[]{:S(2)}) %copy-start) | copy-done | bytes 5242904
  26.0 1.9 %local_partials.1 = (f32[8,32,128]{2,1,0:T(8,128)S(1)}, f32[8,32,128]{2,1,0:T(8,128)S(1)}, f32[8,32,128]{2,1,0:T(8,128)S(1)}) custom-call(s32[3,16]{1,0:T(4,128)S(1)} %get-tuple-element.29.local, bf16[80,128,256]{2,1,0:T(8,128)(2,1)S(1)} %copy-done, bf16[8,32,128]{2,1,0:T(8,128)(2,1)S(1)} %reshape.28.q, bf16[8,16,256]{2,1,0:T(8,128)(2,1)S(1)} %pad.4.fresh), custom_call_target="tpu_custom_call" | custom-call | bytes 18000000 | tf_op jit(solution)/shard_map/local_partials/pallas_call | solution.py:294
  28.0 10.4 %all-to-all-done.pay.asked = bf16[32,128,128]{2,1,0:T(8,128)(2,1)S(1)} async-done(((bf16[32,128,128]{2,1,0:T(8,128)(2,1)}), bf16[32,128,128]{2,1,0:T(8,128)(2,1)S(1)}, u32[]{:S(2)}, u32[]{:S(2)}) %all-to-all-start) | async-done | bytes 1048608 | tf_op jit(solution)/shard_map/all_to_all | solution.py:510
  39.0 4.0 %collective-permute-start.5 = (bf16[4,32,128]{2,1,0:T(8,128)(2,1)S(1)}, bf16[4,32,128]{2,1,0:T(8,128)(2,1)S(1)}, u32[]{:S(2)}, u32[]{:S(2)}) collective-permute-start(bf16[4,32,128]{2,1,0:T(8,128)(2,1)S(1)} %get-tuple-element.33), channel_id=1, source_target_pairs={{0,1},{1,0},{2,3},{3,2},{4,5},{5,4},{6,7},{7,6},{8,9},{9,8},{10,11... | collective-permute-start | bytes 98312 | tf_op jit(solution)/shard_map/ppermute | solution.py:520
  44.8 11.4 %all-to-all-start.1 = ((bf16[32,2,32,128]{3,2,1,0:T(8,128)(2,1)}), bf16[32,2,32,128]{3,2,1,0:T(8,128)(2,1)S(1)}, u32[]{:S(2)}, u32[]{:S(2)}) async-start(bf16[32,2,32,128]{3,2,1,0:T(8,128)(2,1)} %bitcast.11), calls=%async_computation.1 | async-start | bytes 1048576 | tf_op jit(solution)/shard_map/all_to_all | solution.py:536
  56.6 1.7 %collective-permute-start.7 = (bf16[256,128]{1,0:T(8,128)(2,1)S(1)}, bf16[256,128]{1,0:T(8,128)(2,1)S(1)}, u32[]{:S(2)}, u32[]{:S(2)}) collective-permute-start(bf16[256,128]{1,0:T(8,128)(2,1)S(1)} %reshape_reshape.3.refs_0_), channel_id=1, source_target_pairs={{0,32},{8,40},{16,48},{24,56},{32,0},{40,8},{48,16},{56,24},{64,96... | collective-permute-start | bytes 196616 | tf_op jit(solution)/shard_map/ppermute | solution.py:479
  59.3 2.5 %copy-done.1 = bf16[80,128,256]{2,1,0:T(8,128)(2,1)S(1)} copy-done((bf16[80,128,256]{2,1,0:T(8,128)(2,1)S(1)}, bf16[80,128,256]{2,1,0:T(8,128)(2,1)}, u32[]{:S(2)}) %copy-start.1) | copy-done | bytes 5242904
  61.8 5.4 %remote_partials.1 = f32[32,72,128]{2,1,0:T(8,128)} custom-call(s32[64]{0:T(128)S(1)} %reshape.26.outbox, bf16[80,128,256]{2,1,0:T(8,128)(2,1)S(1)} %copy-done.1, bf16[32,128,128]{2,1,0:T(8,128)(2,1)S(1)} %all-to-all-done.pay.asked), custom_call_target="tpu_custom_call" | custom-call | bytes 18000000 | tf_op jit(solution)/shard_map/remote_partials/pallas_call | solution.py:245
  67.3 6.3 %all-to-all-start.2 = ((f32[32,72,128]{2,1,0:T(8,128)}), f32[32,72,128]{2,1,0:T(8,128)S(1)}, u32[]{:S(2)}, u32[]{:S(2)}) async-start(f32[32,72,128]{2,1,0:T(8,128)} %remote_partials.1), calls=%async_computation.2 | async-start | bytes 2359296 | tf_op jit(solution)/shard_map/all_to_all | solution.py:545
  73.6 3.1 %prefix_partials.2 = (f32[272,128]{1,0:T(8,128)S(1)}, f32[272,128]{1,0:T(8,128)S(1)}, f32[272,128]{1,0:T(8,128)S(1)}) custom-call(bf16[256,128]{1,0:T(8,128)(2,1)S(1)} %collective-permute-done.6.refs_0_, bf16[256,128]{1,0:T(8,128)(2,1)S(1)} %collective-permute-done.7.refs_1_, bf16[256,128]{1,0:T(8,128)(2,1)S(1)} %collective-permute-done.8.refs_2_, ...), custom_call_target="tpu_custom_call" | custom-call | bytes 9000000 | tf_op jit(solution)/shard_map/prefix_partials/pallas_call | solution.py:351
  76.7 2.5 %collective-permute-start.9 = (f32[272,128]{1,0:T(8,128)S(1)}, f32[272,128]{1,0:T(8,128)S(1)}, u32[]{:S(2)}, u32[]{:S(2)}) collective-permute-start(f32[272,128]{1,0:T(8,128)S(1)} %get-tuple-element.39), channel_id=1, source_target_pairs={{0,48},{8,56},{16,0},{24,8},{32,16},{40,24},{48,32},{56,40},{64,11... | collective-permute-start | bytes 417800 | tf_op jit(solution)/shard_map/ppermute | solution.py:479
  80.3 1.9 %prefix_partials.3.p0 = f32[272,128]{1,0:T(8,128)S(1)} custom-call(bf16[256,128]{1,0:T(8,128)(2,1)S(1)} %reshape_reshape.3.refs_0_, bf16[4,4,2,2,32,128]{5,4,3,2,1,0:T(8,128)(2,1)S(1)} %bitcast.19), custom_call_target="tpu_custom_call" | custom-call | bytes 3000000 | tf_op jit(solution)/shard_map/prefix_partials/pallas_call | solution.py:351
  82.2 9.5 %all-to-all-done.2.ret = f32[32,72,128]{2,1,0:T(8,128)S(1)} async-done(((f32[32,72,128]{2,1,0:T(8,128)}), f32[32,72,128]{2,1,0:T(8,128)S(1)}, u32[]{:S(2)}, u32[]{:S(2)}) %all-to-all-start.2) | async-done | bytes 1179680 | tf_op jit(solution)/shard_map/all_to_all | solution.py:545
  91.8 1.9 %merge.1 = (f32[8,32,128]{2,1,0:T(8,128)S(1)}, f32[8,32,128]{2,1,0:T(8,128)S(1)}, f32[8,32,128]{2,1,0:T(8,128)S(1)}) custom-call(s32[1]{0:T(128)} %bitcast.me, s32[64]{0:T(128)S(1)} %get-tuple-element.24.slot_req, f32[32,72,128]{2,1,0:T(8,128)S(1)} %all-to-all-done.2.ret, f32[8,32,128]{2,1,0:T(8,128)S(1)} %get-tuple-element.30.lo, ...), custom_call_target="tpu_custom_call" | custom-call | bytes 6000000 | tf_op jit(solution)/shard_map/merge/pallas_call | solution.py:400
  93.7 1.8 %collective-permute-done.11.p3 = f32[272,128]{1,0:T(8,128)S(1)} collective-permute-done((f32[272,128]{1,0:T(8,128)S(1)}, f32[272,128]{1,0:T(8,128)S(1)}, u32[]{:S(2)}, u32[]{:S(2)}) %collective-permute-start.11) | collective-permute-done | bytes 139296 | tf_op jit(solution)/shard_map/ppermute | solution.py:479
  (44 shorter events, 10.0 us)
Async XLA Ops:
  0.0 12.1 %copy-start.5 = (bf16[8,4,1024]{2,1,0:T(4,128)(2,1)S(1)}, bf16[8,4,1024]{2,1,0:T(4,128)(2,1)}, u32[]{:S(2)}) copy-start(bf16[8,4,1024]{2,1,0:T(4,128)(2,1)} %param.9) | copy-start | bytes 196612
  0.0 13.2 %copy-start.2 = (s32[8,32]{1,0:T(8,128)S(1)}, s32[8,32]{1,0:T(8,128)}, u32[]{:S(2)}) copy-start(s32[8,32]{1,0:T(8,128)} %page.1) | copy-start | bytes 3076
  0.0 13.2 %copy-start.4 = (s32[8]{0:T(128)S(1)}, s32[8]{0:T(128)}, u32[]{:S(2)}) copy-start(s32[8]{0:T(128)} %lens.1) | copy-start | bytes 100
  1.4 14.9 %collective-permute-start = (bf16[512,384]{1,0:T(8,128)(2,1)S(1)}, bf16[512,384]{1,0:T(8,128)(2,1)S(1)}, u32[]{:S(2)}, u32[]{:S(2)}) collective-permute-start(bf16[512,384]{1,0:T(8,128)(2,1)S(1)} %get-tuple-element.47), channel_id=1, source_target_pairs={{0,8},{8,0},{16,24},{24,16},{32,40},{40,32},{48,56},{56,48},{64,72... | collective-permute-start | bytes 1179656 | tf_op jit(solution)/shard_map/ppermute | solution.py:479
  4.0 12.4 %collective-permute-start.1 = (bf16[512,384]{1,0:T(8,128)(2,1)S(1)}, bf16[512,384]{1,0:T(8,128)(2,1)S(1)}, u32[]{:S(2)}, u32[]{:S(2)}) collective-permute-start(bf16[512,384]{1,0:T(8,128)(2,1)S(1)} %get-tuple-element.46), channel_id=1, source_target_pairs={{0,16},{8,24},{16,32},{24,40},{32,48},{40,56},{48,0},{56,8},{64,80... | collective-permute-start | bytes 1179656 | tf_op jit(solution)/shard_map/ppermute | solution.py:479
  5.2 11.2 %collective-permute-start.2 = (bf16[512,384]{1,0:T(8,128)(2,1)S(1)}, bf16[512,384]{1,0:T(8,128)(2,1)S(1)}, u32[]{:S(2)}, u32[]{:S(2)}) collective-permute-start(bf16[512,384]{1,0:T(8,128)(2,1)S(1)} %get-tuple-element.45), channel_id=1, source_target_pairs={{0,48},{8,56},{16,0},{24,8},{32,16},{40,24},{48,32},{56,40},{64,11... | collective-permute-start | bytes 1179656 | tf_op jit(solution)/shard_map/ppermute | solution.py:479
  8.5 7.8 %collective-permute-start.3 = (bf16[512,256]{1,0:T(8,128)(2,1)}, bf16[512,256]{1,0:T(8,128)(2,1)S(1)}, u32[]{:S(2)}, u32[]{:S(2)}) collective-permute-start(bf16[512,256]{1,0:T(8,128)(2,1)} %get-tuple-element.44), channel_id=1, source_target_pairs={{0,64},{8,72},{16,80},{24,88},{32,96},{40,104},{48,112},{56,120},{... | collective-permute-start | bytes 786440 | tf_op jit(solution)/shard_map/ppermute | solution.py:479
  9.8 6.5 %collective-permute-start.4 = (bf16[512,256]{1,0:T(8,128)(2,1)}, bf16[512,256]{1,0:T(8,128)(2,1)S(1)}, u32[]{:S(2)}, u32[]{:S(2)}) collective-permute-start(bf16[512,256]{1,0:T(8,128)(2,1)} %get-tuple-element.43), channel_id=1, source_target_pairs={{0,192},{8,200},{16,208},{24,216},{32,224},{40,232},{48,240},{56,2... | collective-permute-start | bytes 786440 | tf_op jit(solution)/shard_map/ppermute | solution.py:479
  16.4 7.1 %copy-start.6 = (bf16[8,4,256]{2,1,0:T(4,128)(2,1)S(1)}, bf16[8,4,256]{2,1,0:T(4,128)(2,1)}, u32[]{:S(2)}) copy-start(bf16[8,4,256]{2,1,0:T(4,128)(2,1)} %param.10) | copy-start | bytes 49156
  18.0 20.4 %all-to-all-start = ((bf16[32,128,128]{2,1,0:T(8,128)(2,1)}), bf16[32,128,128]{2,1,0:T(8,128)(2,1)S(1)}, u32[]{:S(2)}, u32[]{:S(2)}) async-start(bf16[32,128,128]{2,1,0:T(8,128)(2,1)} %pack.1), calls=%async_computation | async-start | bytes 2097152 | tf_op jit(solution)/shard_map/all_to_all | solution.py:510
  23.5 2.5 %copy-start = (bf16[80,128,256]{2,1,0:T(8,128)(2,1)S(1)}, bf16[80,128,256]{2,1,0:T(8,128)(2,1)}, u32[]{:S(2)}) copy-start(bf16[80,128,256]{2,1,0:T(8,128)(2,1)} %pool.3) | copy-start | bytes 15728644
  27.9 31.3 %copy-start.7 = (s32[1,32,2]{1,2,0:T(2,128)S(1)}, s32[1,32,2]{1,2,0:T(2,128)}, u32[]{:S(2)}) copy-start(s32[1,32,2]{1,2,0:T(2,128)} %param.14) | copy-start | bytes 772
  39.0 4.9 %collective-permute-start.5 = (bf16[4,32,128]{2,1,0:T(8,128)(2,1)S(1)}, bf16[4,32,128]{2,1,0:T(8,128)(2,1)S(1)}, u32[]{:S(2)}, u32[]{:S(2)}) collective-permute-start(bf16[4,32,128]{2,1,0:T(8,128)(2,1)S(1)} %get-tuple-element.33), channel_id=1, source_target_pairs={{0,1},{1,0},{2,3},{3,2},{4,5},{5,4},{6,7},{7,6},{8,9},{9,8},{10,11... | collective-permute-start | bytes 98312 | tf_op jit(solution)/shard_map/ppermute | solution.py:520
  44.8 22.5 %all-to-all-start.1 = ((bf16[32,2,32,128]{3,2,1,0:T(8,128)(2,1)}), bf16[32,2,32,128]{3,2,1,0:T(8,128)(2,1)S(1)}, u32[]{:S(2)}, u32[]{:S(2)}) async-start(bf16[32,2,32,128]{3,2,1,0:T(8,128)(2,1)} %bitcast.11), calls=%async_computation.1 | async-start | bytes 1048576 | tf_op jit(solution)/shard_map/all_to_all | solution.py:536
  56.2 11.0 %collective-permute-start.6 = (bf16[256,128]{1,0:T(8,128)(2,1)S(1)}, bf16[256,128]{1,0:T(8,128)(2,1)S(1)}, u32[]{:S(2)}, u32[]{:S(2)}) collective-permute-start(bf16[256,128]{1,0:T(8,128)(2,1)S(1)} %reshape_reshape.3.refs_0_), channel_id=1, source_target_pairs={{0,16},{8,24},{16,32},{24,40},{32,48},{40,56},{48,0},{56,8},{64,80... | collective-permute-start | bytes 196616 | tf_op jit(solution)/shard_map/ppermute | solution.py:479
  56.6 10.6 %collective-permute-start.7 = (bf16[256,128]{1,0:T(8,128)(2,1)S(1)}, bf16[256,128]{1,0:T(8,128)(2,1)S(1)}, u32[]{:S(2)}, u32[]{:S(2)}) collective-permute-start(bf16[256,128]{1,0:T(8,128)(2,1)S(1)} %reshape_reshape.3.refs_0_), channel_id=1, source_target_pairs={{0,32},{8,40},{16,48},{24,56},{32,0},{40,8},{48,16},{56,24},{64,96... | collective-permute-start | bytes 196616 | tf_op jit(solution)/shard_map/ppermute | solution.py:479
  58.3 8.9 %collective-permute-start.8 = (bf16[256,128]{1,0:T(8,128)(2,1)S(1)}, bf16[256,128]{1,0:T(8,128)(2,1)S(1)}, u32[]{:S(2)}, u32[]{:S(2)}) collective-permute-start(bf16[256,128]{1,0:T(8,128)(2,1)S(1)} %reshape_reshape.3.refs_0_), channel_id=1, source_target_pairs={{0,48},{8,56},{16,0},{24,8},{32,16},{40,24},{48,32},{56,40},{64,11... | collective-permute-start | bytes 196616 | tf_op jit(solution)/shard_map/ppermute | solution.py:479
  59.3 2.5 %copy-start.1 = (bf16[80,128,256]{2,1,0:T(8,128)(2,1)S(1)}, bf16[80,128,256]{2,1,0:T(8,128)(2,1)}, u32[]{:S(2)}) copy-start(bf16[80,128,256]{2,1,0:T(8,128)(2,1)} %pool.3) | copy-start | bytes 15728644
  67.3 24.5 %all-to-all-start.2 = ((f32[32,72,128]{2,1,0:T(8,128)}), f32[32,72,128]{2,1,0:T(8,128)S(1)}, u32[]{:S(2)}, u32[]{:S(2)}) async-start(f32[32,72,128]{2,1,0:T(8,128)} %remote_partials.1), calls=%async_computation.2 | async-start | bytes 2359296 | tf_op jit(solution)/shard_map/all_to_all | solution.py:545
  73.6 22.0 %copy-start.3 = (s32[8]{0:T(128)S(1)}, s32[8]{0:T(128)}, u32[]{:S(2)}) copy-start(s32[8]{0:T(128)} %flags.1) | copy-start | bytes 100
  76.7 17.1 %collective-permute-start.9 = (f32[272,128]{1,0:T(8,128)S(1)}, f32[272,128]{1,0:T(8,128)S(1)}, u32[]{:S(2)}, u32[]{:S(2)}) collective-permute-start(f32[272,128]{1,0:T(8,128)S(1)} %get-tuple-element.39), channel_id=1, source_target_pairs={{0,48},{8,56},{16,0},{24,8},{32,16},{40,24},{48,32},{56,40},{64,11... | collective-permute-start | bytes 417800 | tf_op jit(solution)/shard_map/ppermute | solution.py:479
  79.1 14.6 %collective-permute-start.10 = (f32[272,128]{1,0:T(8,128)S(1)}, f32[272,128]{1,0:T(8,128)S(1)}, u32[]{:S(2)}, u32[]{:S(2)}) collective-permute-start(f32[272,128]{1,0:T(8,128)S(1)} %get-tuple-element.41), channel_id=1, source_target_pairs={{0,32},{8,40},{16,48},{24,56},{32,0},{40,8},{48,16},{56,24},{64,96... | collective-permute-start | bytes 417800 | tf_op jit(solution)/shard_map/ppermute | solution.py:479
  79.7 15.8 %collective-permute-start.11 = (f32[272,128]{1,0:T(8,128)S(1)}, f32[272,128]{1,0:T(8,128)S(1)}, u32[]{:S(2)}, u32[]{:S(2)}) collective-permute-start(f32[272,128]{1,0:T(8,128)S(1)} %get-tuple-element.42), channel_id=1, source_target_pairs={{0,16},{8,24},{16,32},{24,40},{32,48},{40,56},{48,0},{56,8},{64,80... | collective-permute-start | bytes 417800 | tf_op jit(solution)/shard_map/ppermute | solution.py:479
